TPU v7x, 256 devices: a whole 4x4x8 slice. The times are simulated.
256 devices in a mesh: region: 32 (over x, z), rep: 8 (over y, core).
Axes of the slice: x: 4, y: 4, z: 8, core: 2. Of those that a mesh axis runs over, the one named last changes fastest.
Arguments:
- features: bfloat16 [8, 512, 2048], P('rep', None, 'region'), may hold values from -6 to 6
- weight_first: bfloat16 [27, 32, 64], replicated, may hold values from -0.3125 to 0.3125
- weight_second: bfloat16 [27, 64, 64], replicated, may hold values from -0.21875 to 0.21875
- cotangent: bfloat16 [8, 512, 4096], P('rep', None, 'region'), may hold values from -6 to 6
- neighbours: int32 [8, 64, 27], P('rep', 'region'), may hold values from 0 to 6, as said below
- voxel_mask: int32 [8, 64, 512], P('rep', 'region'), may hold values from 0 to 1, as said below
Outputs:
- block_out: bfloat16 [8, 512, 4096], P('rep', None, 'region')
- grad_first: float32 [27, 32, 64], replicated
- grad_second: float32 [27, 64, 64], replicated
Inputs may be any that keep to these rules, and one draw needn't show every extreme that they name: `neighbours`: tiles of region r (slots r * 2 to (r + 1) * 2 - 1 of an event) lie in one plane of tiles along the first dimension, regions in order. A value n from 2 to 3 is a tile of the same region; below 2 a tile of the region before, only at offsets with a = -1; from 4 to 5 a tile of the region after, only at offsets with a = 1; no tile outside the regions is named. Offset 13 names the tile itself for every used slot; neighbour relations are symmetric; unused slots name no tile. Some region of each event uses all its slots. `voxel_mask`: unused tile slots have no active voxel.
All inputs are finite; a program needn't handle non-finite values.
Results may differ from a plain program's by a relative error of at most 0.0057.
Values may be sent and summed in bfloat16 or wider, within the bound.
A program may use at most 128 MiB of HBM per device.

v0:
```python
import math

import jax
import jax.numpy as jnp
from jax import lax
from jax.sharding import PartitionSpec as P


def padded_2(shard, sides, width):
    for axis, dim in sides:
        size, length = (lax.axis_size(axis), shard.shape[dim])
        up = [(i, (i + 1) % size) for i in range(size - 1)]
        down = [(j, i) for i, j in up]
        last = lax.slice_in_dim(shard, length - width, length, axis=dim)
        first = lax.slice_in_dim(shard, 0, width, axis=dim)
        before = lax.ppermute(last, axis, up)
        after = lax.ppermute(first, axis, down)
        shard = jnp.concatenate([before, shard, after], axis=dim)
    return shard


def spans(step):
    if step < 0:
        return (slice(7, 8), slice(0, 1))
    if step == 0:
        return (slice(0, 8), slice(1, 9))
    return (slice(0, 1), slice(9, 10))


def assemble(extended, links, tile_count, channels):
    padded = jnp.zeros((10, 10, 10, tile_count, channels), extended.dtype)
    for offset in range(27):
        src_x, dst_x = spans(offset // 9 - 1)
        src_y, dst_y = spans(offset // 3 % 3 - 1)
        src_z, dst_z = spans(offset % 3 - 1)
        chosen = jnp.take(extended[src_x, src_y, src_z], links[:, offset], axis=3)
        padded = padded.at[dst_x, dst_y, dst_z].set(chosen)
    return padded


def pad_block(columns, links, tile_count, channels):
    gathered = padded_2(columns[None], (("region", 0),), 1)
    stacked = gathered.reshape(3, 8, 8, 8, tile_count, channels)
    extended = jnp.moveaxis(stacked, 0, 3).reshape(8, 8, 8, 3 * tile_count, channels)
    empty = jnp.zeros((8, 8, 8, 1, channels), columns.dtype)
    extended = jnp.concatenate([extended, empty], axis=3)
    return assemble(extended, links, tile_count, channels)


def forward_conv(padded, weight):
    summed = jnp.zeros((8, 8, 8, padded.shape[3], weight.shape[2]), jnp.float32)
    for offset in range(27):
        shift_x, shift_y, shift_z = (offset // 9, offset // 3 % 3, offset % 3)
        window = padded[shift_x : shift_x + 8, shift_y : shift_y + 8, shift_z : shift_z + 8]
        summed = summed + jnp.einsum(
            "xyztc,co->xyzto", window, weight[offset], preferred_element_type=jnp.float32
        )
    return summed


def transpose_conv(padded, weight):
    summed = jnp.zeros((8, 8, 8, padded.shape[3], weight.shape[1]), jnp.float32)
    for offset in range(27):
        shift_x, shift_y, shift_z = (2 - offset // 9, 2 - offset // 3 % 3, 2 - offset % 3)
        window = padded[shift_x : shift_x + 8, shift_y : shift_y + 8, shift_z : shift_z + 8]
        summed = summed + jnp.einsum(
            "xyzto,co->xyztc", window, weight[offset], preferred_element_type=jnp.float32
        )
    return summed


def kernel_grad(padded, delta):
    grads = []
    for offset in range(27):
        shift_x, shift_y, shift_z = (offset // 9, offset // 3 % 3, offset % 3)
        window = padded[shift_x : shift_x + 8, shift_y : shift_y + 8, shift_z : shift_z + 8]
        grads.append(
            jnp.einsum("xyztc,xyzto->co", window, delta, preferred_element_type=jnp.float32)
        )
    return jnp.stack(grads)


def body(features, weight_first, weight_second, cotangent, neighbours, voxel_mask):
    tile_count = neighbours.shape[1]
    in_channels = weight_first.shape[1]
    channels = weight_first.shape[2]
    links = neighbours[0]
    live = voxel_mask[0].T.astype(jnp.float32)[:, :, None]
    live_low = voxel_mask[0].T.astype(jnp.bfloat16)[:, :, None]
    masked = features[0].reshape(512, tile_count, in_channels) * live_low
    pad_first = pad_block(
        masked.reshape(512, tile_count * in_channels), links, tile_count, in_channels
    )
    pre_first = forward_conv(pad_first, weight_first).reshape(512, tile_count, channels)
    sig_first = jax.nn.sigmoid(pre_first)
    hidden = (live * pre_first * sig_first).astype(jnp.bfloat16)
    pad_second = pad_block(hidden.reshape(512, tile_count * channels), links, tile_count, channels)
    pre_second = forward_conv(pad_second, weight_second).reshape(512, tile_count, channels)
    sig_second = jax.nn.sigmoid(pre_second)
    block_out = (live * pre_second * sig_second).astype(jnp.bfloat16)
    upstream = cotangent[0].reshape(512, tile_count, channels).astype(jnp.float32)
    delta_second = (upstream * live * sig_second * (1.0 + pre_second * (1.0 - sig_second))).astype(
        jnp.bfloat16
    )
    grad_second = kernel_grad(pad_second, delta_second.reshape(8, 8, 8, tile_count, channels))
    pad_delta = pad_block(
        delta_second.reshape(512, tile_count * channels), links, tile_count, channels
    )
    back_hidden = transpose_conv(pad_delta, weight_second).reshape(512, tile_count, channels)
    delta_first = (back_hidden * live * sig_first * (1.0 + pre_first * (1.0 - sig_first))).astype(
        jnp.bfloat16
    )
    grad_first = kernel_grad(pad_first, delta_first.reshape(8, 8, 8, tile_count, channels))
    grad_first, grad_second = lax.psum((grad_first, grad_second), ("region", "rep"))
    normaliser = 1.0 / math.sqrt(lax.axis_size("rep") * tile_count * lax.axis_size("region") * 512)
    return (
        block_out.reshape(1, 512, tile_count * channels),
        grad_first * normaliser,
        grad_second * normaliser,
    )


def solution(mesh):
    in_specs = (
        P("rep", None, "region"),
        P(),
        P(),
        P("rep", None, "region"),
        P("rep", "region", None),
        P("rep", "region", None),
    )
    out_specs = (P("rep", None, "region"), P(), P())
    return jax.shard_map(body, mesh=mesh, in_specs=in_specs, out_specs=out_specs, check_vma=False)
```

profile of v0, /device:TPU:1, one launch (start us, length us, event | category | flops | bytes accessed | tf_op | source)
XLA Modules:
  0.0 586.6 jit_solution(12780226512594868508)
XLA Ops:
  8.8 1.3 collective-permute-start.1
  10.1 5.0 collective-permute-start
  25.9 1.1 reshape.3813
  38.1 1.5 maximum_bitcast_fusion
  48.5 1.4 gather_fusion.2
  52.0 1.4 gather_fusion.4
  54.4 1.6 gather_fusion.5
  56.9 1.4 gather_fusion.6
  61.2 1.4 gather_fusion.8
  65.4 1.4 gather_fusion.10
  69.1 1.4 gather_fusion.12
  72.8 1.4 scatter.290
  75.2 2.8 scatter.291
  79.4 1.4 scatter.294
  102.8 1.3 collective-permute-start.3
  104.1 4.2 collective-permute-start.2
  108.3 1.4 fusion.430
  109.7 2.6 fusion.429
  161.9 1.4 scatter.335
  164.9 2.8 scatter.336
  167.7 1.4 scatter.339
  176.6 1.1 fusion.60
  179.2 1.3 collective-permute-start.5
  180.6 5.2 collective-permute-start.4
  185.8 1.4 fusion.428
  187.2 2.4 fusion.427
  190.6 1.9 fusion.30
  192.5 0.9 fusion.29
  194.4 0.9 fusion.27
  196.3 0.9 fusion.25
  197.2 0.9 fusion.24
  198.2 0.9 fusion.23
  200.1 0.9 fusion.21
  202.0 0.9 fusion.19
  203.9 0.9 fusion.17
  205.8 0.9 fusion.15
  207.7 0.9 fusion.13
  209.6 0.9 fusion.11
  211.5 0.9 fusion.9
  216.7 1.0 copy.526
  217.9 1.0 copy.524
  219.0 1.5 maximum_bitcast_fusion.2
  270.7 1.4 scatter.380
  272.1 2.8 scatter.381
  275.0 1.4 scatter.384
  311.6 265.0 %all-reduce.9.cloned.1.call-done = (f32[27,32,64]{2,1,0:T(8,128)}, f32[27,64,64]{2,1,0:T(8,128)}) async-done(((f32[27,32,64]{2,1,0:T(8,128)}, f32[27,64,64]{2,1,0:T(8,128)}), (f32[27,32,64]{2,1,0:T(8,128)}, f32[27,64,64]{2,1,0:T(8,128)})) %all-reduce.9.cloned.1.call-update) | async-done | bytes 663568 | tf_op jit(solution)/shard_map/psum | solution.py:114
  576.7 1.9 broadcast_multiply_fusion.1
  578.6 1.0 broadcast_multiply_fusion
  (908 shorter events, 229.1 us)
Async XLA Ops:
  7.2 569.5 %all-reduce.9.cloned.1.call-start = ((), (), s32[]{:S(2)}) async-start(), calls=%async_computation | async-start | bytes 2654208 | tf_op jit(solution)/shard_map/psum | solution.py:114
  8.8 28.7 %collective-permute-start.1 = (bf16[1,512,64]{1,2,0:T(8,128)(2,1)S(1)}, bf16[1,512,64]{1,2,0:T(8,128)(2,1)S(1)}, u32[]{:S(2)}, u32[]{:S(2)}) collective-permute-start(bf16[1,512,64]{1,2,0:T(8,128)(2,1)S(1)} %bitcast_multiply_fusion.3), channel_id=1, source_target_pairs={{8,0},{16,8},{24,16},{32,24},{40,32},{48,40},{56,48},{64,56},{72,6... | collective-permute-start | bytes 196616 | tf_op jit(solution)/shard_map/ppermute | solution.py:17
  10.1 27.7 %collective-permute-start = (bf16[1,512,64]{1,2,0:T(8,128)(2,1)S(1)}, bf16[1,512,64]{1,2,0:T(8,128)(2,1)S(1)}, u32[]{:S(2)}, u32[]{:S(2)}) collective-permute-start(bf16[1,512,64]{1,2,0:T(8,128)(2,1)S(1)} %bitcast_multiply_fusion.3), channel_id=1, source_target_pairs={{0,8},{8,16},{16,24},{24,32},{32,40},{40,48},{48,56},{56,64},{64,7... | collective-permute-start | bytes 196616 | tf_op jit(solution)/shard_map/ppermute | solution.py:16
  15.3 10.4 %copy-start.64 = (bf16[1,512,128]{2,1,0:T(8,128)(2,1)S(1)}, bf16[1,512,128]{2,1,0:T(8,128)(2,1)}, u32[]{:S(2)}) copy-start(bf16[1,512,128]{2,1,0:T(8,128)(2,1)} %param.201) | copy-start | bytes 393220
  16.8 29.7 %copy-start.164 = (pred[2]{0:T(512)(128)(4,1)}, pred[2]{0:T(512)(128)(4,1)S(1)}, u32[]{:S(2)}) copy-start(pred[2]{0:T(512)(128)(4,1)S(1)} %get-tuple-element.1172) | copy-start | bytes 10
  27.1 85.2 %copy-start.60 = (f32[8,8,8,2]{2,3,1,0:T(2,128)}, f32[8,8,8,2]{2,3,1,0:T(2,128)S(1)}, u32[]{:S(2)}) copy-start(f32[8,8,8,2]{2,3,1,0:T(2,128)S(1)} %copy.469) | copy-start | bytes 12292
  27.3 18.7 %copy-start.173 = (s32[1024]{0:T(1024)}, s32[1024]{0:T(1024)S(1)}, u32[]{:S(2)}) copy-start(s32[1024]{0:T(1024)S(1)} %pad_clamp_fusion.27) | copy-start | bytes 12292
  48.5 1.4 copy-start.176
  82.2 4.5 copy-start.162
  82.3 5.2 copy-start.130
  82.3 6.0 %copy-start.156 = (pred[2]{0:T(512)(128)(4,1)S(1)}, pred[2]{0:T(512)(128)(4,1)}, u32[]{:S(2)}) copy-start(pred[2]{0:T(512)(128)(4,1)} %get-tuple-element.1207) | copy-start | bytes 10
  83.7 5.5 copy-start.127
  83.8 6.2 %copy-start.104 = (pred[2]{0:T(512)(128)(4,1)S(1)}, pred[2]{0:T(512)(128)(4,1)}, u32[]{:S(2)}) copy-start(pred[2]{0:T(512)(128)(4,1)} %get-tuple-element.1205) | copy-start | bytes 10
  85.4 10.8 %copy-start.63 = (bf16[27,32,64]{2,1,0:T(8,128)(2,1)S(1)}, bf16[27,32,64]{2,1,0:T(8,128)(2,1)}, u32[]{:S(2)}) copy-start(bf16[27,32,64]{2,1,0:T(8,128)(2,1)} %param.199) | copy-start | bytes 331780
  102.8 9.8 %collective-permute-start.3 = (bf16[1,512,128]{1,2,0:T(8,128)(2,1)S(1)}, bf16[1,512,128]{1,2,0:T(8,128)(2,1)S(1)}, u32[]{:S(2)}, u32[]{:S(2)}) collective-permute-start(bf16[1,512,128]{1,2,0:T(8,128)(2,1)S(1)} %fusion.62), channel_id=1, source_target_pairs={{8,0},{16,8},{24,16},{32,24},{40,32},{48,40},{56,48},{64,56},{72,6... | collective-permute-start | bytes 393224 | tf_op jit(solution)/shard_map/ppermute | solution.py:17
  104.1 8.8 %collective-permute-start.2 = (bf16[1,512,128]{1,2,0:T(8,128)(2,1)S(1)}, bf16[1,512,128]{1,2,0:T(8,128)(2,1)S(1)}, u32[]{:S(2)}, u32[]{:S(2)}) collective-permute-start(bf16[1,512,128]{1,2,0:T(8,128)(2,1)S(1)} %fusion.62), channel_id=1, source_target_pairs={{0,8},{8,16},{16,24},{24,32},{32,40},{40,48},{48,56},{56,64},{64,7... | collective-permute-start | bytes 393224 | tf_op jit(solution)/shard_map/ppermute | solution.py:16
  141.9 12.3 %copy-start.125 = (pred[2]{0:T(512)(128)(4,1)S(1)}, pred[2]{0:T(512)(128)(4,1)}, u32[]{:S(2)}) copy-start(pred[2]{0:T(512)(128)(4,1)} %get-tuple-element.1204) | copy-start | bytes 10
  144.8 2.9 copy-start.76
  147.7 2.9 copy-start.75
  153.4 2.9 copy-start.72
  157.1 1.6 copy-start.102
  159.4 1.4 copy-start.87
  164.8 5.3 copy-start
  175.6 1.0 copy-start.4
  175.6 1.0 copy-start.61
  179.2 37.5 %collective-permute-start.5 = (bf16[1,512,128]{1,2,0:T(8,128)(2,1)S(1)}, bf16[1,512,128]{1,2,0:T(8,128)(2,1)}, u32[]{:S(2)}, u32[]{:S(2)}) collective-permute-start(bf16[1,512,128]{1,2,0:T(8,128)(2,1)S(1)} %get-tuple-element.1158), channel_id=1, source_target_pairs={{8,0},{16,8},{24,16},{32,24},{40,32},{48,40},{56,48},{64,56},{72,6... | collective-permute-start | bytes 393224 | tf_op jit(solution)/shard_map/ppermute | solution.py:17
  180.6 37.3 %collective-permute-start.4 = (bf16[1,512,128]{1,2,0:T(8,128)(2,1)S(1)}, bf16[1,512,128]{1,2,0:T(8,128)(2,1)}, u32[]{:S(2)}, u32[]{:S(2)}) collective-permute-start(bf16[1,512,128]{1,2,0:T(8,128)(2,1)S(1)} %get-tuple-element.1158), channel_id=1, source_target_pairs={{0,8},{8,16},{16,24},{24,32},{32,40},{40,48},{48,56},{56,64},{64,7... | collective-permute-start | bytes 393224 | tf_op jit(solution)/shard_map/ppermute | solution.py:16
  189.6 1.0 copy-start.59
  190.6 1.9 copy-start.58
  190.6 1.9 copy-start.186
  192.5 1.0 copy-start.57
  248.7 15.0 %copy-start.126 = (pred[2]{0:T(512)(128)(4,1)S(1)}, pred[2]{0:T(512)(128)(4,1)}, u32[]{:S(2)}) copy-start(pred[2]{0:T(512)(128)(4,1)} %get-tuple-element.1204) | copy-start | bytes 10
  248.7 17.9 %copy-start.123 = (pred[2]{0:T(512)(128)(4,1)S(1)}, pred[2]{0:T(512)(128)(4,1)}, u32[]{:S(2)}) copy-start(pred[2]{0:T(512)(128)(4,1)} %get-tuple-element.1202) | copy-start | bytes 10
  248.7 18.6 %copy-start.152 = (pred[2]{0:T(512)(128)(4,1)S(1)}, pred[2]{0:T(512)(128)(4,1)}, u32[]{:S(2)}) copy-start(pred[2]{0:T(512)(128)(4,1)} %get-tuple-element.1201) | copy-start | bytes 10
  250.4 2.9 copy-start.6
  253.4 1.0 copy-start.74
  253.4 2.4 copy-start.93
  253.5 3.7 copy-start.71
  254.3 7.2 %copy-start.5 = (bf16[8,8,7,64]{3,2,1,0:T(8,128)(2,1)S(1)}, bf16[8,8,7,64]{3,2,1,0:T(8,128)(2,1)}, u32[]{:S(2)}) copy-start(bf16[8,8,7,64]{3,2,1,0:T(8,128)(2,1)} %get-tuple-element.1042) | copy-start | bytes 172036
  257.2 2.9 copy-start.70
  262.2 4.5 copy-start.89
  262.9 2.8 copy-start.68
  263.8 3.7 copy-start.100
  265.8 1.8 copy-start.179
  265.8 2.4 copy-start.65
  268.3 1.4 copy-start.84
  309.8 1.0 copy-start.3
  576.7 1.9 copy-start.1
  (146 other events, 112.7 us)
Sparse Core Ops, SparseCore 0:
  310.7 265.8 all-reduce.8
where the time goes:
time: 599 us; the launch traced here: 587 us
  waiting for transfers between devices  265 us (44%)
  local copies, waits for them, and re-layouts  187 us (31%)
  other arithmetic  50.4 us (8%)
  matrix products  48.7 us (8%)
  starting transfers between devices  18.3 us (3%)
  between operations  17.1 us (3%)
    psum x1, waiting for transfers between devices, body(): lax.psum((grad_first, grad_second), ('region', 'rep'))  265 us
    unnamed x379, local copies, waits for them, and re-layouts  70.9 us
    gather x81, local copies, waits for them, and re-layouts, assemble(): chosen = jnp.take(extended[src_x, src_y, src_z], links[:, offset], axis=3)  62 us
    dot_general x54, matrix products, kernel_grad(): jnp.einsum('xyztc,xyzto->co', window, delta, preferred_element_type=jnp.f...  30.1 us
    scatter x81, local copies, waits for them, and re-layouts, assemble(): padded = padded.at[dst_x, dst_y, dst_z].set(chosen)  23.3 us
    select_n x104, other arithmetic, assemble(): chosen = jnp.take(extended[src_x, src_y, src_z], links[:, offset], axis=3)  22.1 us
    ppermute x3, starting transfers between devices, padded_2(): before = lax.ppermute(last, axis, up)  14.4 us
    another operation x75, local copies, waits for them, and re-layouts, assemble(): chosen = jnp.take(extended[src_x, src_y, src_z], links[:, offset], axis=3)  14.3 us
  transfers between devices with their start and end apart: 7, of which 1 were waited for; matrix products, arithmetic and copies ran while one was open for 10% of the time, Pallas kernels for 0%

commit v1 on v0

v1 whole, which is shorter than its diff:
```python
import functools
import math

import jax
import jax.numpy as jnp
from jax import lax
from jax.experimental import pallas as pl
from jax.experimental.pallas import tpu as pltpu
from jax.sharding import PartitionSpec as P

MESH = pl.DeviceIdType.MESH
F32 = jnp.float32
BF16 = jnp.bfloat16
ROWS = (0, 80, 16)
ROWS_FIRST = (0, 80, 16, 144, 208)
PAIRS_SECOND = 16
PAIRS_FIRST = 8


def iota(shape, axis):
    return lax.broadcasted_iota(jnp.int32, shape, axis)


def dot(a, b):
    return jnp.dot(a, b, preferred_element_type=F32)


def kernel(
    sizes,
    scale,
    feat_ref,
    w1_ref,
    w2_ref,
    cot_ref,
    nbr_ref,
    mask_ref,
    out_ref,
    g1_ref,
    g2_ref,
    live_ref,
    field_ref,
    face_ref,
    halo_ref,
    side_ref,
    far_ref,
    c1_ref,
    c2_ref,
    c3_ref,
    w1b_ref,
    w2b_ref,
    w2t_ref,
    acc_ref,
    slope_ref,
    full1_ref,
    full2_ref,
    send1_ref,
    send2_ref,
    pair1_ref,
    pair2_ref,
    half1_ref,
    half2_ref,
    mine1_ref,
    mine2_ref,
    plane1_ref,
    plane2_ref,
    line1_ref,
    line2_ref,
    fin1_ref,
    fin2_ref,
    halo_send,
    halo_recv,
    pair_send,
    pair_recv,
    plane_send,
    plane_recv,
    line_send,
    line_recv,
    back_send,
    back_recv,
    twin_send,
    twin_recv,
):
    nx, nz, ny = sizes
    n_region = nx * nz
    n_plane = nx * ny
    region = lax.axis_index("region")
    rep = lax.axis_index("rep")
    my_x = region // nz
    my_z = lax.rem(region, nz)
    my_y = rep // 2
    core = lax.rem(rep, 2)
    member = my_x * ny + my_y
    right = lax.rem(region + 1, n_region)
    left = lax.rem(region + n_region - 1, n_region)

    def plane_peer(step):
        other = lax.rem(member + step, n_plane)
        return other, {"region": (other // ny) * nz + my_z, "rep": lax.rem(other, ny) * 2 + core}

    def line_peer(step):
        other = lax.rem(my_z + step, nz)
        return other, {"region": my_x * nz + other, "rep": rep}

    twin = {"region": region, "rep": my_y * 2 + 1 - core}

    barrier = pltpu.get_barrier_semaphore()
    pl.semaphore_signal(barrier, inc=1, device_id={"region": right, "rep": rep}, device_id_type=MESH)
    pl.semaphore_signal(barrier, inc=1, device_id={"region": left, "rep": rep}, device_id_type=MESH)
    pl.semaphore_signal(barrier, inc=1, device_id=twin, device_id_type=MESH)

    @pl.loop(1, n_plane)
    def _(step):
        pl.semaphore_signal(barrier, inc=1, device_id=plane_peer(step)[1], device_id_type=MESH)

    @pl.loop(1, nz)
    def _(step):
        pl.semaphore_signal(barrier, inc=1, device_id=line_peer(step)[1], device_id_type=MESH)

    mask = jnp.concatenate([mask_ref[...].astype(F32), jnp.zeros((6, 512), F32)], axis=0).T
    tile_of = (iota((8, 128), 1) // 64 == iota((8, 128), 0)).astype(F32)
    tile_of_first = (lax.rem(iota((8, 128), 1) // 32, 2) == iota((8, 128), 0)).astype(F32)
    live_ref[...] = dot(mask, tile_of).reshape(8, 64, 128)
    twice = (iota((64, 128), 0) == lax.rem(iota((64, 128), 1), 64)).astype(BF16)
    spread = dot(feat_ref[...], twice) * dot(mask, tile_of_first)
    field_ref[...] = spread.reshape(8, 64, 128)
    face_ref[...] = spread.astype(BF16).reshape(8, 64, 128)

    def halo_copies(which):
        return [
            pltpu.make_async_remote_copy(
                src_ref=face_ref.at[x],
                dst_ref=halo_ref.at[which, side],
                send_sem=halo_send.at[which, side],
                recv_sem=halo_recv.at[which, side],
                device_id={"region": to, "rep": rep},
                device_id_type=MESH,
            )
            for side, x, to in ((0, 7, right), (1, 0, left))
        ]

    pl.semaphore_wait(barrier, 3 + n_plane - 1 + nz - 1)
    halo = halo_copies(0)
    for copy in halo:
        copy.start()

    eye = iota((64, 256), 0)
    put = ((eye == iota((64, 256), 1)) | (eye == iota((64, 256), 1) - 192)).astype(BF16)
    spread1 = dot(w1_ref[...].reshape(27 * 32, 64), put).astype(BF16)
    top = spread1[:, :128].reshape(3, 3, 3, 32, 128)
    low = spread1[:, 128:].reshape(3, 3, 3, 32, 128)
    for b in range(3):
        for at, c in ((0, 0), (64, 2)):
            w1b_ref[:, b, at : at + 32, :] = top[:, b, c]
            w1b_ref[:, b, at + 32 : at + 64, :] = low[:, b, c]
    for at, b in ((0, 0), (64, 2)):
        w1b_ref[:, 3, at : at + 32, :] = top[:, b, 1]
        w1b_ref[:, 3, at + 32 : at + 64, :] = low[:, b, 1]
    w1b_ref[:, 4, 0:32, :] = top[:, 1, 1]
    w1b_ref[:, 4, 32:64, :] = low[:, 1, 1]
    w1b_ref[:, 4, 64:128, :] = jnp.zeros((3, 64, 128), BF16)
    spread2 = dot(w2_ref[...].reshape(27 * 64, 64), put).astype(BF16)
    w2b_ref[:, 0:64, :] = spread2[:, :128].reshape(27, 64, 128)
    w2b_ref[:, 64:128, :] = spread2[:, 128:].reshape(27, 64, 128)

    @pl.loop(0, 27)
    def _(k):
        w2t_ref[26 - k] = w2b_ref[k].T

    side_ref[2] = jnp.zeros((8, 64, 128), F32)
    far_ref[:, 2] = jnp.zeros((2, 64, 128), F32)
    lane = iota((8, 128), 1)
    first_half = lane < 64
    even_quarter = lax.rem(lane // 32, 2) == 0
    z_row = iota((8, 128), 0)
    z_first, z_last = z_row == 0, z_row == 7

    def rows_of(masked, count):
        return jnp.concatenate([masked] * count, axis=0) if count > 1 else masked

    def split_first():
        source, target = iota((128, 256), 0), iota((128, 256), 1)
        return (source == (target // 128) * 32 + lax.rem(target, 32)).astype(BF16)

    def split_second():
        source, target = iota((128, 256), 0), iota((128, 256), 1)
        return (source == (target // 128) * 64 + lax.rem(target, 64)).astype(BF16)

    def shifted(middle, load, tile_lane):
        ext = []
        for c in range(3):
            groups = [load(0, c, 56, 64)]
            if c == 1 and middle is not None:
                mid = middle
            else:
                mid = load(1, c, 0, 64)
            groups += [mid[8 * y : 8 * y + 8] for y in range(8)]
            groups.append(load(2, c, 0, 8))
            ext.append(groups)
        down = [pltpu.roll(jnp.where(z_last, ext[0][y], ext[1][y]), 1, 0) for y in range(10)]
        up = [pltpu.roll(jnp.where(z_first, ext[2][y], ext[1][y]), 7, 0) for y in range(10)]
        return down, ext[1], up

    def store_first(c_ref, slab, down, mid, up):
        both = [jnp.where(first_half, d, u) for d, u in zip(down, up)]
        c_ref[slab, 0:80, :] = jnp.concatenate(both, axis=0).astype(BF16)
        c_ref[slab, 80:144, :] = jnp.concatenate(both[1:9], axis=0).astype(BF16)
        ends = [jnp.where(first_half, mid[y], mid[y + 2]) for y in range(8)]
        c_ref[slab, 144:208, :] = jnp.concatenate(ends, axis=0).astype(BF16)
        c_ref[slab, 208:272, :] = jnp.concatenate(mid[1:9], axis=0).astype(BF16)

    def store_second(c_ref, slab, down, mid, up):
        for c, groups in enumerate((down, mid, up)):
            c_ref[c, slab, 0:80, :] = jnp.concatenate(groups, axis=0).astype(BF16)
            c_ref[c, slab, 80:144, :] = jnp.concatenate(groups[1:9], axis=0).astype(BF16)

    def build_inner(c_ref, store, splitter, tile_lane):
        whole = dot(face_ref[...].reshape(512, 128), splitter)
        side_ref[0] = whole[:, :128].reshape(8, 64, 128)
        side_ref[1] = whole[:, 128:].reshape(8, 64, 128)
        named = [
            [jnp.minimum(jnp.maximum(nbr_ref[t, 9 + k] - 2, 0), 2) for k in range(9)]
            for t in range(2)
        ]

        @pl.loop(0, 8)
        def _(x):
            def load(b, c, start, stop):
                k = 3 * b + c
                return jnp.where(
                    rows_of(tile_lane, (stop - start) // 8),
                    side_ref[named[0][k], x, start:stop, :],
                    side_ref[named[1][k], x, start:stop, :],
                )

            store(c_ref, x + 1, *shifted(field_ref[x], load, tile_lane))

    def build_faces(which, c_ref, store, splitter, tile_lane):
        for side in range(2):
            whole = dot(halo_ref[which, side], splitter)
            far_ref[side, 0] = whole[:, :128]
            far_ref[side, 1] = whole[:, 128:]
            named = [
                [
                    jnp.minimum(jnp.maximum(nbr_ref[t, 18 * side + k] - 4 * side, 0), 2)
                    for k in range(9)
                ]
                for t in range(2)
            ]

            def load(b, c, start, stop):
                k = 3 * b + c
                return jnp.where(
                    rows_of(tile_lane, (stop - start) // 8),
                    far_ref[side, named[0][k], start:stop, :],
                    far_ref[side, named[1][k], start:stop, :],
                )

            store(c_ref, 9 * side, *shifted(None, load, tile_lane))

    def windows_first(start, count):
        return [
            c1_ref[start : start + count, r : r + 64, :].reshape(count * 64, 128)
            for r in ROWS_FIRST
        ]

    def windows_second(c_ref, start, count):
        return [
            c_ref[c, start : start + count, ROWS[b] : ROWS[b] + 64, :].reshape(count * 64, 128)
            for b in range(3)
            for c in range(3)
        ]

    def conv_inner(windows, weight):
        acc_ref[...] = dot(jnp.concatenate(windows(1, 8), axis=1), weight(1))
        acc_ref[64:512] += dot(jnp.concatenate(windows(1, 7), axis=1), weight(0))
        acc_ref[0:448] += dot(jnp.concatenate(windows(2, 7), axis=1), weight(2))

    def conv_faces(windows, weight):
        acc_ref[0:64] += dot(jnp.concatenate(windows(0, 1), axis=1), weight(0))
        acc_ref[448:512] += dot(jnp.concatenate(windows(9, 1), axis=1), weight(2))

    def weight_first(a):
        return w1b_ref[a].reshape(5 * 128, 128)

    def weight_second(a):
        return w2b_ref[9 * a : 9 * a + 9].reshape(9 * 128, 128)

    def weight_back(a):
        return w2t_ref[9 * a : 9 * a + 9].reshape(9 * 128, 128)

    build_inner(c1_ref, store_first, split_first(), even_quarter)
    conv_inner(windows_first, weight_first)
    for copy in halo:
        copy.wait()
    build_faces(0, c1_ref, store_first, split_first(), even_quarter)
    conv_faces(windows_first, weight_first)

    @pl.loop(0, 8)
    def _(x):
        rows = pl.ds(pl.multiple_of(x * 64, 64), 64)
        pre = acc_ref[rows, :]
        live = live_ref[x]
        sig = jax.nn.sigmoid(pre)
        hidden = (live * pre * sig).astype(BF16)
        face_ref[x] = hidden
        field_ref[x] = hidden.astype(F32)
        slope_ref[x] = live * sig * (1.0 + pre * (1.0 - sig))

    halo = halo_copies(1)
    for copy in halo:
        copy.start()

    second = functools.partial(windows_second, c2_ref)
    build_inner(c2_ref, store_second, split_second(), first_half)
    conv_inner(second, weight_second)
    for copy in halo:
        copy.wait()
    build_faces(1, c2_ref, store_second, split_second(), first_half)
    conv_faces(second, weight_second)

    @pl.loop(0, 8)
    def _(x):
        rows = pl.ds(pl.multiple_of(x * 64, 64), 64)
        pre = acc_ref[rows, :]
        live = live_ref[x]
        sig = jax.nn.sigmoid(pre)
        out_ref[rows, :] = (live * pre * sig).astype(BF16)
        upstream = cot_ref[rows, :].astype(F32)
        delta = (upstream * live * sig * (1.0 + pre * (1.0 - sig))).astype(BF16)
        face_ref[x] = delta
        field_ref[x] = delta.astype(F32)

    halo = halo_copies(2)
    for copy in halo:
        copy.start()

    wide_half = iota((64, 128), 1) < 64
    wide_quarter = lax.rem(iota((64, 128), 1) // 32, 2) == 0
    per_core1, per_core2 = PAIRS_FIRST // 2, PAIRS_SECOND // 2

    def put_gradient(full, send, per_core, pair, value):
        value = value.reshape(4, 16, 128)
        units = pl.ds((pair % per_core) * 4, 4)
        full[pair // per_core, units] = value
        send[pair // per_core, units] = value.astype(BF16)

    delta_t = face_ref[...].reshape(512, 128).T
    for pair in range(14):
        both = []
        for k in (2 * pair, min(2 * pair + 1, 26)):
            a, b, c = k // 9, k // 3 % 3, k % 3
            window = c2_ref[c, a : a + 8, ROWS[b] : ROWS[b] + 64, :]
            both.append(window.reshape(512, 128))
        got = dot(delta_t, jnp.concatenate(both, axis=1))
        one, two = got[:, :128], got[:, 128:]
        straight = jnp.where(wide_half, one[0:64], two[64:128])
        crossed = jnp.where(wide_half, two[0:64], one[64:128])
        put_gradient(full2_ref, send2_ref, per_core2, pair, straight + pltpu.roll(crossed, 64, 1))
    for pair in range(14, PAIRS_SECOND):
        put_gradient(full2_ref, send2_ref, per_core2, pair, jnp.zeros((64, 128), F32))

    unit1, unit2 = 4 * per_core1 // n_plane, 4 * per_core2 // n_plane

    def reducer(which, unit, full, send, pair, half, mine, plane, line, fin):
        def pair_copy():
            return pltpu.make_async_remote_copy(
                src_ref=send.at[1 - core],
                dst_ref=pair,
                send_sem=pair_send.at[which],
                recv_sem=pair_recv.at[which],
                device_id=twin,
                device_id_type=MESH,
            )

        def plane_copy(step):
            other, device = plane_peer(step)
            return pltpu.make_async_remote_copy(
                src_ref=half.at[pl.ds(other * unit, unit)],
                dst_ref=plane.at[step],
                send_sem=plane_send.at[which, step],
                recv_sem=plane_recv.at[which, step],
                device_id=device,
                device_id_type=MESH,
            )

        def line_copy(step):
            _, device = line_peer(step)
            return pltpu.make_async_remote_copy(
                src_ref=line.at[my_z],
                dst_ref=line.at[my_z],
                send_sem=line_send.at[which, step],
                recv_sem=line_recv.at[which, step],
                device_id=device,
                device_id_type=MESH,
            )

        def back_copy(step):
            _, device = plane_peer(step)
            place = fin.at[core, pl.ds(member * unit, unit)]
            return pltpu.make_async_remote_copy(
                src_ref=place,
                dst_ref=place,
                send_sem=back_send.at[which, step],
                recv_sem=back_recv.at[which, step],
                device_id=device,
                device_id_type=MESH,
            )

        def twin_copy():
            return pltpu.make_async_remote_copy(
                src_ref=fin.at[core],
                dst_ref=fin.at[core],
                send_sem=twin_send.at[which],
                recv_sem=twin_recv.at[which],
                device_id=twin,
                device_id_type=MESH,
            )

        def start_pair():
            pair_copy().start()

        def start_plane():
            pair_copy().wait()
            total = full[core] + pair[...].astype(F32)
            half[...] = total.astype(BF16)
            mine[...] = total

            @pl.loop(1, n_plane)
            def _(step):
                plane_copy(step).start()

        def start_line():
            @pl.loop(1, n_plane)
            def _(step):
                plane_copy(step).wait()

            total = mine[pl.ds(member * unit, unit)]
            for step in range(1, n_plane):
                total = total + plane[step].astype(F32)
            line[my_z] = total.astype(BF16)

            @pl.loop(1, nz)
            def _(step):
                line_copy(step).start()

        def start_back():
            @pl.loop(1, nz)
            def _(step):
                line_copy(step).wait()

            total = line[0].astype(F32)
            for z in range(1, nz):
                total = total + line[z].astype(F32)
            fin[core, pl.ds(member * unit, unit)] = (total * scale).astype(BF16)

            @pl.loop(1, n_plane)
            def _(step):
                back_copy(step).start()

        def start_twin():
            @pl.loop(1, n_plane)
            def _(step):
                back_copy(step).wait()

            twin_copy().start()

        def finish():
            twin_copy().wait()

        return start_pair, start_plane, start_line, start_back, start_twin, finish

    sum1 = reducer(
        0, unit1, full1_ref, send1_ref, pair1_ref, half1_ref, mine1_ref, plane1_ref, line1_ref, fin1_ref
    )
    sum2 = reducer(
        1, unit2, full2_ref, send2_ref, pair2_ref, half2_ref, mine2_ref, plane2_ref, line2_ref, fin2_ref
    )

    sum2[0]()

    third = functools.partial(windows_second, c3_ref)
    build_inner(c3_ref, store_second, split_second(), first_half)
    sum2[1]()
    conv_inner(third, weight_back)
    for copy in halo:
        copy.wait()
    build_faces(2, c3_ref, store_second, split_second(), first_half)
    conv_faces(third, weight_back)
    sum2[2]()
    delta_t = (acc_ref[...] * slope_ref[...].reshape(512, 128)).astype(BF16).T
    for pair in range(PAIRS_FIRST):
        both = []
        for block in (2 * pair, min(2 * pair + 1, 14)):
            a, r = block // 5, ROWS_FIRST[block % 5]
            both.append(c1_ref[a : a + 8, r : r + 64, :].reshape(512, 128))
        got = dot(delta_t, jnp.concatenate(both, axis=1))
        one, two = got[:, :128], got[:, 128:]
        straight = jnp.where(wide_quarter, one[0:64], two[64:128])
        crossed = jnp.where(wide_quarter, two[0:64], one[64:128])
        swapped = jnp.where(wide_quarter, pltpu.roll(crossed, 96, 1), pltpu.roll(crossed, 32, 1))
        put_gradient(full1_ref, send1_ref, per_core1, pair, straight + swapped)
    sum1[0]()
    sum2[3]()
    sum1[1]()
    sum2[4]()
    sum1[2]()
    sum2[5]()
    sum1[3]()
    for pair in range(14):
        units = pl.ds((pair % per_core2) * 4, 4)
        value = fin2_ref[pair // per_core2, units].reshape(64, 128).astype(F32).T
        g2_ref[2 * pair] = value[0:64]
        if pair < 13:
            g2_ref[2 * pair + 1] = value[64:128]
    sum1[4]()
    sum1[5]()
    for pair in range(PAIRS_FIRST):
        units = pl.ds((pair % per_core1) * 4, 4)
        value = fin1_ref[pair // per_core1, units].reshape(64, 128).astype(F32).T
        for j in range(2):
            block = 2 * pair + j
            if block > 14:
                continue
            a, kind = block // 5, block % 5
            if kind < 3:
                offsets = (9 * a + 3 * kind, 9 * a + 3 * kind + 2)
            elif kind == 3:
                offsets = (9 * a + 1, 9 * a + 7)
            else:
                offsets = (9 * a + 4,)
            for i, k in enumerate(offsets):
                g1_ref[k] = value[64 * i + 32 * j : 64 * i + 32 * j + 32]


def solution(mesh):
    n_region, n_rep = mesh.shape["region"], mesh.shape["rep"]
    nx, ny = (4, 4) if n_region == 32 else (2, n_rep // 2)
    nz = n_region // nx
    n_plane = nx * ny
    core1, core2 = 2 * PAIRS_FIRST, 2 * PAIRS_SECOND
    unit1, unit2 = core1 // n_plane, core2 // n_plane
    vmem = pl.BlockSpec(memory_space=pltpu.VMEM)
    smem = pl.BlockSpec(memory_space=pltpu.SMEM)

    def body(features, weight_first, weight_second, cotangent, neighbours, voxel_mask):
        scale = 1.0 / math.sqrt(n_rep * 2 * n_region * 512)
        out, g1, g2 = pl.pallas_call(
            functools.partial(kernel, (nx, nz, ny), scale),
            out_shape=(
                jax.ShapeDtypeStruct((512, 128), BF16),
                jax.ShapeDtypeStruct((27, 32, 64), F32),
                jax.ShapeDtypeStruct((27, 64, 64), F32),
            ),
            in_specs=[vmem, vmem, vmem, vmem, smem, vmem],
            out_specs=(vmem, vmem, vmem),
            scratch_shapes=[
                pltpu.VMEM((8, 64, 128), F32),
                pltpu.VMEM((8, 64, 128), F32),
                pltpu.VMEM((8, 64, 128), BF16),
                pltpu.VMEM((3, 2, 64, 128), BF16),
                pltpu.VMEM((3, 8, 64, 128), F32),
                pltpu.VMEM((2, 3, 64, 128), F32),
                pltpu.VMEM((10, 272, 128), BF16),
                pltpu.VMEM((3, 10, 144, 128), BF16),
                pltpu.VMEM((3, 10, 144, 128), BF16),
                pltpu.VMEM((3, 5, 128, 128), BF16),
                pltpu.VMEM((27, 128, 128), BF16),
                pltpu.VMEM((27, 128, 128), BF16),
                pltpu.VMEM((512, 128), F32),
                pltpu.VMEM((8, 64, 128), F32),
                pltpu.VMEM((2, core1, 16, 128), F32),
                pltpu.VMEM((2, core2, 16, 128), F32),
                pltpu.VMEM((2, core1, 16, 128), BF16),
                pltpu.VMEM((2, core2, 16, 128), BF16),
                pltpu.VMEM((core1, 16, 128), BF16),
                pltpu.VMEM((core2, 16, 128), BF16),
                pltpu.VMEM((core1, 16, 128), BF16),
                pltpu.VMEM((core2, 16, 128), BF16),
                pltpu.VMEM((core1, 16, 128), F32),
                pltpu.VMEM((core2, 16, 128), F32),
                pltpu.VMEM((n_plane, unit1, 16, 128), BF16),
                pltpu.VMEM((n_plane, unit2, 16, 128), BF16),
                pltpu.VMEM((nz, unit1, 16, 128), BF16),
                pltpu.VMEM((nz, unit2, 16, 128), BF16),
                pltpu.VMEM((2, core1, 16, 128), BF16),
                pltpu.VMEM((2, core2, 16, 128), BF16),
                pltpu.SemaphoreType.DMA((3, 2)),
                pltpu.SemaphoreType.DMA((3, 2)),
                pltpu.SemaphoreType.DMA((2,)),
                pltpu.SemaphoreType.DMA((2,)),
                pltpu.SemaphoreType.DMA((2, n_plane)),
                pltpu.SemaphoreType.DMA((2, n_plane)),
                pltpu.SemaphoreType.DMA((2, nz)),
                pltpu.SemaphoreType.DMA((2, nz)),
                pltpu.SemaphoreType.DMA((2, n_plane)),
                pltpu.SemaphoreType.DMA((2, n_plane)),
                pltpu.SemaphoreType.DMA((2,)),
                pltpu.SemaphoreType.DMA((2,)),
            ],
            compiler_params=pltpu.CompilerParams(
                collective_id=0, has_side_effects=True, vmem_limit_bytes=40 * 2**20
            ),
        )(
            features.reshape(512, 64),
            weight_first,
            weight_second,
            cotangent.reshape(512, 128),
            neighbours.reshape(2, 27),
            voxel_mask.reshape(2, 512),
        )
        return out.reshape(1, 512, 128), g1, g2

    in_specs = (
        P("rep", None, "region"),
        P(),
        P(),
        P("rep", None, "region"),
        P("rep", "region", None),
        P("rep", "region", None),
    )
    out_specs = (P("rep", None, "region"), P(), P())
    return jax.shard_map(body, mesh=mesh, in_specs=in_specs, out_specs=out_specs, check_vma=False)
```

time: 599 us -> 57.8 us (0.10); the launches traced: 587 us -> 57.6 us
  waiting for transfers between devices: 265 us -> 0 us
  local copies, waits for them, and re-layouts: 187 us -> 5.93 us
  Pallas kernels: 0 us -> 51 us
  other arithmetic: 50.4 us -> 0 us
  matrix products: 48.7 us -> 0 us
  starting transfers between devices: 18.3 us -> 0 us
  between operations: 17.1 us -> 0.69 us
    psum x1 -> x0, waiting for transfers between devices: 265 us -> none  [body(): lax.psum((grad_first, grad_second), ('region', 'rep'))]
    unnamed x379 -> x14, local copies, waits for them, and re-layouts: 70.9 us -> 5.93 us
    gather x81 -> x0, local copies, waits for them, and re-layouts: 62 us -> none  [assemble(): chosen = jnp.take(extended[src_x, src_y, src_z], links[:, offset], axis=3)]
    pallas_call x0 -> x1, Pallas kernels: none -> 51 us  [body(): pl.pallas_call(functools.partial(kernel, (nx, nz, ny), scale), out_shape=...]
    dot_general x135 -> x0, matrix products: 48.7 us -> none  [the longest x54 30.1 us: kernel_grad(): jnp.einsum('xyztc,xyzto->co', window, delta, preferred_element_type=jnp.f...]
    scatter x81 -> x0, local copies, waits for them, and re-layouts: 23.3 us -> none  [assemble(): padded = padded.at[dst_x, dst_y, dst_z].set(chosen)]
    select_n x104 -> x0, other arithmetic: 22.1 us -> none  [assemble(): chosen = jnp.take(extended[src_x, src_y, src_z], links[:, offset], axis=3)]
    ppermute x6 -> x0, starting transfers between devices: 18.3 us -> none  [the longest x3 14.4 us: padded_2(): before = lax.ppermute(last, axis, up)]
  transfers between devices with their start and end apart: 7 -> 0, of which waited for: 1 -> 0; matrix products, arithmetic and copies ran while one was open for 10% -> 0% of each run, Pallas kernels for 0% -> 0%
where the time goes in v1:
time: 57.8 us; the launch traced here: 57.6 us
  Pallas kernels  51 us (88%)
  local copies, waits for them, and re-layouts  5.93 us (10%)
  between operations  0.69 us (1%)
    pallas_call x1, Pallas kernels, body(): pl.pallas_call(functools.partial(kernel, (nx, nz, ny), scale), out_shape=...  51 us
    unnamed x14, local copies, waits for them, and re-layouts  5.93 us

profile of v1, /device:TPU:1, one launch (start us, length us, event | category | flops | bytes accessed | tf_op | source)
XLA Modules:
  0.0 57.6 jit_solution(14892175358177620624)
XLA Ops:
  0.6 0.0 copy-start.2
  0.6 0.0 copy-start.3
  0.7 1.0 %copy.9 = bf16[1,512,64]{2,1,0:T(8,128)(2,1)S(1)} copy(bf16[1,512,64]{1,2,0:T(8,128)(2,1)} %param.6) | data formatting | bytes 131072 | tf_op args[0]
  1.6 0.0 copy-start.4
  1.7 0.0 copy-done.2
  1.7 0.0 copy-done.3
  1.7 0.7 %copy-done.4 = s32[1,2,27]{2,1,0:T(2,128)S(1)} copy-done((s32[1,2,27]{2,1,0:T(2,128)S(1)}, s32[1,2,27]{2,1,0:T(2,128)}, u32[]{:S(2)}) %copy-start.4) | copy-done | bytes 240
  2.3 0.0 copy-start
  2.3 1.0 %copy-done = bf16[27,64,64]{2,1,0:T(8,128)(2,1)S(1)} copy-done((bf16[27,64,64]{2,1,0:T(8,128)(2,1)S(1)}, bf16[27,64,64]{2,1,0:T(8,128)(2,1)}, u32[]{:S(2)}) %copy-start) | copy-done | bytes 221208
  3.3 0.0 copy-start.1
  3.3 0.9 %copy-done.1 = bf16[27,32,64]{2,1,0:T(8,128)(2,1)S(1)} copy-done((bf16[27,32,64]{2,1,0:T(8,128)(2,1)S(1)}, bf16[27,32,64]{2,1,0:T(8,128)(2,1)}, u32[]{:S(2)}) %copy-start.1) | copy-done | bytes 110616
  4.3 51.0 %shard_map.85 = (bf16[512,128]{1,0:T(8,128)(2,1)S(1)}, f32[27,32,64]{2,1,0:T(8,128)S(1)}, f32[27,64,64]{2,1,0:T(8,128)S(1)}) custom-call(bf16[512,64]{1,0:T(8,128)(2,1)S(1)} %bitcast.5, bf16[27,32,64]{2,1,0:T(8,128)(2,1)S(1)} %copy-done.1, bf16[27,64,64]{2,1,0:T(8,128)(2,1)S(1)} %copy-done, bf16[512,128]{1,0:T(8,128)(2,1)S(1)} %bitcast.7, ...), custom_call_target="tpu_custom_call" | custom-call | tf_op jit(solution)/shard_map/pallas_call | solution.py:547
  55.3 0.7 %copy.13 = bf16[1,512,128]{2,1,0:T(8,128)(2,1)} copy(bf16[1,512,128]{2,1,0:T(8,128)(2,1)S(1)} %bitcast.6) | data formatting | bytes 262144
  56.0 0.8 %copy.14 = f32[27,32,64]{2,1,0:T(8,128)} copy(f32[27,32,64]{2,1,0:T(8,128)S(1)} %get-tuple-element.13) | data formatting | bytes 442368
  56.7 0.9 %copy.15 = f32[27,64,64]{2,1,0:T(8,128)} copy(f32[27,64,64]{2,1,0:T(8,128)S(1)} %get-tuple-element.14) | data formatting | bytes 884736
Async XLA Ops:
  0.6 1.0 %copy-start.2 = (bf16[1,512,128]{2,1,0:T(8,128)(2,1)S(1)}, bf16[1,512,128]{2,1,0:T(8,128)(2,1)}, u32[]{:S(2)}) copy-start(bf16[1,512,128]{2,1,0:T(8,128)(2,1)} %param.9) | copy-start | bytes 393220
  0.6 1.0 %copy-start.3 = (s32[1,2,512]{2,1,0:T(2,128)S(1)}, s32[1,2,512]{2,1,0:T(2,128)}, u32[]{:S(2)}) copy-start(s32[1,2,512]{2,1,0:T(2,128)} %param.11) | copy-start | bytes 12292
  1.6 0.7 %copy-start.4 = (s32[1,2,27]{2,1,0:T(2,128)S(1)}, s32[1,2,27]{2,1,0:T(2,128)}, u32[]{:S(2)}) copy-start(s32[1,2,27]{2,1,0:T(2,128)} %param.10) | copy-start | bytes 652
  2.3 1.0 %copy-start = (bf16[27,64,64]{2,1,0:T(8,128)(2,1)S(1)}, bf16[27,64,64]{2,1,0:T(8,128)(2,1)}, u32[]{:S(2)}) copy-start(bf16[27,64,64]{2,1,0:T(8,128)(2,1)} %w2_ref.1) | copy-start | bytes 663556
  3.3 0.9 %copy-start.1 = (bf16[27,32,64]{2,1,0:T(8,128)(2,1)S(1)}, bf16[27,32,64]{2,1,0:T(8,128)(2,1)}, u32[]{:S(2)}) copy-start(bf16[27,32,64]{2,1,0:T(8,128)(2,1)} %w1_ref.1) | copy-start | bytes 331780

commit v2 on v1

v2 whole, which is shorter than its diff:
```python
import functools
import math

import jax
import jax.numpy as jnp
from jax import lax
from jax.experimental import pallas as pl
from jax.experimental.pallas import tpu as pltpu
from jax.sharding import PartitionSpec as P

MESH = pl.DeviceIdType.MESH
F32 = jnp.float32
BF16 = jnp.bfloat16
ROWS = (0, 80, 16)
ROWS_FIRST = (0, 80, 16, 144, 208)
PAIRS_SECOND = 16
PAIRS_FIRST = 8
HALF = (PAIRS_SECOND + PAIRS_FIRST) // 2


def iota(shape, axis):
    return lax.broadcasted_iota(jnp.int32, shape, axis)


def dot(a, b):
    return jnp.dot(a, b, preferred_element_type=F32)


def dot_nt(a, b):
    return lax.dot_general(a, b, (((1,), (1,)), ((), ())), preferred_element_type=F32)


def places(sizes):
    nx, nz, ny = sizes
    region = lax.axis_index("region")
    rep = lax.axis_index("rep")
    return region // nz, lax.rem(region, nz), rep // 2, lax.rem(rep, 2), region, rep


def compute_kernel(
    sizes,
    feat_hbm,
    w1_hbm,
    w2_hbm,
    cot_hbm,
    nbr_ref,
    mask_hbm,
    out_ref,
    grad_ref,
    feat_ref,
    w1_ref,
    w2_ref,
    cot_ref,
    mask_ref,
    live_ref,
    field_ref,
    face_ref,
    halo_ref,
    side_ref,
    far_ref,
    c1_ref,
    c2_ref,
    c3_ref,
    w1b_ref,
    w2b_ref,
    acc_ref,
    slope_ref,
    load_sem,
    halo_send,
    halo_recv,
):
    n_region = sizes[0] * sizes[1]
    region, rep = places(sizes)[4:]
    right = lax.rem(region + 1, n_region)
    left = lax.rem(region + n_region - 1, n_region)

    barrier = pltpu.get_barrier_semaphore()
    for to in (right, left):
        pl.semaphore_signal(barrier, inc=1, device_id={"region": to, "rep": rep}, device_id_type=MESH)
    loads = [
        pltpu.make_async_copy(src, dst, load_sem.at[i])
        for i, (src, dst) in enumerate(
            (
                (mask_hbm, mask_ref),
                (feat_hbm, feat_ref),
                (w1_hbm, w1_ref),
                (w2_hbm, w2_ref),
                (cot_hbm, cot_ref),
            )
        )
    ]
    for load in loads:
        load.start()
    loads[0].wait()
    loads[1].wait()

    mask = jnp.concatenate([mask_ref[...].astype(F32), jnp.zeros((6, 512), F32)], axis=0).T
    tile_of = (iota((8, 128), 1) // 64 == iota((8, 128), 0)).astype(F32)
    tile_of_first = (lax.rem(iota((8, 128), 1) // 32, 2) == iota((8, 128), 0)).astype(F32)
    live_ref[...] = dot(mask, tile_of).reshape(8, 64, 128)
    twice = (iota((64, 128), 0) == lax.rem(iota((64, 128), 1), 64)).astype(BF16)
    spread = dot(feat_ref[...].T, twice) * dot(mask, tile_of_first)
    field_ref[...] = spread.reshape(8, 64, 128)
    face_ref[...] = spread.astype(BF16).reshape(8, 64, 128)

    def halo_copies(which):
        return [
            pltpu.make_async_remote_copy(
                src_ref=face_ref.at[x],
                dst_ref=halo_ref.at[which, side],
                send_sem=halo_send.at[which, side],
                recv_sem=halo_recv.at[which, side],
                device_id={"region": to, "rep": rep},
                device_id_type=MESH,
            )
            for side, x, to in ((0, 7, right), (1, 0, left))
        ]

    pl.semaphore_wait(barrier, 2)
    halo = halo_copies(0)
    for copy in halo:
        copy.start()

    loads[2].wait()
    eye = iota((64, 256), 0)
    put = ((eye == iota((64, 256), 1)) | (eye == iota((64, 256), 1) - 192)).astype(BF16)
    spread1 = dot(w1_ref[...].reshape(27 * 32, 64), put).astype(BF16)
    top = spread1[:, :128].reshape(3, 3, 3, 32, 128)
    low = spread1[:, 128:].reshape(3, 3, 3, 32, 128)
    for b in range(3):
        for at, c in ((0, 0), (64, 2)):
            w1b_ref[:, b, at : at + 32, :] = top[:, b, c]
            w1b_ref[:, b, at + 32 : at + 64, :] = low[:, b, c]
    for at, b in ((0, 0), (64, 2)):
        w1b_ref[:, 3, at : at + 32, :] = top[:, b, 1]
        w1b_ref[:, 3, at + 32 : at + 64, :] = low[:, b, 1]
    w1b_ref[:, 4, 0:32, :] = top[:, 1, 1]
    w1b_ref[:, 4, 32:64, :] = low[:, 1, 1]
    w1b_ref[:, 4, 64:128, :] = jnp.zeros((3, 64, 128), BF16)
    loads[3].wait()
    spread2 = dot(w2_ref[...].reshape(27 * 64, 64), put).astype(BF16)
    w2b_ref[:, 0:64, :] = spread2[:, :128].reshape(27, 64, 128)
    w2b_ref[:, 64:128, :] = spread2[:, 128:].reshape(27, 64, 128)

    side_ref[2] = jnp.zeros((8, 64, 128), F32)
    far_ref[:, 2] = jnp.zeros((2, 64, 128), F32)
    lane = iota((8, 128), 1)
    first_half = lane < 64
    even_quarter = lax.rem(lane // 32, 2) == 0
    z_row = iota((8, 128), 0)
    z_first, z_last = z_row == 0, z_row == 7

    def rows_of(masked, count):
        return jnp.concatenate([masked] * count, axis=0) if count > 1 else masked

    def split_first():
        source, target = iota((128, 256), 0), iota((128, 256), 1)
        return (source == (target // 128) * 32 + lax.rem(target, 32)).astype(BF16)

    def split_second():
        source, target = iota((128, 256), 0), iota((128, 256), 1)
        return (source == (target // 128) * 64 + lax.rem(target, 64)).astype(BF16)

    def shifted(middle, load, tile_lane):
        ext = []
        for c in range(3):
            groups = [load(0, c, 56, 64)]
            if c == 1 and middle is not None:
                mid = middle
            else:
                mid = load(1, c, 0, 64)
            groups += [mid[8 * y : 8 * y + 8] for y in range(8)]
            groups.append(load(2, c, 0, 8))
            ext.append(groups)
        down = [pltpu.roll(jnp.where(z_last, ext[0][y], ext[1][y]), 1, 0) for y in range(10)]
        up = [pltpu.roll(jnp.where(z_first, ext[2][y], ext[1][y]), 7, 0) for y in range(10)]
        return down, ext[1], up

    def store_first(c_ref, slab, down, mid, up):
        both = [jnp.where(first_half, d, u) for d, u in zip(down, up)]
        c_ref[slab, 0:80, :] = jnp.concatenate(both, axis=0).astype(BF16)
        c_ref[slab, 80:144, :] = jnp.concatenate(both[1:9], axis=0).astype(BF16)
        ends = [jnp.where(first_half, mid[y], mid[y + 2]) for y in range(8)]
        c_ref[slab, 144:208, :] = jnp.concatenate(ends, axis=0).astype(BF16)
        c_ref[slab, 208:272, :] = jnp.concatenate(mid[1:9], axis=0).astype(BF16)

    def store_second(c_ref, slab, down, mid, up):
        for c, groups in enumerate((down, mid, up)):
            c_ref[c, slab, 0:80, :] = jnp.concatenate(groups, axis=0).astype(BF16)
            c_ref[c, slab, 80:144, :] = jnp.concatenate(groups[1:9], axis=0).astype(BF16)

    def build_inner(c_ref, store, splitter, tile_lane):
        whole = dot(face_ref[...].reshape(512, 128), splitter)
        side_ref[0] = whole[:, :128].reshape(8, 64, 128)
        side_ref[1] = whole[:, 128:].reshape(8, 64, 128)
        named = [
            [jnp.minimum(jnp.maximum(nbr_ref[t, 9 + k] - 2, 0), 2) for k in range(9)]
            for t in range(2)
        ]

        @pl.loop(0, 8)
        def _(x):
            def load(b, c, start, stop):
                k = 3 * b + c
                return jnp.where(
                    rows_of(tile_lane, (stop - start) // 8),
                    side_ref[named[0][k], x, start:stop, :],
                    side_ref[named[1][k], x, start:stop, :],
                )

            store(c_ref, x + 1, *shifted(field_ref[x], load, tile_lane))

    def build_faces(which, c_ref, store, splitter, tile_lane):
        for side in range(2):
            whole = dot(halo_ref[which, side], splitter)
            far_ref[side, 0] = whole[:, :128]
            far_ref[side, 1] = whole[:, 128:]
            named = [
                [
                    jnp.minimum(jnp.maximum(nbr_ref[t, 18 * side + k] - 4 * side, 0), 2)
                    for k in range(9)
                ]
                for t in range(2)
            ]

            def load(b, c, start, stop):
                k = 3 * b + c
                return jnp.where(
                    rows_of(tile_lane, (stop - start) // 8),
                    far_ref[side, named[0][k], start:stop, :],
                    far_ref[side, named[1][k], start:stop, :],
                )

            store(c_ref, 9 * side, *shifted(None, load, tile_lane))

    def windows_first(start, count):
        return [
            c1_ref[start : start + count, r : r + 64, :].reshape(count * 64, 128)
            for r in ROWS_FIRST
        ]

    def windows_second(c_ref, start, count):
        return [
            c_ref[c, start : start + count, ROWS[b] : ROWS[b] + 64, :].reshape(count * 64, 128)
            for b in range(3)
            for c in range(3)
        ]

    def conv_inner(windows, weight, product=dot):
        acc_ref[...] = product(jnp.concatenate(windows(1, 8), axis=1), weight(1))
        acc_ref[64:512] += product(jnp.concatenate(windows(1, 7), axis=1), weight(0))
        acc_ref[0:448] += product(jnp.concatenate(windows(2, 7), axis=1), weight(2))

    def conv_faces(windows, weight, product=dot):
        acc_ref[0:64] += product(jnp.concatenate(windows(0, 1), axis=1), weight(0))
        acc_ref[448:512] += product(jnp.concatenate(windows(9, 1), axis=1), weight(2))

    def weight_first(a):
        return w1b_ref[a].reshape(5 * 128, 128)

    def weight_second(a):
        return w2b_ref[9 * a : 9 * a + 9].reshape(9 * 128, 128)

    def weight_back(a):
        return jnp.concatenate([w2b_ref[26 - k] for k in range(9 * a, 9 * a + 9)], axis=1)

    def layer(which, c_ref, store, splitter, tile_lane, windows, weight, product, activate, halo):
        build_inner(c_ref, store, splitter, tile_lane)
        conv_inner(windows, weight, product)
        pl.loop(1, 7)(activate)
        for copy in halo:
            copy.wait()
        build_faces(which, c_ref, store, splitter, tile_lane)
        conv_faces(windows, weight, product)
        pl.loop(0, 2)(lambda i: activate(7 * i))

    def hidden_of(x):
        rows = pl.ds(pl.multiple_of(x * 64, 64), 64)
        pre = acc_ref[rows, :]
        live = live_ref[x]
        sig = jax.nn.sigmoid(pre)
        hidden = (live * pre * sig).astype(BF16)
        face_ref[x] = hidden
        field_ref[x] = hidden.astype(F32)
        slope_ref[x] = live * sig * (1.0 + pre * (1.0 - sig))

    def outputs_of(x):
        rows = pl.ds(pl.multiple_of(x * 64, 64), 64)
        pre = acc_ref[rows, :]
        live = live_ref[x]
        sig = jax.nn.sigmoid(pre)
        out_ref[rows, :] = (live * pre * sig).astype(BF16)
        upstream = cot_ref[rows, :].astype(F32)
        delta = (upstream * live * sig * (1.0 + pre * (1.0 - sig))).astype(BF16)
        face_ref[x] = delta
        field_ref[x] = delta.astype(F32)

    def back_of(x):
        rows = pl.ds(pl.multiple_of(x * 64, 64), 64)
        face_ref[x] = (acc_ref[rows, :] * slope_ref[x]).astype(BF16)

    layer(0, c1_ref, store_first, split_first(), even_quarter, windows_first, weight_first, dot, hidden_of, halo)
    halo = halo_copies(1)
    for copy in halo:
        copy.start()

    second = functools.partial(windows_second, c2_ref)
    loads[4].wait()
    layer(1, c2_ref, store_second, split_second(), first_half, second, weight_second, dot, outputs_of, halo)
    halo = halo_copies(2)
    for copy in halo:
        copy.start()

    wide_half = iota((64, 128), 1) < 64
    wide_quarter = lax.rem(iota((64, 128), 1) // 32, 2) == 0

    def put_gradient(pair, value):
        grad_ref[pair // HALF, (pair % HALF) * 4 : (pair % HALF) * 4 + 4] = value.reshape(4, 16, 128)

    delta_t = face_ref[...].reshape(512, 128).T
    for pair in range(14):
        both = []
        for k in (2 * pair, min(2 * pair + 1, 26)):
            a, b, c = k // 9, k // 3 % 3, k % 3
            window = c2_ref[c, a : a + 8, ROWS[b] : ROWS[b] + 64, :]
            both.append(window.reshape(512, 128))
        got = dot(delta_t, jnp.concatenate(both, axis=1))
        one, two = got[:, :128], got[:, 128:]
        straight = jnp.where(wide_half, one[0:64], two[64:128])
        crossed = jnp.where(wide_half, two[0:64], one[64:128])
        put_gradient(pair, straight + pltpu.roll(crossed, 64, 1))
    for pair in range(14, PAIRS_SECOND):
        put_gradient(pair, jnp.zeros((64, 128), F32))

    third = functools.partial(windows_second, c3_ref)
    layer(2, c3_ref, store_second, split_second(), first_half, third, weight_back, dot_nt, back_of, halo)
    delta_t = face_ref[...].reshape(512, 128).T
    for pair in range(PAIRS_FIRST):
        both = []
        for block in (2 * pair, min(2 * pair + 1, 14)):
            a, r = block // 5, ROWS_FIRST[block % 5]
            both.append(c1_ref[a : a + 8, r : r + 64, :].reshape(512, 128))
        got = dot(delta_t, jnp.concatenate(both, axis=1))
        one, two = got[:, :128], got[:, 128:]
        straight = jnp.where(wide_quarter, one[0:64], two[64:128])
        crossed = jnp.where(wide_quarter, two[0:64], one[64:128])
        swapped = jnp.where(wide_quarter, pltpu.roll(crossed, 96, 1), pltpu.roll(crossed, 32, 1))
        put_gradient(PAIRS_SECOND + pair, straight + swapped)


def sum_kernel(
    sizes,
    scale,
    grad_ref,
    fin_ref,
    send_ref,
    pair_ref,
    half_ref,
    mine_ref,
    plane_ref,
    line_ref,
    pair_send,
    pair_recv,
    plane_send,
    plane_recv,
    line_send,
    line_recv,
    back_send,
    back_recv,
    twin_send,
    twin_recv,
):
    nx, nz, ny = sizes
    n_plane = nx * ny
    my_x, my_z, my_y, core, region, rep = places(sizes)
    member = my_x * ny + my_y
    unit = 4 * HALF // n_plane

    def plane_peer(step):
        other = lax.rem(member + step, n_plane)
        return other, {"region": (other // ny) * nz + my_z, "rep": lax.rem(other, ny) * 2 + core}

    def line_peer(step):
        return {"region": my_x * nz + lax.rem(my_z + step, nz), "rep": rep}

    twin = {"region": region, "rep": my_y * 2 + 1 - core}

    barrier = pltpu.get_barrier_semaphore()
    pl.semaphore_signal(barrier, inc=1, device_id=twin, device_id_type=MESH)

    @pl.loop(1, n_plane)
    def _(step):
        pl.semaphore_signal(barrier, inc=1, device_id=plane_peer(step)[1], device_id_type=MESH)

    @pl.loop(1, nz)
    def _(step):
        pl.semaphore_signal(barrier, inc=1, device_id=line_peer(step), device_id_type=MESH)

    def remote(src, dst, send_sem, recv_sem, device):
        return pltpu.make_async_remote_copy(
            src_ref=src,
            dst_ref=dst,
            send_sem=send_sem,
            recv_sem=recv_sem,
            device_id=device,
            device_id_type=MESH,
        )

    def plane_copy(step):
        other, device = plane_peer(step)
        source = half_ref.at[pl.ds(other * unit, unit)]
        return remote(source, plane_ref.at[step], plane_send.at[step], plane_recv.at[step], device)

    def line_copy(step):
        place = line_ref.at[my_z]
        return remote(place, place, line_send.at[step], line_recv.at[step], line_peer(step))

    def back_copy(step):
        place = fin_ref.at[core, pl.ds(member * unit, unit)]
        return remote(place, place, back_send.at[step], back_recv.at[step], plane_peer(step)[1])

    send_ref[...] = grad_ref[1 - core].astype(BF16)
    pl.semaphore_wait(barrier, 1 + n_plane - 1 + nz - 1)
    pair_copy = remote(send_ref, pair_ref, pair_send.at[0], pair_recv.at[0], twin)
    pair_copy.start()
    pair_copy.wait()
    total = grad_ref[core] + pair_ref[...].astype(F32)
    half_ref[...] = total.astype(BF16)
    mine_ref[...] = total

    @pl.loop(1, n_plane)
    def _(step):
        plane_copy(step).start()

    @pl.loop(1, n_plane)
    def _(step):
        plane_copy(step).wait()

    total = mine_ref[pl.ds(member * unit, unit)]
    for step in range(1, n_plane):
        total = total + plane_ref[step].astype(F32)
    line_ref[my_z] = total.astype(BF16)

    @pl.loop(1, nz)
    def _(step):
        line_copy(step).start()

    @pl.loop(1, nz)
    def _(step):
        line_copy(step).wait()

    total = line_ref[0].astype(F32)
    for z in range(1, nz):
        total = total + line_ref[z].astype(F32)
    fin_ref[core, pl.ds(member * unit, unit)] = (total * scale).astype(BF16)

    @pl.loop(1, n_plane)
    def _(step):
        back_copy(step).start()

    @pl.loop(1, n_plane)
    def _(step):
        back_copy(step).wait()

    twin_copy = remote(fin_ref.at[core], fin_ref.at[core], twin_send.at[0], twin_recv.at[0], twin)
    twin_copy.start()
    twin_copy.wait()


def unpack_kernel(block_ref, fin_ref, out_hbm, g1_hbm, g2_hbm, g1_ref, g2_ref, sem):
    block_copy = pltpu.make_async_copy(block_ref, out_hbm, sem.at[0])
    block_copy.start()
    for pair in range(PAIRS_SECOND + PAIRS_FIRST):
        if pair in (14, 15):
            continue
        at = (pair % HALF) * 4
        value = fin_ref[pair // HALF, at : at + 4].reshape(64, 128).astype(F32).T
        if pair < 14:
            g2_ref[2 * pair] = value[0:64]
            if pair < 13:
                g2_ref[2 * pair + 1] = value[64:128]
            continue
        if pair == PAIRS_SECOND:
            second_copy = pltpu.make_async_copy(g2_ref, g2_hbm, sem.at[1])
            second_copy.start()
        for j in range(2):
            block = 2 * (pair - PAIRS_SECOND) + j
            if block > 14:
                continue
            a, kind = block // 5, block % 5
            if kind < 3:
                offsets = (9 * a + 3 * kind, 9 * a + 3 * kind + 2)
            elif kind == 3:
                offsets = (9 * a + 1, 9 * a + 7)
            else:
                offsets = (9 * a + 4,)
            for i, k in enumerate(offsets):
                g1_ref[k] = value[64 * i + 32 * j : 64 * i + 32 * j + 32]
    first_copy = pltpu.make_async_copy(g1_ref, g1_hbm, sem.at[2])
    first_copy.start()
    block_copy.wait()
    second_copy.wait()
    first_copy.wait()


def solution(mesh):
    n_region, n_rep = mesh.shape["region"], mesh.shape["rep"]
    nx, ny = (4, 4) if n_region == 32 else (2, n_rep // 2)
    nz = n_region // nx
    sizes = (nx, nz, ny)
    n_plane = nx * ny
    units = 4 * HALF
    unit = units // n_plane
    vmem = pl.BlockSpec(memory_space=pltpu.VMEM)
    smem = pl.BlockSpec(memory_space=pltpu.SMEM)
    hbm = pl.BlockSpec(memory_space=pl.ANY)
    dma = pltpu.SemaphoreType.DMA

    def body(features, weight_first, weight_second, cotangent, neighbours, voxel_mask):
        scale = 1.0 / math.sqrt(n_rep * 2 * n_region * 512)
        block, grad = pl.pallas_call(
            functools.partial(compute_kernel, sizes),
            out_shape=(
                jax.ShapeDtypeStruct((512, 128), BF16),
                jax.ShapeDtypeStruct((2, units, 16, 128), F32),
            ),
            in_specs=[hbm, hbm, hbm, hbm, smem, hbm],
            out_specs=(vmem, vmem),
            scratch_shapes=[
                pltpu.VMEM((64, 512), BF16),
                pltpu.VMEM((27, 32, 64), BF16),
                pltpu.VMEM((27, 64, 64), BF16),
                pltpu.VMEM((512, 128), BF16),
                pltpu.VMEM((2, 512), jnp.int32),
                pltpu.VMEM((8, 64, 128), F32),
                pltpu.VMEM((8, 64, 128), F32),
                pltpu.VMEM((8, 64, 128), BF16),
                pltpu.VMEM((3, 2, 64, 128), BF16),
                pltpu.VMEM((3, 8, 64, 128), F32),
                pltpu.VMEM((2, 3, 64, 128), F32),
                pltpu.VMEM((10, 272, 128), BF16),
                pltpu.VMEM((3, 10, 144, 128), BF16),
                pltpu.VMEM((3, 10, 144, 128), BF16),
                pltpu.VMEM((3, 5, 128, 128), BF16),
                pltpu.VMEM((27, 128, 128), BF16),
                pltpu.VMEM((512, 128), F32),
                pltpu.VMEM((8, 64, 128), F32),
                dma((5,)),
                dma((3, 2)),
                dma((3, 2)),
            ],
            compiler_params=pltpu.CompilerParams(
                collective_id=0, has_side_effects=True, vmem_limit_bytes=56 * 2**20
            ),
        )(
            jnp.swapaxes(features, 1, 2).reshape(64, 512),
            weight_first,
            weight_second,
            cotangent.reshape(512, 128),
            neighbours.reshape(2, 27),
            voxel_mask.reshape(2, 512),
        )
        fin = pl.pallas_call(
            functools.partial(sum_kernel, sizes, scale),
            out_shape=jax.ShapeDtypeStruct((2, units, 16, 128), BF16),
            in_specs=[vmem],
            out_specs=vmem,
            scratch_shapes=[
                pltpu.VMEM((units, 16, 128), BF16),
                pltpu.VMEM((units, 16, 128), BF16),
                pltpu.VMEM((units, 16, 128), BF16),
                pltpu.VMEM((units, 16, 128), F32),
                pltpu.VMEM((n_plane, unit, 16, 128), BF16),
                pltpu.VMEM((nz, unit, 16, 128), BF16),
                dma((1,)),
                dma((1,)),
                dma((n_plane,)),
                dma((n_plane,)),
                dma((nz,)),
                dma((nz,)),
                dma((n_plane,)),
                dma((n_plane,)),
                dma((1,)),
                dma((1,)),
            ],
            compiler_params=pltpu.CompilerParams(
                collective_id=1, has_side_effects=True, vmem_limit_bytes=40 * 2**20
            ),
        )(grad)
        out, g1, g2 = pl.pallas_call(
            unpack_kernel,
            out_shape=(
                jax.ShapeDtypeStruct((512, 128), BF16),
                jax.ShapeDtypeStruct((27, 32, 64), F32),
                jax.ShapeDtypeStruct((27, 64, 64), F32),
            ),
            in_specs=[vmem, vmem],
            out_specs=(hbm, hbm, hbm),
            scratch_shapes=[
                pltpu.VMEM((27, 32, 64), F32),
                pltpu.VMEM((27, 64, 64), F32),
                dma((3,)),
            ],
            compiler_params=pltpu.CompilerParams(vmem_limit_bytes=40 * 2**20),
        )(block, fin)
        return out.reshape(1, 512, 128), g1, g2

    in_specs = (
        P("rep", None, "region"),
        P(),
        P(),
        P("rep", None, "region"),
        P("rep", "region", None),
        P("rep", "region", None),
    )
    out_specs = (P("rep", None, "region"), P(), P())
    return jax.shard_map(body, mesh=mesh, in_specs=in_specs, out_specs=out_specs, check_vma=False)
```

time: 57.8 us -> 52.1 us (0.901)
  local copies, waits for them, and re-layouts: 5.93 us -> 1.13 us
  Pallas kernels: 51 us -> 50.2 us
    unnamed x14 -> x4, local copies, waits for them, and re-layouts: 5.93 us -> 1.13 us
    pallas_call x1 -> x3, Pallas kernels: 51 us -> 50.2 us  [the longest x1 26.9 us: body(): pl.pallas_call(functools.partial(sum_kernel, sizes, scale), out_shape=jax...]
where the time goes in v2:
time: 52.1 us; the launch traced here: 52 us
  Pallas kernels  50.2 us (96%)
  local copies, waits for them, and re-layouts  1.13 us (2%)
  between operations  0.66 us (1%)
    pallas_call x1, Pallas kernels, body(): pl.pallas_call(functools.partial(sum_kernel, sizes, scale), out_shape=jax...  26.9 us
    pallas_call x1, Pallas kernels, body(): pl.pallas_call(functools.partial(compute_kernel, sizes), out_shape=(jax.S...  22 us
    pallas_call x1, Pallas kernels, body(): pl.pallas_call(unpack_kernel, out_shape=(jax.ShapeDtypeStruct((512, 128),...  1.29 us
    unnamed x4, local copies, waits for them, and re-layouts  1.13 us

profile of v2, /device:TPU:1, one launch (start us, length us, event | category | flops | bytes accessed | tf_op | source)
XLA Modules:
  0.0 52.0 jit_solution(2747765249128177328)
XLA Ops:
  0.6 22.0 %shard_map.85 = (bf16[512,128]{1,0:T(8,128)(2,1)}, f32[2,48,16,128]{3,2,1,0:T(8,128)}) custom-call(bf16[64,512]{1,0:T(8,128)(2,1)} %bitcast.8, bf16[27,32,64]{2,1,0:T(8,128)(2,1)} %w1_hbm.1, bf16[27,64,64]{2,1,0:T(8,128)(2,1)} %w2_hbm.1, bf16[512,128]{1,0:T(8,128)(2,1)} %bitcast.7, s32[2,27]{1,0:T(2,128)} %bitcast.10, s32[2,512]{1,0:T(2,128)} %bitcast.9), custom_call_target="tpu_custom_call" | custom-call | tf_op jit(solution)/shard_map/pallas_call | solution.py:521
  22.6 0.0 copy-start
  22.6 1.1 %copy-done = f32[2,48,16,128]{3,2,1,0:T(8,128)S(1)} copy-done((f32[2,48,16,128]{3,2,1,0:T(8,128)S(1)}, f32[2,48,16,128]{3,2,1,0:T(8,128)}, u32[]{:S(2)}) %copy-start) | copy-done | bytes 786456
  23.7 0.0 copy-start.1
  23.7 26.9 %shard_map.86.fin_ref = bf16[2,48,16,128]{3,2,1,0:T(8,128)(2,1)S(1)} custom-call(f32[2,48,16,128]{3,2,1,0:T(8,128)S(1)} %copy-done), custom_call_target="tpu_custom_call" | custom-call | tf_op jit(solution)/shard_map/pallas_call | solution.py:563
  50.7 0.0 copy-done.1
  50.7 1.3 %shard_map.87 = (bf16[512,128]{1,0:T(8,128)(2,1)}, f32[27,32,64]{2,1,0:T(8,128)}, f32[27,64,64]{2,1,0:T(8,128)}) custom-call(bf16[512,128]{1,0:T(8,128)(2,1)S(1)} %copy-done.1, bf16[2,48,16,128]{3,2,1,0:T(8,128)(2,1)S(1)} %shard_map.86.fin_ref), custom_call_target="tpu_custom_call" | custom-call | tf_op jit(solution)/shard_map/pallas_call | solution.py:590
Async XLA Ops:
  22.6 1.1 %copy-start = (f32[2,48,16,128]{3,2,1,0:T(8,128)S(1)}, f32[2,48,16,128]{3,2,1,0:T(8,128)}, u32[]{:S(2)}) copy-start(f32[2,48,16,128]{3,2,1,0:T(8,128)} %get-tuple-element.9.grad_ref) | copy-start | bytes 2359300
  23.7 26.9 %copy-start.1 = (bf16[512,128]{1,0:T(8,128)(2,1)S(1)}, bf16[512,128]{1,0:T(8,128)(2,1)}, u32[]{:S(2)}) copy-start(bf16[512,128]{1,0:T(8,128)(2,1)} %get-tuple-element.8.block_ref) | copy-start | bytes 393220

commit v3 on v2

--- a/solution.py
+++ b/solution.py
@@ -15,7 +15,6 @@
 ROWS_FIRST = (0, 80, 16, 144, 208)
 PAIRS_SECOND = 16
 PAIRS_FIRST = 8
-HALF = (PAIRS_SECOND + PAIRS_FIRST) // 2
 
 
 def iota(shape, axis):
@@ -37,16 +36,18 @@
     return region // nz, lax.rem(region, nz), rep // 2, lax.rem(rep, 2), region, rep
 
 
-def compute_kernel(
+def main_kernel(
     sizes,
+    scale,
     feat_hbm,
     w1_hbm,
     w2_hbm,
     cot_hbm,
     nbr_ref,
     mask_hbm,
-    out_ref,
-    grad_ref,
+    out_hbm,
+    fin1_hbm,
+    fin2_hbm,
     feat_ref,
     w1_ref,
     w2_ref,
@@ -65,18 +66,51 @@
     w2b_ref,
     acc_ref,
     slope_ref,
+    full1_ref,
+    full2_ref,
+    send1_ref,
+    send2_ref,
+    pair1_ref,
+    pair2_ref,
+    half1_ref,
+    half2_ref,
+    plane1_ref,
+    plane2_ref,
+    line1_ref,
+    line2_ref,
+    fin1_ref,
+    fin2_ref,
+    out_ref,
     load_sem,
+    store_sem,
     halo_send,
     halo_recv,
+    sum_send,
+    sum_recv,
 ):
-    n_region = sizes[0] * sizes[1]
-    region, rep = places(sizes)[4:]
+    nx, nz, ny = sizes
+    n_region, n_plane = nx * nz, nx * ny
+    my_x, my_z, my_y, core, region, rep = places(sizes)
+    member = my_x * ny + my_y
     right = lax.rem(region + 1, n_region)
     left = lax.rem(region + n_region - 1, n_region)
+    twin = {"region": region, "rep": my_y * 2 + 1 - core}
+    plane_peers = []
+    for step in range(1, n_plane):
+        other = lax.rem(member + step, n_plane)
+        at = {"region": (other // ny) * nz + my_z, "rep": lax.rem(other, ny) * 2 + core}
+        plane_peers.append((step, other, at))
+    line_peers = [
+        {"region": my_x * nz + lax.rem(my_z + step, nz), "rep": rep} for step in range(1, nz)
+    ]
+
+    halo_ref[...] = jnp.zeros((3, 2, 64, 128), BF16)
 
     barrier = pltpu.get_barrier_semaphore()
-    for to in (right, left):
-        pl.semaphore_signal(barrier, inc=1, device_id={"region": to, "rep": rep}, device_id_type=MESH)
+    partners = [{"region": right, "rep": rep}, {"region": left, "rep": rep}, twin]
+    partners += [at for _, _, at in plane_peers] + line_peers
+    for at in partners:
+        pl.semaphore_signal(barrier, inc=1, device_id=at, device_id_type=MESH)
     loads = [
         pltpu.make_async_copy(src, dst, load_sem.at[i])
         for i, (src, dst) in enumerate(
@@ -103,23 +137,36 @@
     field_ref[...] = spread.reshape(8, 64, 128)
     face_ref[...] = spread.astype(BF16).reshape(8, 64, 128)
 
-    def halo_copies(which):
-        return [
-            pltpu.make_async_remote_copy(
-                src_ref=face_ref.at[x],
-                dst_ref=halo_ref.at[which, side],
-                send_sem=halo_send.at[which, side],
-                recv_sem=halo_recv.at[which, side],
-                device_id={"region": to, "rep": rep},
-                device_id_type=MESH,
-            )
-            for side, x, to in ((0, 7, right), (1, 0, left))
-        ]
-
-    pl.semaphore_wait(barrier, 2)
-    halo = halo_copies(0)
-    for copy in halo:
-        copy.start()
+    def halo_copy(which, side):
+        return pltpu.make_async_remote_copy(
+            src_ref=face_ref.at[7 if side == 0 else 0],
+            dst_ref=halo_ref.at[which, side],
+            send_sem=halo_send.at[which, side],
+            recv_sem=halo_recv.at[which, side],
+            device_id={"region": right if side == 0 else left, "rep": rep},
+            device_id_type=MESH,
+        )
+
+    has_right, has_left = region < n_region - 1, region > 0
+
+    def halo_start(which):
+        pl.when(has_right)(lambda: halo_copy(which, 0).start())
+        pl.when(has_left)(lambda: halo_copy(which, 1).start())
+
+    def halo_wait(which):
+        @pl.when(has_left)
+        def _():
+            halo_copy(which, 0).wait_recv()
+
+        @pl.when(has_right)
+        def _():
+            halo_copy(which, 1).wait_recv()
+
+        pl.when(has_right)(lambda: halo_copy(which, 0).wait_send())
+        pl.when(has_left)(lambda: halo_copy(which, 1).wait_send())
+
+    pl.semaphore_wait(barrier, len(partners))
+    halo_start(0)
 
     loads[2].wait()
     eye = iota((64, 256), 0)
@@ -264,12 +311,13 @@
     def weight_back(a):
         return jnp.concatenate([w2b_ref[26 - k] for k in range(9 * a, 9 * a + 9)], axis=1)
 
-    def layer(which, c_ref, store, splitter, tile_lane, windows, weight, product, activate, halo):
+    def layer(which, c_ref, store, splitter, tile_lane, windows, weight, product, activate, between=None):
         build_inner(c_ref, store, splitter, tile_lane)
         conv_inner(windows, weight, product)
+        if between is not None:
+            between()
         pl.loop(1, 7)(activate)
-        for copy in halo:
-            copy.wait()
+        halo_wait(which)
         build_faces(which, c_ref, store, splitter, tile_lane)
         conv_faces(windows, weight, product)
         pl.loop(0, 2)(lambda i: activate(7 * i))
@@ -299,23 +347,25 @@
         rows = pl.ds(pl.multiple_of(x * 64, 64), 64)
         face_ref[x] = (acc_ref[rows, :] * slope_ref[x]).astype(BF16)
 
-    layer(0, c1_ref, store_first, split_first(), even_quarter, windows_first, weight_first, dot, hidden_of, halo)
-    halo = halo_copies(1)
-    for copy in halo:
-        copy.start()
+    layer(0, c1_ref, store_first, split_first(), even_quarter, windows_first, weight_first, dot, hidden_of)
+    halo_start(1)
 
     second = functools.partial(windows_second, c2_ref)
     loads[4].wait()
-    layer(1, c2_ref, store_second, split_second(), first_half, second, weight_second, dot, outputs_of, halo)
-    halo = halo_copies(2)
-    for copy in halo:
-        copy.start()
+    layer(1, c2_ref, store_second, split_second(), first_half, second, weight_second, dot, outputs_of)
+    halo_start(2)
+    block_store = pltpu.make_async_copy(out_ref, out_hbm, store_sem.at[0])
+    block_store.start()
 
     wide_half = iota((64, 128), 1) < 64
     wide_quarter = lax.rem(iota((64, 128), 1) // 32, 2) == 0
-
-    def put_gradient(pair, value):
-        grad_ref[pair // HALF, (pair % HALF) * 4 : (pair % HALF) * 4 + 4] = value.reshape(4, 16, 128)
+    per_core1, per_core2 = PAIRS_FIRST // 2, PAIRS_SECOND // 2
+
+    def put_gradient(full, send, per_core, pair, value):
+        value = value.reshape(4, 16, 128)
+        units = pl.ds((pair % per_core) * 4, 4)
+        full[pair // per_core, units] = value
+        send[pair // per_core, units] = value.astype(BF16)
 
     delta_t = face_ref[...].reshape(512, 128).T
     for pair in range(14):
@@ -328,12 +378,87 @@
         one, two = got[:, :128], got[:, 128:]
         straight = jnp.where(wide_half, one[0:64], two[64:128])
         crossed = jnp.where(wide_half, two[0:64], one[64:128])
-        put_gradient(pair, straight + pltpu.roll(crossed, 64, 1))
+        put_gradient(full2_ref, send2_ref, per_core2, pair, straight + pltpu.roll(crossed, 64, 1))
     for pair in range(14, PAIRS_SECOND):
-        put_gradient(pair, jnp.zeros((64, 128), F32))
+        put_gradient(full2_ref, send2_ref, per_core2, pair, jnp.zeros((64, 128), F32))
+
+    def reducer(which, per_core, full, send, pair, half, plane, line, fin):
+        unit = 4 * per_core // n_plane
+
+        def remote(stage, src, dst, device):
+            return pltpu.make_async_remote_copy(
+                src_ref=src,
+                dst_ref=dst,
+                send_sem=sum_send.at[which, stage],
+                recv_sem=sum_recv.at[which, stage],
+                device_id=device,
+                device_id_type=MESH,
+            )
+
+        mine = fin.at[core, pl.ds(member * unit, unit)]
+        plane_part = plane.at[pl.ds(1, n_plane - 1)]
+        line_part = line.at[pl.ds(0, nz - 1)]
+        back_part = fin.at[core, pl.ds(0, (n_plane - 1) * unit)]
+        whole = [
+            remote(0, send.at[1 - core], pair, twin),
+            remote(1, plane_part, plane_part, twin),
+            remote(2, line_part, line_part, twin),
+            remote(3, back_part, back_part, twin),
+            remote(4, fin.at[core], fin.at[core], twin),
+        ]
+
+        def start_pair():
+            whole[0].start()
+
+        def start_plane():
+            whole[0].wait_recv()
+            total = full[core] + pair[...].astype(F32)
+            full[core] = total
+            half[...] = total.astype(BF16)
+            for step, other, at in plane_peers:
+                remote(1, half.at[pl.ds(other * unit, unit)], plane.at[step], at).start()
+
+        def start_line():
+            whole[1].wait_recv()
+            total = full[core, pl.ds(member * unit, unit)]
+            for step in range(1, n_plane):
+                total = total + plane[step].astype(F32)
+            line[my_z] = total.astype(BF16)
+            for at in line_peers:
+                remote(2, line.at[my_z], line.at[my_z], at).start()
+
+        def start_back():
+            whole[2].wait_recv()
+            total = line[0].astype(F32)
+            for z in range(1, nz):
+                total = total + line[z].astype(F32)
+            fin[core, pl.ds(member * unit, unit)] = (total * scale).astype(BF16)
+            for _, _, at in plane_peers:
+                remote(3, mine, mine, at).start()
+
+        def start_twin():
+            whole[3].wait_recv()
+            whole[4].start()
+
+        def finish():
+            whole[4].wait_recv()
+
+        def sent():
+            for copy in whole:
+                copy.wait_send()
+
+        return start_pair, start_plane, start_line, start_back, start_twin, finish, sent
+
+    sum1 = reducer(
+        0, per_core1, full1_ref, send1_ref, pair1_ref, half1_ref, plane1_ref, line1_ref, fin1_ref
+    )
+    sum2 = reducer(
+        1, per_core2, full2_ref, send2_ref, pair2_ref, half2_ref, plane2_ref, line2_ref, fin2_ref
+    )
+    sum2[0]()
 
     third = functools.partial(windows_second, c3_ref)
-    layer(2, c3_ref, store_second, split_second(), first_half, third, weight_back, dot_nt, back_of, halo)
+    layer(2, c3_ref, store_second, split_second(), first_half, third, weight_back, dot_nt, back_of, sum2[1])
     delta_t = face_ref[...].reshape(512, 128).T
     for pair in range(PAIRS_FIRST):
         both = []
@@ -345,146 +470,57 @@
         straight = jnp.where(wide_quarter, one[0:64], two[64:128])
         crossed = jnp.where(wide_quarter, two[0:64], one[64:128])
         swapped = jnp.where(wide_quarter, pltpu.roll(crossed, 96, 1), pltpu.roll(crossed, 32, 1))
-        put_gradient(PAIRS_SECOND + pair, straight + swapped)
-
-
-def sum_kernel(
-    sizes,
-    scale,
-    grad_ref,
-    fin_ref,
-    send_ref,
-    pair_ref,
-    half_ref,
-    mine_ref,
-    plane_ref,
-    line_ref,
-    pair_send,
-    pair_recv,
-    plane_send,
-    plane_recv,
-    line_send,
-    line_recv,
-    back_send,
-    back_recv,
-    twin_send,
-    twin_recv,
+        put_gradient(full1_ref, send1_ref, per_core1, pair, straight + swapped)
+    sum1[0]()
+    sum2[2]()
+    sum1[1]()
+    sum2[3]()
+    sum1[2]()
+    sum2[4]()
+    sum1[3]()
+    sum2[5]()
+    second_store = pltpu.make_async_copy(fin2_ref, fin2_hbm, store_sem.at[1])
+    second_store.start()
+    sum1[4]()
+    sum2[6]()
+    block_store.wait()
+    sum1[5]()
+    first_store = pltpu.make_async_copy(fin1_ref, fin1_hbm, store_sem.at[2])
+    first_store.start()
+    sum1[6]()
+    second_store.wait()
+    first_store.wait()
+
+
+def unpack_kernel(
+    block_hbm, fin1_hbm, fin2_hbm, out_hbm, g1_hbm, g2_hbm, block_ref, fin1_ref, fin2_ref, g1_ref, g2_ref, sem
 ):
-    nx, nz, ny = sizes
-    n_plane = nx * ny
-    my_x, my_z, my_y, core, region, rep = places(sizes)
-    member = my_x * ny + my_y
-    unit = 4 * HALF // n_plane
-
-    def plane_peer(step):
-        other = lax.rem(member + step, n_plane)
-        return other, {"region": (other // ny) * nz + my_z, "rep": lax.rem(other, ny) * 2 + core}
-
-    def line_peer(step):
-        return {"region": my_x * nz + lax.rem(my_z + step, nz), "rep": rep}
-
-    twin = {"region": region, "rep": my_y * 2 + 1 - core}
-
-    barrier = pltpu.get_barrier_semaphore()
-    pl.semaphore_signal(barrier, inc=1, device_id=twin, device_id_type=MESH)
-
-    @pl.loop(1, n_plane)
-    def _(step):
-        pl.semaphore_signal(barrier, inc=1, device_id=plane_peer(step)[1], device_id_type=MESH)
-
-    @pl.loop(1, nz)
-    def _(step):
-        pl.semaphore_signal(barrier, inc=1, device_id=line_peer(step), device_id_type=MESH)
-
-    def remote(src, dst, send_sem, recv_sem, device):
-        return pltpu.make_async_remote_copy(
-            src_ref=src,
-            dst_ref=dst,
-            send_sem=send_sem,
-            recv_sem=recv_sem,
-            device_id=device,
-            device_id_type=MESH,
+    loads = [
+        pltpu.make_async_copy(src, dst, sem.at[i])
+        for i, (src, dst) in enumerate(
+            ((fin2_hbm, fin2_ref), (fin1_hbm, fin1_ref), (block_hbm, block_ref))
         )
-
-    def plane_copy(step):
-        other, device = plane_peer(step)
-        source = half_ref.at[pl.ds(other * unit, unit)]
-        return remote(source, plane_ref.at[step], plane_send.at[step], plane_recv.at[step], device)
-
-    def line_copy(step):
-        place = line_ref.at[my_z]
-        return remote(place, place, line_send.at[step], line_recv.at[step], line_peer(step))
-
-    def back_copy(step):
-        place = fin_ref.at[core, pl.ds(member * unit, unit)]
-        return remote(place, place, back_send.at[step], back_recv.at[step], plane_peer(step)[1])
-
-    send_ref[...] = grad_ref[1 - core].astype(BF16)
-    pl.semaphore_wait(barrier, 1 + n_plane - 1 + nz - 1)
-    pair_copy = remote(send_ref, pair_ref, pair_send.at[0], pair_recv.at[0], twin)
-    pair_copy.start()
-    pair_copy.wait()
-    total = grad_ref[core] + pair_ref[...].astype(F32)
-    half_ref[...] = total.astype(BF16)
-    mine_ref[...] = total
-
-    @pl.loop(1, n_plane)
-    def _(step):
-        plane_copy(step).start()
-
-    @pl.loop(1, n_plane)
-    def _(step):
-        plane_copy(step).wait()
-
-    total = mine_ref[pl.ds(member * unit, unit)]
-    for step in range(1, n_plane):
-        total = total + plane_ref[step].astype(F32)
-    line_ref[my_z] = total.astype(BF16)
-
-    @pl.loop(1, nz)
-    def _(step):
-        line_copy(step).start()
-
-    @pl.loop(1, nz)
-    def _(step):
-        line_copy(step).wait()
-
-    total = line_ref[0].astype(F32)
-    for z in range(1, nz):
-        total = total + line_ref[z].astype(F32)
-    fin_ref[core, pl.ds(member * unit, unit)] = (total * scale).astype(BF16)
-
-    @pl.loop(1, n_plane)
-    def _(step):
-        back_copy(step).start()
-
-    @pl.loop(1, n_plane)
-    def _(step):
-        back_copy(step).wait()
-
-    twin_copy = remote(fin_ref.at[core], fin_ref.at[core], twin_send.at[0], twin_recv.at[0], twin)
-    twin_copy.start()
-    twin_copy.wait()
-
-
-def unpack_kernel(block_ref, fin_ref, out_hbm, g1_hbm, g2_hbm, g1_ref, g2_ref, sem):
-    block_copy = pltpu.make_async_copy(block_ref, out_hbm, sem.at[0])
+    ]
+    for load in loads:
+        load.start()
+    loads[0].wait()
+    for pair in range(14):
+        at = (pair % (PAIRS_SECOND // 2)) * 4
+        value = fin2_ref[pair // (PAIRS_SECOND // 2), at : at + 4].reshape(64, 128).astype(F32).T
+        g2_ref[2 * pair] = value[0:64]
+        if pair < 13:
+            g2_ref[2 * pair + 1] = value[64:128]
+    second_copy = pltpu.make_async_copy(g2_ref, g2_hbm, sem.at[3])
+    second_copy.start()
+    loads[2].wait()
+    block_copy = pltpu.make_async_copy(block_ref, out_hbm, sem.at[4])
     block_copy.start()
-    for pair in range(PAIRS_SECOND + PAIRS_FIRST):
-        if pair in (14, 15):
-            continue
-        at = (pair % HALF) * 4
-        value = fin_ref[pair // HALF, at : at + 4].reshape(64, 128).astype(F32).T
-        if pair < 14:
-            g2_ref[2 * pair] = value[0:64]
-            if pair < 13:
-                g2_ref[2 * pair + 1] = value[64:128]
-            continue
-        if pair == PAIRS_SECOND:
-            second_copy = pltpu.make_async_copy(g2_ref, g2_hbm, sem.at[1])
-            second_copy.start()
+    loads[1].wait()
+    for pair in range(PAIRS_FIRST):
+        at = (pair % (PAIRS_FIRST // 2)) * 4
+        value = fin1_ref[pair // (PAIRS_FIRST // 2), at : at + 4].reshape(64, 128).astype(F32).T
         for j in range(2):
-            block = 2 * (pair - PAIRS_SECOND) + j
+            block = 2 * pair + j
             if block > 14:
                 continue
             a, kind = block // 5, block % 5
@@ -496,10 +532,10 @@
                 offsets = (9 * a + 4,)
             for i, k in enumerate(offsets):
                 g1_ref[k] = value[64 * i + 32 * j : 64 * i + 32 * j + 32]
-    first_copy = pltpu.make_async_copy(g1_ref, g1_hbm, sem.at[2])
+    first_copy = pltpu.make_async_copy(g1_ref, g1_hbm, sem.at[5])
     first_copy.start()
+    second_copy.wait()
     block_copy.wait()
-    second_copy.wait()
     first_copy.wait()
 
 
@@ -509,23 +545,24 @@
     nz = n_region // nx
     sizes = (nx, nz, ny)
     n_plane = nx * ny
-    units = 4 * HALF
-    unit = units // n_plane
+    core1, core2 = 2 * PAIRS_FIRST, 2 * PAIRS_SECOND
+    unit1, unit2 = core1 // n_plane, core2 // n_plane
     vmem = pl.BlockSpec(memory_space=pltpu.VMEM)
     smem = pl.BlockSpec(memory_space=pltpu.SMEM)
-    hbm = pl.BlockSpec(memory_space=pl.ANY)
+    anywhere = pl.BlockSpec(memory_space=pl.ANY)
     dma = pltpu.SemaphoreType.DMA
 
     def body(features, weight_first, weight_second, cotangent, neighbours, voxel_mask):
         scale = 1.0 / math.sqrt(n_rep * 2 * n_region * 512)
-        block, grad = pl.pallas_call(
-            functools.partial(compute_kernel, sizes),
+        block, fin1, fin2 = pl.pallas_call(
+            functools.partial(main_kernel, sizes, scale),
             out_shape=(
                 jax.ShapeDtypeStruct((512, 128), BF16),
-                jax.ShapeDtypeStruct((2, units, 16, 128), F32),
+                jax.ShapeDtypeStruct((2, core1, 16, 128), BF16),
+                jax.ShapeDtypeStruct((2, core2, 16, 128), BF16),
             ),
-            in_specs=[hbm, hbm, hbm, hbm, smem, hbm],
-            out_specs=(vmem, vmem),
+            in_specs=[anywhere, anywhere, anywhere, anywhere, smem, anywhere],
+            out_specs=(anywhere, anywhere, anywhere),
             scratch_shapes=[
                 pltpu.VMEM((64, 512), BF16),
                 pltpu.VMEM((27, 32, 64), BF16),
@@ -545,9 +582,27 @@
                 pltpu.VMEM((27, 128, 128), BF16),
                 pltpu.VMEM((512, 128), F32),
                 pltpu.VMEM((8, 64, 128), F32),
+                pltpu.VMEM((2, core1, 16, 128), F32),
+                pltpu.VMEM((2, core2, 16, 128), F32),
+                pltpu.VMEM((2, core1, 16, 128), BF16),
+                pltpu.VMEM((2, core2, 16, 128), BF16),
+                pltpu.VMEM((core1, 16, 128), BF16),
+                pltpu.VMEM((core2, 16, 128), BF16),
+                pltpu.VMEM((core1, 16, 128), BF16),
+                pltpu.VMEM((core2, 16, 128), BF16),
+                pltpu.VMEM((n_plane, unit1, 16, 128), BF16),
+                pltpu.VMEM((n_plane, unit2, 16, 128), BF16),
+                pltpu.VMEM((nz, unit1, 16, 128), BF16),
+                pltpu.VMEM((nz, unit2, 16, 128), BF16),
+                pltpu.VMEM((2, core1, 16, 128), BF16),
+                pltpu.VMEM((2, core2, 16, 128), BF16),
+                pltpu.VMEM((512, 128), BF16),
                 dma((5,)),
+                dma((3,)),
                 dma((3, 2)),
                 dma((3, 2)),
+                dma((2, 5)),
+                dma((2, 5)),
             ],
             compiler_params=pltpu.CompilerParams(
                 collective_id=0, has_side_effects=True, vmem_limit_bytes=56 * 2**20
@@ -560,33 +615,6 @@
             neighbours.reshape(2, 27),
             voxel_mask.reshape(2, 512),
         )
-        fin = pl.pallas_call(
-            functools.partial(sum_kernel, sizes, scale),
-            out_shape=jax.ShapeDtypeStruct((2, units, 16, 128), BF16),
-            in_specs=[vmem],
-            out_specs=vmem,
-            scratch_shapes=[
-                pltpu.VMEM((units, 16, 128), BF16),
-                pltpu.VMEM((units, 16, 128), BF16),
-                pltpu.VMEM((units, 16, 128), BF16),
-                pltpu.VMEM((units, 16, 128), F32),
-                pltpu.VMEM((n_plane, unit, 16, 128), BF16),
-                pltpu.VMEM((nz, unit, 16, 128), BF16),
-                dma((1,)),
-                dma((1,)),
-                dma((n_plane,)),
-                dma((n_plane,)),
-                dma((nz,)),
-                dma((nz,)),
-                dma((n_plane,)),
-                dma((n_plane,)),
-                dma((1,)),
-                dma((1,)),
-            ],
-            compiler_params=pltpu.CompilerParams(
-                collective_id=1, has_side_effects=True, vmem_limit_bytes=40 * 2**20
-            ),
-        )(grad)
         out, g1, g2 = pl.pallas_call(
             unpack_kernel,
             out_shape=(
@@ -594,15 +622,18 @@
                 jax.ShapeDtypeStruct((27, 32, 64), F32),
                 jax.ShapeDtypeStruct((27, 64, 64), F32),
             ),
-            in_specs=[vmem, vmem],
-            out_specs=(hbm, hbm, hbm),
+            in_specs=[anywhere, anywhere, anywhere],
+            out_specs=(anywhere, anywhere, anywhere),
             scratch_shapes=[
+                pltpu.VMEM((512, 128), BF16),
+                pltpu.VMEM((2, core1, 16, 128), BF16),
+                pltpu.VMEM((2, core2, 16, 128), BF16),
                 pltpu.VMEM((27, 32, 64), F32),
                 pltpu.VMEM((27, 64, 64), F32),
-                dma((3,)),
+                dma((6,)),
             ],
-            compiler_params=pltpu.CompilerParams(vmem_limit_bytes=40 * 2**20),
-        )(block, fin)
+            compiler_params=pltpu.CompilerParams(vmem_limit_bytes=56 * 2**20),
+        )(block, fin1, fin2)
         return out.reshape(1, 512, 128), g1, g2
 
     in_specs = (

time: 52.1 us -> 47 us (0.902)
  Pallas kernels: 50.2 us -> 46.2 us
  local copies, waits for them, and re-layouts: 1.13 us -> 0 us
    pallas_call x2 -> x1, Pallas kernels: 48.9 us -> 43.9 us  [body(): pl.pallas_call(functools.partial(main_kernel, sizes, scale), out_shape=(j...]
    unnamed x4 -> x0, local copies, waits for them, and re-layouts: 1.13 us -> none
    pallas_call x1, Pallas kernels: 1.29 us -> 2.31 us  [body(): pl.pallas_call(unpack_kernel, out_shape=(jax.ShapeDtypeStruct((512, 128),...]
where the time goes in v3:
time: 47 us; the launch traced here: 46.8 us
  Pallas kernels  46.2 us (98%)
  between operations  0.64 us (1%)
    pallas_call x1, Pallas kernels, body(): pl.pallas_call(functools.partial(main_kernel, sizes, scale), out_shape=(j...  43.9 us
    pallas_call x1, Pallas kernels, body(): pl.pallas_call(unpack_kernel, out_shape=(jax.ShapeDtypeStruct((512, 128),...  2.31 us

profile of v3, /device:TPU:1, one launch (start us, length us, event | category | flops | bytes accessed | tf_op | source)
XLA Modules:
  0.0 46.8 jit_solution(8022198534617326512)
XLA Ops:
  0.6 43.9 %shard_map.85 = (bf16[512,128]{1,0:T(8,128)(2,1)}, bf16[2,16,16,128]{3,2,1,0:T(8,128)(2,1)}, bf16[2,32,16,128]{3,2,1,0:T(8,128)(2,1)}) custom-call(bf16[64,512]{1,0:T(8,128)(2,1)} %bitcast.8, bf16[27,32,64]{2,1,0:T(8,128)(2,1)} %w1_hbm.1, bf16[27,64,64]{2,1,0:T(8,128)(2,1)} %w2_hbm.1, bf16[512,128]{1,0:T(8,128)(2,1)} %bitcast.7, s32[2,27]{1,0:T(2,128)} %bitcast.10, ...), custom_call_target="tpu_custom_call" | custom-call | tf_op jit(solution)/shard_map/pallas_call | solution.py:557
  44.5 2.3 %shard_map.86 = (bf16[512,128]{1,0:T(8,128)(2,1)}, f32[27,32,64]{2,1,0:T(8,128)}, f32[27,64,64]{2,1,0:T(8,128)}) custom-call(bf16[512,128]{1,0:T(8,128)(2,1)} %get-tuple-element.9.block_hbm, bf16[2,16,16,128]{3,2,1,0:T(8,128)(2,1)} %get-tuple-element.10.fin1_hbm, bf16[2,32,16,128]{3,2,1,0:T(8,128)(2,1)} %get-tuple-element.11.fin2_hbm), custom_call_target="tpu_custom_call" | custom-call | tf_op jit(solution)/shard_map/pallas_call | solution.py:618

commit v4 on v3

--- a/solution.py
+++ b/solution.py
@@ -45,9 +45,9 @@
     cot_hbm,
     nbr_ref,
     mask_hbm,
-    out_hbm,
-    fin1_hbm,
-    fin2_hbm,
+    out_ref,
+    fin1_ref,
+    g2_ref,
     feat_ref,
     w1_ref,
     w2_ref,
@@ -78,11 +78,8 @@
     plane2_ref,
     line1_ref,
     line2_ref,
-    fin1_ref,
     fin2_ref,
-    out_ref,
     load_sem,
-    store_sem,
     halo_send,
     halo_recv,
     sum_send,
@@ -245,7 +242,7 @@
             for t in range(2)
         ]
 
-        @pl.loop(0, 8)
+        @pl.loop(0, 8, unroll=4)
         def _(x):
             def load(b, c, start, stop):
                 k = 3 * b + c
@@ -316,11 +313,11 @@
         conv_inner(windows, weight, product)
         if between is not None:
             between()
-        pl.loop(1, 7)(activate)
+        pl.loop(1, 7, unroll=3)(activate)
         halo_wait(which)
         build_faces(which, c_ref, store, splitter, tile_lane)
         conv_faces(windows, weight, product)
-        pl.loop(0, 2)(lambda i: activate(7 * i))
+        pl.loop(0, 2, unroll=2)(lambda i: activate(7 * i))
 
     def hidden_of(x):
         rows = pl.ds(pl.multiple_of(x * 64, 64), 64)
@@ -354,8 +351,6 @@
     loads[4].wait()
     layer(1, c2_ref, store_second, split_second(), first_half, second, weight_second, dot, outputs_of)
     halo_start(2)
-    block_store = pltpu.make_async_copy(out_ref, out_hbm, store_sem.at[0])
-    block_store.start()
 
     wide_half = iota((64, 128), 1) < 64
     wide_quarter = lax.rem(iota((64, 128), 1) // 32, 2) == 0
@@ -479,46 +474,27 @@
     sum2[4]()
     sum1[3]()
     sum2[5]()
-    second_store = pltpu.make_async_copy(fin2_ref, fin2_hbm, store_sem.at[1])
-    second_store.start()
-    sum1[4]()
-    sum2[6]()
-    block_store.wait()
-    sum1[5]()
-    first_store = pltpu.make_async_copy(fin1_ref, fin1_hbm, store_sem.at[2])
-    first_store.start()
-    sum1[6]()
-    second_store.wait()
-    first_store.wait()
-
-
-def unpack_kernel(
-    block_hbm, fin1_hbm, fin2_hbm, out_hbm, g1_hbm, g2_hbm, block_ref, fin1_ref, fin2_ref, g1_ref, g2_ref, sem
-):
-    loads = [
-        pltpu.make_async_copy(src, dst, sem.at[i])
-        for i, (src, dst) in enumerate(
-            ((fin2_hbm, fin2_ref), (fin1_hbm, fin1_ref), (block_hbm, block_ref))
-        )
-    ]
-    for load in loads:
-        load.start()
-    loads[0].wait()
     for pair in range(14):
-        at = (pair % (PAIRS_SECOND // 2)) * 4
-        value = fin2_ref[pair // (PAIRS_SECOND // 2), at : at + 4].reshape(64, 128).astype(F32).T
+        units = pl.ds((pair % per_core2) * 4, 4)
+        value = fin2_ref[pair // per_core2, units].reshape(64, 128).astype(F32).T
         g2_ref[2 * pair] = value[0:64]
         if pair < 13:
             g2_ref[2 * pair + 1] = value[64:128]
-    second_copy = pltpu.make_async_copy(g2_ref, g2_hbm, sem.at[3])
+    sum1[4]()
+    sum2[6]()
+    sum1[5]()
+    sum1[6]()
+
+
+def unpack_kernel(block_ref, fin_ref, g2_ref, out_hbm, g1_hbm, g2_hbm, g1_ref, sem):
+    block_copy = pltpu.make_async_copy(block_ref, out_hbm, sem.at[0])
+    second_copy = pltpu.make_async_copy(g2_ref, g2_hbm, sem.at[1])
+    first_copy = pltpu.make_async_copy(g1_ref, g1_hbm, sem.at[2])
     second_copy.start()
-    loads[2].wait()
-    block_copy = pltpu.make_async_copy(block_ref, out_hbm, sem.at[4])
     block_copy.start()
-    loads[1].wait()
     for pair in range(PAIRS_FIRST):
         at = (pair % (PAIRS_FIRST // 2)) * 4
-        value = fin1_ref[pair // (PAIRS_FIRST // 2), at : at + 4].reshape(64, 128).astype(F32).T
+        value = fin_ref[pair // (PAIRS_FIRST // 2), at : at + 4].reshape(64, 128).astype(F32).T
         for j in range(2):
             block = 2 * pair + j
             if block > 14:
@@ -532,7 +508,6 @@
                 offsets = (9 * a + 4,)
             for i, k in enumerate(offsets):
                 g1_ref[k] = value[64 * i + 32 * j : 64 * i + 32 * j + 32]
-    first_copy = pltpu.make_async_copy(g1_ref, g1_hbm, sem.at[5])
     first_copy.start()
     second_copy.wait()
     block_copy.wait()
@@ -549,20 +524,21 @@
     unit1, unit2 = core1 // n_plane, core2 // n_plane
     vmem = pl.BlockSpec(memory_space=pltpu.VMEM)
     smem = pl.BlockSpec(memory_space=pltpu.SMEM)
+    hbm = pl.BlockSpec(memory_space=pltpu.HBM)
     anywhere = pl.BlockSpec(memory_space=pl.ANY)
     dma = pltpu.SemaphoreType.DMA
 
     def body(features, weight_first, weight_second, cotangent, neighbours, voxel_mask):
         scale = 1.0 / math.sqrt(n_rep * 2 * n_region * 512)
-        block, fin1, fin2 = pl.pallas_call(
+        block, fin1, g2 = pl.pallas_call(
             functools.partial(main_kernel, sizes, scale),
             out_shape=(
                 jax.ShapeDtypeStruct((512, 128), BF16),
                 jax.ShapeDtypeStruct((2, core1, 16, 128), BF16),
-                jax.ShapeDtypeStruct((2, core2, 16, 128), BF16),
+                jax.ShapeDtypeStruct((27, 64, 64), F32),
             ),
-            in_specs=[anywhere, anywhere, anywhere, anywhere, smem, anywhere],
-            out_specs=(anywhere, anywhere, anywhere),
+            in_specs=[hbm, hbm, hbm, hbm, smem, hbm],
+            out_specs=(vmem, vmem, vmem),
             scratch_shapes=[
                 pltpu.VMEM((64, 512), BF16),
                 pltpu.VMEM((27, 32, 64), BF16),
@@ -594,26 +570,28 @@
                 pltpu.VMEM((n_plane, unit2, 16, 128), BF16),
                 pltpu.VMEM((nz, unit1, 16, 128), BF16),
                 pltpu.VMEM((nz, unit2, 16, 128), BF16),
-                pltpu.VMEM((2, core1, 16, 128), BF16),
                 pltpu.VMEM((2, core2, 16, 128), BF16),
-                pltpu.VMEM((512, 128), BF16),
                 dma((5,)),
-                dma((3,)),
                 dma((3, 2)),
                 dma((3, 2)),
                 dma((2, 5)),
                 dma((2, 5)),
             ],
             compiler_params=pltpu.CompilerParams(
-                collective_id=0, has_side_effects=True, vmem_limit_bytes=56 * 2**20
+                collective_id=0, has_side_effects=True, vmem_limit_bytes=40 * 2**20
             ),
         )(
-            jnp.swapaxes(features, 1, 2).reshape(64, 512),
-            weight_first,
-            weight_second,
-            cotangent.reshape(512, 128),
-            neighbours.reshape(2, 27),
-            voxel_mask.reshape(2, 512),
+            *(
+                pltpu.with_memory_space_constraint(x, pltpu.HBM)
+                for x in (
+                    jnp.swapaxes(features, 1, 2).reshape(64, 512),
+                    weight_first,
+                    weight_second,
+                    cotangent.reshape(512, 128),
+                    neighbours.reshape(2, 27),
+                    voxel_mask.reshape(2, 512),
+                )
+            )
         )
         out, g1, g2 = pl.pallas_call(
             unpack_kernel,
@@ -622,18 +600,14 @@
                 jax.ShapeDtypeStruct((27, 32, 64), F32),
                 jax.ShapeDtypeStruct((27, 64, 64), F32),
             ),
-            in_specs=[anywhere, anywhere, anywhere],
+            in_specs=[vmem, vmem, vmem],
             out_specs=(anywhere, anywhere, anywhere),
             scratch_shapes=[
-                pltpu.VMEM((512, 128), BF16),
-                pltpu.VMEM((2, core1, 16, 128), BF16),
-                pltpu.VMEM((2, core2, 16, 128), BF16),
                 pltpu.VMEM((27, 32, 64), F32),
-                pltpu.VMEM((27, 64, 64), F32),
-                dma((6,)),
+                dma((3,)),
             ],
-            compiler_params=pltpu.CompilerParams(vmem_limit_bytes=56 * 2**20),
-        )(block, fin1, fin2)
+            compiler_params=pltpu.CompilerParams(vmem_limit_bytes=40 * 2**20),
+        )(block, fin1, g2)
         return out.reshape(1, 512, 128), g1, g2
 
     in_specs = (

time: 47 us -> 45 us (0.957)
  Pallas kernels: 46.2 us -> 44.3 us
    pallas_call x1, Pallas kernels: 2.31 us -> 1.12 us  [body(): pl.pallas_call(unpack_kernel, out_shape=(jax.ShapeDtypeStruct((512, 128),...]
    pallas_call x1, Pallas kernels: 43.9 us -> 43.1 us  [body(): pl.pallas_call(functools.partial(main_kernel, sizes, scale), out_shape=(j...]
where the time goes in v4:
time: 45 us; the launch traced here: 44.9 us
  Pallas kernels  44.3 us (98%)
  between operations  0.64 us (1%)
    pallas_call x1, Pallas kernels, body(): pl.pallas_call(functools.partial(main_kernel, sizes, scale), out_shape=(j...  43.1 us
    pallas_call x1, Pallas kernels, body(): pl.pallas_call(unpack_kernel, out_shape=(jax.ShapeDtypeStruct((512, 128),...  1.12 us

profile of v4, /device:TPU:1, one launch (start us, length us, event | category | flops | bytes accessed | tf_op | source)
XLA Modules:
  0.0 44.9 jit_solution(13873019550164385206)
XLA Ops:
  0.6 43.1 %shard_map.85 = (bf16[512,128]{1,0:T(8,128)(2,1)S(1)}, bf16[2,16,16,128]{3,2,1,0:T(8,128)(2,1)S(1)}, f32[27,64,64]{2,1,0:T(8,128)S(1)}) custom-call(bf16[64,512]{1,0:T(8,128)(2,1)} %bitcast.8, bf16[27,32,64]{2,1,0:T(8,128)(2,1)} %w1_hbm.1, bf16[27,64,64]{2,1,0:T(8,128)(2,1)} %w2_hbm.1, bf16[512,128]{1,0:T(8,128)(2,1)} %bitcast.7, s32[2,27]{1,0:T(2,128)} %bitcast.10, ...), custom_call_target="tpu_custom_call" | custom-call | tf_op jit(solution)/shard_map/pallas_call | solution.py:533
  43.8 1.1 %shard_map.86 = (bf16[512,128]{1,0:T(8,128)(2,1)}, f32[27,32,64]{2,1,0:T(8,128)}, f32[27,64,64]{2,1,0:T(8,128)}) custom-call(bf16[512,128]{1,0:T(8,128)(2,1)S(1)} %get-tuple-element.9.block_ref, bf16[2,16,16,128]{3,2,1,0:T(8,128)(2,1)S(1)} %get-tuple-element.10.fin_ref, f32[27,64,64]{2,1,0:T(8,128)S(1)} %get-tuple-element.11.g2_ref), custom_call_target="tpu_custom_call" | custom-call | tf_op jit(solution)/shard_map/pallas_call | solution.py:596

commit v5 on v4

--- a/solution.py
+++ b/solution.py
@@ -183,8 +183,12 @@
     w1b_ref[:, 4, 64:128, :] = jnp.zeros((3, 64, 128), BF16)
     loads[3].wait()
     spread2 = dot(w2_ref[...].reshape(27 * 64, 64), put).astype(BF16)
-    w2b_ref[:, 0:64, :] = spread2[:, :128].reshape(27, 64, 128)
-    w2b_ref[:, 64:128, :] = spread2[:, 128:].reshape(27, 64, 128)
+    top = spread2[:, :128].reshape(27, 64, 128)
+    low = spread2[:, 128:].reshape(27, 64, 128)
+    for k in range(27):
+        a, b, c = k // 9, k // 3 % 3, k % 3
+        w2b_ref[b, 3 * c + a, 0:64, :] = top[k]
+        w2b_ref[b, 3 * c + a, 64:128, :] = low[k]
 
     side_ref[2] = jnp.zeros((8, 64, 128), F32)
     far_ref[:, 2] = jnp.zeros((2, 64, 128), F32)
@@ -277,46 +281,62 @@
 
             store(c_ref, 9 * side, *shifted(None, load, tile_lane))
 
-    def windows_first(start, count):
-        return [
-            c1_ref[start : start + count, r : r + 64, :].reshape(count * 64, 128)
-            for r in ROWS_FIRST
-        ]
-
-    def windows_second(c_ref, start, count):
-        return [
-            c_ref[c, start : start + count, ROWS[b] : ROWS[b] + 64, :].reshape(count * 64, 128)
-            for b in range(3)
-            for c in range(3)
-        ]
-
-    def conv_inner(windows, weight, product=dot):
-        acc_ref[...] = product(jnp.concatenate(windows(1, 8), axis=1), weight(1))
-        acc_ref[64:512] += product(jnp.concatenate(windows(1, 7), axis=1), weight(0))
-        acc_ref[0:448] += product(jnp.concatenate(windows(2, 7), axis=1), weight(2))
-
-    def conv_faces(windows, weight, product=dot):
-        acc_ref[0:64] += product(jnp.concatenate(windows(0, 1), axis=1), weight(0))
-        acc_ref[448:512] += product(jnp.concatenate(windows(9, 1), axis=1), weight(2))
-
-    def weight_first(a):
-        return w1b_ref[a].reshape(5 * 128, 128)
-
-    def weight_second(a):
-        return w2b_ref[9 * a : 9 * a + 9].reshape(9 * 128, 128)
-
-    def weight_back(a):
-        return jnp.concatenate([w2b_ref[26 - k] for k in range(9 * a, 9 * a + 9)], axis=1)
-
-    def layer(which, c_ref, store, splitter, tile_lane, windows, weight, product, activate, between=None):
+    for x in (0, 9):
+        c1_ref[x] = jnp.zeros((272, 128), BF16)
+        c2_ref[:, x] = jnp.zeros((3, 144, 128), BF16)
+        c3_ref[:, x] = jnp.zeros((3, 144, 128), BF16)
+
+    def conv_first():
+        acc_ref[...] = jnp.zeros((512, 128), F32)
+
+        @pl.loop(0, 3)
+        def _(a):
+            windows = [c1_ref[pl.ds(a, 8), r : r + 64, :].reshape(512, 128) for r in ROWS_FIRST]
+            acc_ref[...] += dot(jnp.concatenate(windows, axis=1), w1b_ref[a].reshape(5 * 128, 128))
+
+    def faces_first():
+        for a, slab, at in ((0, 0, 0), (2, 9, 448)):
+            windows = [c1_ref[slab, r : r + 64, :] for r in ROWS_FIRST]
+            acc_ref[at : at + 64] += dot(
+                jnp.concatenate(windows, axis=1), w1b_ref[a].reshape(5 * 128, 128)
+            )
+
+    def weight_second(b, blocks):
+        return jnp.concatenate([w2b_ref[b, n] for n in blocks], axis=0)
+
+    def weight_back(b, blocks):
+        return jnp.concatenate([w2b_ref[2 - b, 8 - n] for n in blocks], axis=1)
+
+    def conv_second(c_ref, weight, product):
+        acc_ref[...] = jnp.zeros((512, 128), F32)
+
+        @pl.loop(0, 3)
+        def _(b):
+            rows = pl.ds(pl.multiple_of(80 * b * (2 - b) + 8 * b * (b - 1), 16), 64)
+            windows = [
+                c_ref[c, a : a + 8, rows, :].reshape(512, 128) for c in range(3) for a in range(3)
+            ]
+            acc_ref[...] += product(jnp.concatenate(windows, axis=1), weight(b, range(9)))
+
+    def faces_second(c_ref, weight, product, join):
+        for a, slab, at in ((0, 0, 0), (2, 9, 448)):
+            windows = [
+                c_ref[c, slab, ROWS[b] : ROWS[b] + 64, :] for b in range(3) for c in range(3)
+            ]
+            weights = [weight(b, range(a, 9, 3)) for b in range(3)]
+            acc_ref[at : at + 64] += product(
+                jnp.concatenate(windows, axis=1), jnp.concatenate(weights, axis=join)
+            )
+
+    def layer(which, c_ref, store, splitter, tile_lane, inner, faces, activate, between=None):
         build_inner(c_ref, store, splitter, tile_lane)
-        conv_inner(windows, weight, product)
+        inner()
         if between is not None:
             between()
         pl.loop(1, 7, unroll=3)(activate)
         halo_wait(which)
         build_faces(which, c_ref, store, splitter, tile_lane)
-        conv_faces(windows, weight, product)
+        faces()
         pl.loop(0, 2, unroll=2)(lambda i: activate(7 * i))
 
     def hidden_of(x):
@@ -344,12 +364,20 @@
         rows = pl.ds(pl.multiple_of(x * 64, 64), 64)
         face_ref[x] = (acc_ref[rows, :] * slope_ref[x]).astype(BF16)
 
-    layer(0, c1_ref, store_first, split_first(), even_quarter, windows_first, weight_first, dot, hidden_of)
+    layer(0, c1_ref, store_first, split_first(), even_quarter, conv_first, faces_first, hidden_of)
     halo_start(1)
 
-    second = functools.partial(windows_second, c2_ref)
     loads[4].wait()
-    layer(1, c2_ref, store_second, split_second(), first_half, second, weight_second, dot, outputs_of)
+    layer(
+        1,
+        c2_ref,
+        store_second,
+        split_second(),
+        first_half,
+        lambda: conv_second(c2_ref, weight_second, dot),
+        lambda: faces_second(c2_ref, weight_second, dot, 0),
+        outputs_of,
+    )
     halo_start(2)
 
     wide_half = iota((64, 128), 1) < 64
@@ -452,8 +480,17 @@
     )
     sum2[0]()
 
-    third = functools.partial(windows_second, c3_ref)
-    layer(2, c3_ref, store_second, split_second(), first_half, third, weight_back, dot_nt, back_of, sum2[1])
+    layer(
+        2,
+        c3_ref,
+        store_second,
+        split_second(),
+        first_half,
+        lambda: conv_second(c3_ref, weight_back, dot_nt),
+        lambda: faces_second(c3_ref, weight_back, dot_nt, 1),
+        back_of,
+        sum2[1],
+    )
     delta_t = face_ref[...].reshape(512, 128).T
     for pair in range(PAIRS_FIRST):
         both = []
@@ -555,7 +592,7 @@
                 pltpu.VMEM((3, 10, 144, 128), BF16),
                 pltpu.VMEM((3, 10, 144, 128), BF16),
                 pltpu.VMEM((3, 5, 128, 128), BF16),
-                pltpu.VMEM((27, 128, 128), BF16),
+                pltpu.VMEM((3, 9, 128, 128), BF16),
                 pltpu.VMEM((512, 128), F32),
                 pltpu.VMEM((8, 64, 128), F32),
                 pltpu.VMEM((2, core1, 16, 128), F32),

time: 45 us -> 45.4 us (level)
  no operation moved by 1% of the time
where the time goes in v5:
time: 45.4 us; the launch traced here: 45.3 us
  Pallas kernels  44.6 us (98%)
  between operations  0.64 us (1%)
    pallas_call x1, Pallas kernels, body(): pl.pallas_call(functools.partial(main_kernel, sizes, scale), out_shape=(j...  43.5 us
    pallas_call x1, Pallas kernels, body(): pl.pallas_call(unpack_kernel, out_shape=(jax.ShapeDtypeStruct((512, 128),...  1.12 us

profile of v5, /device:TPU:1, one launch (start us, length us, event | category | flops | bytes accessed | tf_op | source)
XLA Modules:
  0.0 45.3 jit_solution(8999004599494449618)
XLA Ops:
  0.6 43.5 %shard_map.85 = (bf16[512,128]{1,0:T(8,128)(2,1)S(1)}, bf16[2,16,16,128]{3,2,1,0:T(8,128)(2,1)S(1)}, f32[27,64,64]{2,1,0:T(8,128)S(1)}) custom-call(bf16[64,512]{1,0:T(8,128)(2,1)} %bitcast.8, bf16[27,32,64]{2,1,0:T(8,128)(2,1)} %w1_hbm.1, bf16[27,64,64]{2,1,0:T(8,128)(2,1)} %w2_hbm.1, bf16[512,128]{1,0:T(8,128)(2,1)} %bitcast.7, s32[2,27]{1,0:T(2,128)} %bitcast.10, ...), custom_call_target="tpu_custom_call" | custom-call | tf_op jit(solution)/shard_map/pallas_call | solution.py:570
  44.1 1.1 %shard_map.86 = (bf16[512,128]{1,0:T(8,128)(2,1)}, f32[27,32,64]{2,1,0:T(8,128)}, f32[27,64,64]{2,1,0:T(8,128)}) custom-call(bf16[512,128]{1,0:T(8,128)(2,1)S(1)} %get-tuple-element.9.block_ref, bf16[2,16,16,128]{3,2,1,0:T(8,128)(2,1)S(1)} %get-tuple-element.10.fin_ref, f32[27,64,64]{2,1,0:T(8,128)S(1)} %get-tuple-element.11.g2_ref), custom_call_target="tpu_custom_call" | custom-call | tf_op jit(solution)/shard_map/pallas_call | solution.py:633

commit v6 on v4

--- a/solution.py
+++ b/solution.py
@@ -70,18 +70,18 @@
     full2_ref,
     send1_ref,
     send2_ref,
-    pair1_ref,
     pair2_ref,
-    half1_ref,
     half2_ref,
-    plane1_ref,
-    plane2_ref,
+    mine2_ref,
+    parts1_ref,
+    parts2_ref,
     line1_ref,
     line2_ref,
     fin2_ref,
     load_sem,
     halo_send,
     halo_recv,
+    pair_sem,
     sum_send,
     sum_recv,
 ):
@@ -92,20 +92,33 @@
     right = lax.rem(region + 1, n_region)
     left = lax.rem(region + n_region - 1, n_region)
     twin = {"region": region, "rep": my_y * 2 + 1 - core}
-    plane_peers = []
-    for step in range(1, n_plane):
-        other = lax.rem(member + step, n_plane)
-        at = {"region": (other // ny) * nz + my_z, "rep": lax.rem(other, ny) * 2 + core}
-        plane_peers.append((step, other, at))
+
+    def apart(offset, size):
+        return min(offset, size - offset)
+
+    offsets = sorted(
+        ((dx, dy, dc) for dx in range(nx) for dy in range(ny) for dc in range(2)),
+        key=lambda d: (-apart(d[0], nx) - apart(d[1], ny), d),
+    )
+    plane_peers, all_peers = [], []
+    for dx, dy, dc in offsets:
+        if (dx, dy, dc) == (0, 0, 0):
+            continue
+        x, y, c = lax.rem(my_x + dx, nx), lax.rem(my_y + dy, ny), lax.rem(core + dc, 2)
+        at = {"region": x * nz + my_z, "rep": y * 2 + c}
+        all_peers.append((c * n_plane + x * ny + y, at))
+        if dc == 0:
+            plane_peers.append((x * ny + y, at))
     line_peers = [
-        {"region": my_x * nz + lax.rem(my_z + step, nz), "rep": rep} for step in range(1, nz)
+        {"region": my_x * nz + lax.rem(my_z + step, nz), "rep": rep}
+        for step in sorted(range(1, nz), key=lambda d: -apart(d, nz))
     ]
 
     halo_ref[...] = jnp.zeros((3, 2, 64, 128), BF16)
 
     barrier = pltpu.get_barrier_semaphore()
-    partners = [{"region": right, "rep": rep}, {"region": left, "rep": rep}, twin]
-    partners += [at for _, _, at in plane_peers] + line_peers
+    partners = [{"region": right, "rep": rep}, {"region": left, "rep": rep}]
+    partners += [at for _, at in all_peers] + line_peers
     for at in partners:
         pl.semaphore_signal(barrier, inc=1, device_id=at, device_id_type=MESH)
     loads = [
@@ -181,11 +194,6 @@
     w1b_ref[:, 4, 0:32, :] = top[:, 1, 1]
     w1b_ref[:, 4, 32:64, :] = low[:, 1, 1]
     w1b_ref[:, 4, 64:128, :] = jnp.zeros((3, 64, 128), BF16)
-    loads[3].wait()
-    spread2 = dot(w2_ref[...].reshape(27 * 64, 64), put).astype(BF16)
-    w2b_ref[:, 0:64, :] = spread2[:, :128].reshape(27, 64, 128)
-    w2b_ref[:, 64:128, :] = spread2[:, 128:].reshape(27, 64, 128)
-
     side_ref[2] = jnp.zeros((8, 64, 128), F32)
     far_ref[:, 2] = jnp.zeros((2, 64, 128), F32)
     lane = iota((8, 128), 1)
@@ -347,6 +355,10 @@
     layer(0, c1_ref, store_first, split_first(), even_quarter, windows_first, weight_first, dot, hidden_of)
     halo_start(1)
 
+    loads[3].wait()
+    spread2 = dot(w2_ref[...].reshape(27 * 64, 64), put).astype(BF16)
+    w2b_ref[:, 0:64, :] = spread2[:, :128].reshape(27, 64, 128)
+    w2b_ref[:, 64:128, :] = spread2[:, 128:].reshape(27, 64, 128)
     second = functools.partial(windows_second, c2_ref)
     loads[4].wait()
     layer(1, c2_ref, store_second, split_second(), first_half, second, weight_second, dot, outputs_of)
@@ -356,11 +368,10 @@
     wide_quarter = lax.rem(iota((64, 128), 1) // 32, 2) == 0
     per_core1, per_core2 = PAIRS_FIRST // 2, PAIRS_SECOND // 2
 
-    def put_gradient(full, send, per_core, pair, value):
+    def put_gradient(full, send, pair, value):
         value = value.reshape(4, 16, 128)
-        units = pl.ds((pair % per_core) * 4, 4)
-        full[pair // per_core, units] = value
-        send[pair // per_core, units] = value.astype(BF16)
+        full[4 * pair : 4 * pair + 4] = value
+        send[4 * pair : 4 * pair + 4] = value.astype(BF16)
 
     delta_t = face_ref[...].reshape(512, 128).T
     for pair in range(14):
@@ -373,12 +384,12 @@
         one, two = got[:, :128], got[:, 128:]
         straight = jnp.where(wide_half, one[0:64], two[64:128])
         crossed = jnp.where(wide_half, two[0:64], one[64:128])
-        put_gradient(full2_ref, send2_ref, per_core2, pair, straight + pltpu.roll(crossed, 64, 1))
+        put_gradient(full2_ref, send2_ref, pair, straight + pltpu.roll(crossed, 64, 1))
     for pair in range(14, PAIRS_SECOND):
-        put_gradient(full2_ref, send2_ref, per_core2, pair, jnp.zeros((64, 128), F32))
-
-    def reducer(which, per_core, full, send, pair, half, plane, line, fin):
-        unit = 4 * per_core // n_plane
+        put_gradient(full2_ref, send2_ref, pair, jnp.zeros((64, 128), F32))
+
+    def reducer(which, unit, send, parts, line, fin):
+        half = n_plane * unit
 
         def remote(stage, src, dst, device):
             return pltpu.make_async_remote_copy(
@@ -390,70 +401,74 @@
                 device_id_type=MESH,
             )
 
-        mine = fin.at[core, pl.ds(member * unit, unit)]
-        plane_part = plane.at[pl.ds(1, n_plane - 1)]
-        line_part = line.at[pl.ds(0, nz - 1)]
-        back_part = fin.at[core, pl.ds(0, (n_plane - 1) * unit)]
+        place = pl.ds((core * n_plane + member) * unit, unit)
+        parts_whole = parts.at[pl.ds(1, parts.shape[0] - 1)]
+        line_whole = line.at[pl.ds(0, nz - 1)]
+        fin_whole = fin.at[pl.ds(0, (2 * n_plane - 1) * unit)]
         whole = [
-            remote(0, send.at[1 - core], pair, twin),
-            remote(1, plane_part, plane_part, twin),
-            remote(2, line_part, line_part, twin),
-            remote(3, back_part, back_part, twin),
-            remote(4, fin.at[core], fin.at[core], twin),
+            remote(0, parts_whole, parts_whole, twin),
+            remote(1, line_whole, line_whole, twin),
+            remote(2, fin_whole, fin_whole, twin),
         ]
 
-        def start_pair():
-            whole[0].start()
-
-        def start_plane():
+        def start_parts(peers):
+            for i, (other, at) in enumerate(peers):
+                remote(0, send.at[pl.ds(other * unit, unit)], parts.at[i + 1], at).start()
+
+        def start_line(own):
             whole[0].wait_recv()
-            total = full[core] + pair[...].astype(F32)
-            full[core] = total
-            half[...] = total.astype(BF16)
-            for step, other, at in plane_peers:
-                remote(1, half.at[pl.ds(other * unit, unit)], plane.at[step], at).start()
-
-        def start_line():
-            whole[1].wait_recv()
-            total = full[core, pl.ds(member * unit, unit)]
-            for step in range(1, n_plane):
-                total = total + plane[step].astype(F32)
+            total = own
+            for i in range(1, parts.shape[0]):
+                total = total + parts[i].astype(F32)
             line[my_z] = total.astype(BF16)
             for at in line_peers:
-                remote(2, line.at[my_z], line.at[my_z], at).start()
+                remote(1, line.at[my_z], line.at[my_z], at).start()
 
         def start_back():
-            whole[2].wait_recv()
+            whole[1].wait_recv()
             total = line[0].astype(F32)
             for z in range(1, nz):
                 total = total + line[z].astype(F32)
-            fin[core, pl.ds(member * unit, unit)] = (total * scale).astype(BF16)
-            for _, _, at in plane_peers:
-                remote(3, mine, mine, at).start()
-
-        def start_twin():
-            whole[3].wait_recv()
-            whole[4].start()
+            fin[place] = (total * scale).astype(BF16)
+            for _, at in all_peers:
+                remote(2, fin.at[place], fin.at[place], at).start()
 
         def finish():
-            whole[4].wait_recv()
+            whole[2].wait_recv()
 
         def sent():
             for copy in whole:
                 copy.wait_send()
 
-        return start_pair, start_plane, start_line, start_back, start_twin, finish, sent
-
-    sum1 = reducer(
-        0, per_core1, full1_ref, send1_ref, pair1_ref, half1_ref, plane1_ref, line1_ref, fin1_ref
+        return start_parts, start_line, start_back, finish, sent
+
+    unit1, unit2 = 4 * per_core1 // n_plane, 4 * per_core2 // n_plane
+    place1 = pl.ds((core * n_plane + member) * unit1, unit1)
+    sum1 = reducer(0, unit1, send1_ref, parts1_ref, line1_ref, fin1_ref)
+    sum2 = reducer(1, unit2, half2_ref, parts2_ref, line2_ref, fin2_ref)
+
+    def half_units(which_core):
+        return pl.ds(which_core * 4 * per_core2, 4 * per_core2)
+
+    pair_copy = pltpu.make_async_remote_copy(
+        src_ref=send2_ref.at[half_units(1 - core)],
+        dst_ref=pair2_ref,
+        send_sem=pair_sem.at[0],
+        recv_sem=pair_sem.at[1],
+        device_id=twin,
+        device_id_type=MESH,
     )
-    sum2 = reducer(
-        1, per_core2, full2_ref, send2_ref, pair2_ref, half2_ref, plane2_ref, line2_ref, fin2_ref
-    )
-    sum2[0]()
+    pair_copy.start()
+
+    def start_second():
+        pair_copy.wait_recv()
+        total = full2_ref[half_units(core)] + pair2_ref[...].astype(F32)
+        mine2_ref[...] = total
+        half2_ref[...] = total.astype(BF16)
+        sum2[0](plane_peers)
 
     third = functools.partial(windows_second, c3_ref)
-    layer(2, c3_ref, store_second, split_second(), first_half, third, weight_back, dot_nt, back_of, sum2[1])
+    layer(2, c3_ref, store_second, split_second(), first_half, third, weight_back, dot_nt, back_of, start_second)
     delta_t = face_ref[...].reshape(512, 128).T
     for pair in range(PAIRS_FIRST):
         both = []
@@ -465,25 +480,22 @@
         straight = jnp.where(wide_quarter, one[0:64], two[64:128])
         crossed = jnp.where(wide_quarter, two[0:64], one[64:128])
         swapped = jnp.where(wide_quarter, pltpu.roll(crossed, 96, 1), pltpu.roll(crossed, 32, 1))
-        put_gradient(full1_ref, send1_ref, per_core1, pair, straight + swapped)
-    sum1[0]()
+        put_gradient(full1_ref, send1_ref, pair, straight + swapped)
+    sum1[0](all_peers)
+    sum2[1](mine2_ref[pl.ds(member * unit2, unit2)])
+    sum1[1](full1_ref[place1])
     sum2[2]()
-    sum1[1]()
+    sum1[2]()
     sum2[3]()
-    sum1[2]()
-    sum2[4]()
-    sum1[3]()
-    sum2[5]()
     for pair in range(14):
-        units = pl.ds((pair % per_core2) * 4, 4)
-        value = fin2_ref[pair // per_core2, units].reshape(64, 128).astype(F32).T
+        value = fin2_ref[4 * pair : 4 * pair + 4].reshape(64, 128).astype(F32).T
         g2_ref[2 * pair] = value[0:64]
         if pair < 13:
             g2_ref[2 * pair + 1] = value[64:128]
+    sum1[3]()
+    pair_copy.wait_send()
+    sum2[4]()
     sum1[4]()
-    sum2[6]()
-    sum1[5]()
-    sum1[6]()
 
 
 def unpack_kernel(block_ref, fin_ref, g2_ref, out_hbm, g1_hbm, g2_hbm, g1_ref, sem):
@@ -493,8 +505,7 @@
     second_copy.start()
     block_copy.start()
     for pair in range(PAIRS_FIRST):
-        at = (pair % (PAIRS_FIRST // 2)) * 4
-        value = fin_ref[pair // (PAIRS_FIRST // 2), at : at + 4].reshape(64, 128).astype(F32).T
+        value = fin_ref[4 * pair : 4 * pair + 4].reshape(64, 128).astype(F32).T
         for j in range(2):
             block = 2 * pair + j
             if block > 14:
@@ -534,7 +545,7 @@
             functools.partial(main_kernel, sizes, scale),
             out_shape=(
                 jax.ShapeDtypeStruct((512, 128), BF16),
-                jax.ShapeDtypeStruct((2, core1, 16, 128), BF16),
+                jax.ShapeDtypeStruct((2 * core1, 16, 128), BF16),
                 jax.ShapeDtypeStruct((27, 64, 64), F32),
             ),
             in_specs=[hbm, hbm, hbm, hbm, smem, hbm],
@@ -558,24 +569,24 @@
                 pltpu.VMEM((27, 128, 128), BF16),
                 pltpu.VMEM((512, 128), F32),
                 pltpu.VMEM((8, 64, 128), F32),
-                pltpu.VMEM((2, core1, 16, 128), F32),
-                pltpu.VMEM((2, core2, 16, 128), F32),
-                pltpu.VMEM((2, core1, 16, 128), BF16),
-                pltpu.VMEM((2, core2, 16, 128), BF16),
-                pltpu.VMEM((core1, 16, 128), BF16),
+                pltpu.VMEM((2 * core1, 16, 128), F32),
+                pltpu.VMEM((2 * core2, 16, 128), F32),
+                pltpu.VMEM((2 * core1, 16, 128), BF16),
+                pltpu.VMEM((2 * core2, 16, 128), BF16),
                 pltpu.VMEM((core2, 16, 128), BF16),
-                pltpu.VMEM((core1, 16, 128), BF16),
                 pltpu.VMEM((core2, 16, 128), BF16),
-                pltpu.VMEM((n_plane, unit1, 16, 128), BF16),
+                pltpu.VMEM((core2, 16, 128), F32),
+                pltpu.VMEM((2 * n_plane, unit1, 16, 128), BF16),
                 pltpu.VMEM((n_plane, unit2, 16, 128), BF16),
                 pltpu.VMEM((nz, unit1, 16, 128), BF16),
                 pltpu.VMEM((nz, unit2, 16, 128), BF16),
-                pltpu.VMEM((2, core2, 16, 128), BF16),
+                pltpu.VMEM((2 * core2, 16, 128), BF16),
                 dma((5,)),
                 dma((3, 2)),
                 dma((3, 2)),
-                dma((2, 5)),
-                dma((2, 5)),
+                dma((2,)),
+                dma((2, 3)),
+                dma((2, 3)),
             ],
             compiler_params=pltpu.CompilerParams(
                 collective_id=0, has_side_effects=True, vmem_limit_bytes=40 * 2**20

time: 45 us -> 40.7 us (0.904)
  Pallas kernels: 44.3 us -> 39.9 us
    pallas_call x1, Pallas kernels: 43.1 us -> 38.8 us  [body(): pl.pallas_call(functools.partial(main_kernel, sizes, scale), out_shape=(j...]
where the time goes in v6:
time: 40.7 us; the launch traced here: 40.6 us
  Pallas kernels  39.9 us (98%)
  between operations  0.64 us (2%)
    pallas_call x1, Pallas kernels, body(): pl.pallas_call(functools.partial(main_kernel, sizes, scale), out_shape=(j...  38.8 us
    pallas_call x1, Pallas kernels, body(): pl.pallas_call(unpack_kernel, out_shape=(jax.ShapeDtypeStruct((512, 128),...  1.12 us

profile of v6, /device:TPU:1, one launch (start us, length us, event | category | flops | bytes accessed | tf_op | source)
XLA Modules:
  0.0 40.6 jit_solution(16643039962172812389)
XLA Ops:
  0.6 38.8 %shard_map.85 = (bf16[512,128]{1,0:T(8,128)(2,1)S(1)}, bf16[32,16,128]{2,1,0:T(8,128)(2,1)S(1)}, f32[27,64,64]{2,1,0:T(8,128)S(1)}) custom-call(bf16[64,512]{1,0:T(8,128)(2,1)} %bitcast.8, bf16[27,32,64]{2,1,0:T(8,128)(2,1)} %w1_hbm.1, bf16[27,64,64]{2,1,0:T(8,128)(2,1)} %w2_hbm.1, bf16[512,128]{1,0:T(8,128)(2,1)} %bitcast.7, s32[2,27]{1,0:T(2,128)} %bitcast.10, ...), custom_call_target="tpu_custom_call" | custom-call | tf_op jit(solution)/shard_map/pallas_call | solution.py:544
  39.4 1.1 %shard_map.86 = (bf16[512,128]{1,0:T(8,128)(2,1)}, f32[27,32,64]{2,1,0:T(8,128)}, f32[27,64,64]{2,1,0:T(8,128)}) custom-call(bf16[512,128]{1,0:T(8,128)(2,1)S(1)} %get-tuple-element.9.block_ref, bf16[32,16,128]{2,1,0:T(8,128)(2,1)S(1)} %get-tuple-element.10.fin_ref, f32[27,64,64]{2,1,0:T(8,128)S(1)} %get-tuple-element.11.g2_ref), custom_call_target="tpu_custom_call" | custom-call | tf_op jit(solution)/shard_map/pallas_call | solution.py:607

commit v7 on v6

--- a/solution.py
+++ b/solution.py
@@ -70,9 +70,6 @@
     full2_ref,
     send1_ref,
     send2_ref,
-    pair2_ref,
-    half2_ref,
-    mine2_ref,
     parts1_ref,
     parts2_ref,
     line1_ref,
@@ -81,7 +78,6 @@
     load_sem,
     halo_send,
     halo_recv,
-    pair_sem,
     sum_send,
     sum_recv,
 ):
@@ -100,15 +96,13 @@
         ((dx, dy, dc) for dx in range(nx) for dy in range(ny) for dc in range(2)),
         key=lambda d: (-apart(d[0], nx) - apart(d[1], ny), d),
     )
-    plane_peers, all_peers = [], []
+    all_peers = []
     for dx, dy, dc in offsets:
         if (dx, dy, dc) == (0, 0, 0):
             continue
         x, y, c = lax.rem(my_x + dx, nx), lax.rem(my_y + dy, ny), lax.rem(core + dc, 2)
         at = {"region": x * nz + my_z, "rep": y * 2 + c}
         all_peers.append((c * n_plane + x * ny + y, at))
-        if dc == 0:
-            plane_peers.append((x * ny + y, at))
     line_peers = [
         {"region": my_x * nz + lax.rem(my_z + step, nz), "rep": rep}
         for step in sorted(range(1, nz), key=lambda d: -apart(d, nz))
@@ -263,10 +257,10 @@
             store(c_ref, x + 1, *shifted(field_ref[x], load, tile_lane))
 
     def build_faces(which, c_ref, store, splitter, tile_lane):
+        whole = dot(halo_ref[which].reshape(128, 128), splitter)
         for side in range(2):
-            whole = dot(halo_ref[which, side], splitter)
-            far_ref[side, 0] = whole[:, :128]
-            far_ref[side, 1] = whole[:, 128:]
+            far_ref[side, 0] = whole[64 * side : 64 * side + 64, :128]
+            far_ref[side, 1] = whole[64 * side : 64 * side + 64, 128:]
             named = [
                 [
                     jnp.minimum(jnp.maximum(nbr_ref[t, 18 * side + k] - 4 * side, 0), 2)
@@ -298,14 +292,19 @@
             for c in range(3)
         ]
 
-    def conv_inner(windows, weight, product=dot):
-        acc_ref[...] = product(jnp.concatenate(windows(1, 8), axis=1), weight(1))
-        acc_ref[64:512] += product(jnp.concatenate(windows(1, 7), axis=1), weight(0))
-        acc_ref[0:448] += product(jnp.concatenate(windows(2, 7), axis=1), weight(2))
-
-    def conv_faces(windows, weight, product=dot):
-        acc_ref[0:64] += product(jnp.concatenate(windows(0, 1), axis=1), weight(0))
-        acc_ref[448:512] += product(jnp.concatenate(windows(9, 1), axis=1), weight(2))
+    def conv_inner(windows, weight, product=dot, columns=1):
+        weights = jnp.concatenate([weight(0), weight(2), weight(1)], axis=columns)
+        got = product(jnp.concatenate(windows(1, 8), axis=1), weights)
+        acc_ref[...] = got[:, 256:384]
+        acc_ref[64:512] += got[0:448, 0:128]
+        acc_ref[0:448] += got[64:512, 128:256]
+
+    def conv_faces(windows, weight, product=dot, columns=1):
+        weights = jnp.concatenate([weight(0), weight(2)], axis=columns)
+        rows = [jnp.concatenate(both, axis=0) for both in zip(windows(0, 1), windows(9, 1))]
+        got = product(jnp.concatenate(rows, axis=1), weights)
+        acc_ref[0:64] += got[0:64, 0:128]
+        acc_ref[448:512] += got[64:128, 128:256]
 
     def weight_first(a):
         return w1b_ref[a].reshape(5 * 128, 128)
@@ -316,15 +315,15 @@
     def weight_back(a):
         return jnp.concatenate([w2b_ref[26 - k] for k in range(9 * a, 9 * a + 9)], axis=1)
 
-    def layer(which, c_ref, store, splitter, tile_lane, windows, weight, product, activate, between=None):
+    def layer(which, c_ref, store, splitter, tile_lane, windows, weight, product, columns, activate, between=None):
         build_inner(c_ref, store, splitter, tile_lane)
-        conv_inner(windows, weight, product)
+        conv_inner(windows, weight, product, columns)
         if between is not None:
             between()
         pl.loop(1, 7, unroll=3)(activate)
         halo_wait(which)
         build_faces(which, c_ref, store, splitter, tile_lane)
-        conv_faces(windows, weight, product)
+        conv_faces(windows, weight, product, columns)
         pl.loop(0, 2, unroll=2)(lambda i: activate(7 * i))
 
     def hidden_of(x):
@@ -352,7 +351,7 @@
         rows = pl.ds(pl.multiple_of(x * 64, 64), 64)
         face_ref[x] = (acc_ref[rows, :] * slope_ref[x]).astype(BF16)
 
-    layer(0, c1_ref, store_first, split_first(), even_quarter, windows_first, weight_first, dot, hidden_of)
+    layer(0, c1_ref, store_first, split_first(), even_quarter, windows_first, weight_first, dot, 1, hidden_of)
     halo_start(1)
 
     loads[3].wait()
@@ -361,7 +360,7 @@
     w2b_ref[:, 64:128, :] = spread2[:, 128:].reshape(27, 64, 128)
     second = functools.partial(windows_second, c2_ref)
     loads[4].wait()
-    layer(1, c2_ref, store_second, split_second(), first_half, second, weight_second, dot, outputs_of)
+    layer(1, c2_ref, store_second, split_second(), first_half, second, weight_second, dot, 1, outputs_of)
     halo_start(2)
 
     wide_half = iota((64, 128), 1) < 64
@@ -388,8 +387,7 @@
     for pair in range(14, PAIRS_SECOND):
         put_gradient(full2_ref, send2_ref, pair, jnp.zeros((64, 128), F32))
 
-    def reducer(which, unit, send, parts, line, fin):
-        half = n_plane * unit
+    def reducer(which, unit, full, send, parts, line, fin):
 
         def remote(stage, src, dst, device):
             return pltpu.make_async_remote_copy(
@@ -411,13 +409,13 @@
             remote(2, fin_whole, fin_whole, twin),
         ]
 
-        def start_parts(peers):
-            for i, (other, at) in enumerate(peers):
+        def start_parts():
+            for i, (other, at) in enumerate(all_peers):
                 remote(0, send.at[pl.ds(other * unit, unit)], parts.at[i + 1], at).start()
 
-        def start_line(own):
+        def start_line():
             whole[0].wait_recv()
-            total = own
+            total = full[place]
             for i in range(1, parts.shape[0]):
                 total = total + parts[i].astype(F32)
             line[my_z] = total.astype(BF16)
@@ -443,32 +441,12 @@
         return start_parts, start_line, start_back, finish, sent
 
     unit1, unit2 = 4 * per_core1 // n_plane, 4 * per_core2 // n_plane
-    place1 = pl.ds((core * n_plane + member) * unit1, unit1)
-    sum1 = reducer(0, unit1, send1_ref, parts1_ref, line1_ref, fin1_ref)
-    sum2 = reducer(1, unit2, half2_ref, parts2_ref, line2_ref, fin2_ref)
-
-    def half_units(which_core):
-        return pl.ds(which_core * 4 * per_core2, 4 * per_core2)
-
-    pair_copy = pltpu.make_async_remote_copy(
-        src_ref=send2_ref.at[half_units(1 - core)],
-        dst_ref=pair2_ref,
-        send_sem=pair_sem.at[0],
-        recv_sem=pair_sem.at[1],
-        device_id=twin,
-        device_id_type=MESH,
-    )
-    pair_copy.start()
-
-    def start_second():
-        pair_copy.wait_recv()
-        total = full2_ref[half_units(core)] + pair2_ref[...].astype(F32)
-        mine2_ref[...] = total
-        half2_ref[...] = total.astype(BF16)
-        sum2[0](plane_peers)
+    sum1 = reducer(0, unit1, full1_ref, send1_ref, parts1_ref, line1_ref, fin1_ref)
+    sum2 = reducer(1, unit2, full2_ref, send2_ref, parts2_ref, line2_ref, fin2_ref)
+    sum2[0]()
 
     third = functools.partial(windows_second, c3_ref)
-    layer(2, c3_ref, store_second, split_second(), first_half, third, weight_back, dot_nt, back_of, start_second)
+    layer(2, c3_ref, store_second, split_second(), first_half, third, weight_back, dot_nt, 0, back_of)
     delta_t = face_ref[...].reshape(512, 128).T
     for pair in range(PAIRS_FIRST):
         both = []
@@ -481,9 +459,9 @@
         crossed = jnp.where(wide_quarter, two[0:64], one[64:128])
         swapped = jnp.where(wide_quarter, pltpu.roll(crossed, 96, 1), pltpu.roll(crossed, 32, 1))
         put_gradient(full1_ref, send1_ref, pair, straight + swapped)
-    sum1[0](all_peers)
-    sum2[1](mine2_ref[pl.ds(member * unit2, unit2)])
-    sum1[1](full1_ref[place1])
+    sum1[0]()
+    sum2[1]()
+    sum1[1]()
     sum2[2]()
     sum1[2]()
     sum2[3]()
@@ -493,16 +471,19 @@
         if pair < 13:
             g2_ref[2 * pair + 1] = value[64:128]
     sum1[3]()
-    pair_copy.wait_send()
     sum2[4]()
     sum1[4]()
 
 
 def unpack_kernel(block_ref, fin_ref, g2_ref, out_hbm, g1_hbm, g2_hbm, g1_ref, sem):
     block_copy = pltpu.make_async_copy(block_ref, out_hbm, sem.at[0])
-    second_copy = pltpu.make_async_copy(g2_ref, g2_hbm, sem.at[1])
+    second_copies = [
+        pltpu.make_async_copy(g2_ref.at[pl.ds(k, 9)], g2_hbm.at[pl.ds(k, 9)], sem.at[3 + k // 9])
+        for k in (0, 9, 18)
+    ]
     first_copy = pltpu.make_async_copy(g1_ref, g1_hbm, sem.at[2])
-    second_copy.start()
+    for copy in second_copies:
+        copy.start()
     block_copy.start()
     for pair in range(PAIRS_FIRST):
         value = fin_ref[4 * pair : 4 * pair + 4].reshape(64, 128).astype(F32).T
@@ -520,7 +501,8 @@
             for i, k in enumerate(offsets):
                 g1_ref[k] = value[64 * i + 32 * j : 64 * i + 32 * j + 32]
     first_copy.start()
-    second_copy.wait()
+    for copy in second_copies:
+        copy.wait()
     block_copy.wait()
     first_copy.wait()
 
@@ -573,18 +555,14 @@
                 pltpu.VMEM((2 * core2, 16, 128), F32),
                 pltpu.VMEM((2 * core1, 16, 128), BF16),
                 pltpu.VMEM((2 * core2, 16, 128), BF16),
-                pltpu.VMEM((core2, 16, 128), BF16),
-                pltpu.VMEM((core2, 16, 128), BF16),
-                pltpu.VMEM((core2, 16, 128), F32),
                 pltpu.VMEM((2 * n_plane, unit1, 16, 128), BF16),
-                pltpu.VMEM((n_plane, unit2, 16, 128), BF16),
+                pltpu.VMEM((2 * n_plane, unit2, 16, 128), BF16),
                 pltpu.VMEM((nz, unit1, 16, 128), BF16),
                 pltpu.VMEM((nz, unit2, 16, 128), BF16),
                 pltpu.VMEM((2 * core2, 16, 128), BF16),
                 dma((5,)),
                 dma((3, 2)),
                 dma((3, 2)),
-                dma((2,)),
                 dma((2, 3)),
                 dma((2, 3)),
             ],
@@ -615,7 +593,7 @@
             out_specs=(anywhere, anywhere, anywhere),
             scratch_shapes=[
                 pltpu.VMEM((27, 32, 64), F32),
-                dma((3,)),
+                dma((6,)),
             ],
             compiler_params=pltpu.CompilerParams(vmem_limit_bytes=40 * 2**20),
         )(block, fin1, g2)

time: 40.7 us -> 39.7 us (0.975)
  Pallas kernels: 39.9 us -> 39 us
    pallas_call x1, Pallas kernels: 38.8 us -> 37.8 us  [body(): pl.pallas_call(functools.partial(main_kernel, sizes, scale), out_shape=(j...]
where the time goes in v7:
time: 39.7 us; the launch traced here: 39.6 us
  Pallas kernels  39 us (98%)
  between operations  0.64 us (2%)
    pallas_call x1, Pallas kernels, body(): pl.pallas_call(functools.partial(main_kernel, sizes, scale), out_shape=(j...  37.8 us
    pallas_call x1, Pallas kernels, body(): pl.pallas_call(unpack_kernel, out_shape=(jax.ShapeDtypeStruct((512, 128),...  1.15 us

profile of v7, /device:TPU:1, one launch (start us, length us, event | category | flops | bytes accessed | tf_op | source)
XLA Modules:
  0.0 39.6 jit_solution(8347584747968336999)
XLA Ops:
  0.6 37.8 %shard_map.85 = (bf16[512,128]{1,0:T(8,128)(2,1)S(1)}, bf16[32,16,128]{2,1,0:T(8,128)(2,1)S(1)}, f32[27,64,64]{2,1,0:T(8,128)S(1)}) custom-call(bf16[64,512]{1,0:T(8,128)(2,1)} %bitcast.8, bf16[27,32,64]{2,1,0:T(8,128)(2,1)} %w1_hbm.1, bf16[27,64,64]{2,1,0:T(8,128)(2,1)} %w2_hbm.1, bf16[512,128]{1,0:T(8,128)(2,1)} %bitcast.7, s32[2,27]{1,0:T(2,128)} %bitcast.10, ...), custom_call_target="tpu_custom_call" | custom-call | tf_op jit(solution)/shard_map/pallas_call | solution.py:526
  38.5 1.2 %shard_map.86 = (bf16[512,128]{1,0:T(8,128)(2,1)}, f32[27,32,64]{2,1,0:T(8,128)}, f32[27,64,64]{2,1,0:T(8,128)}) custom-call(bf16[512,128]{1,0:T(8,128)(2,1)S(1)} %get-tuple-element.9.block_ref, bf16[32,16,128]{2,1,0:T(8,128)(2,1)S(1)} %get-tuple-element.10.fin_ref, f32[27,64,64]{2,1,0:T(8,128)S(1)} %get-tuple-element.11.g2_ref), custom_call_target="tpu_custom_call" | custom-call | tf_op jit(solution)/shard_map/pallas_call | solution.py:585

commit v8 on v7

--- a/solution.py
+++ b/solution.py
@@ -96,13 +96,15 @@
         ((dx, dy, dc) for dx in range(nx) for dy in range(ny) for dc in range(2)),
         key=lambda d: (-apart(d[0], nx) - apart(d[1], ny), d),
     )
-    all_peers = []
+    plane_peers, all_peers = [], []
     for dx, dy, dc in offsets:
         if (dx, dy, dc) == (0, 0, 0):
             continue
         x, y, c = lax.rem(my_x + dx, nx), lax.rem(my_y + dy, ny), lax.rem(core + dc, 2)
         at = {"region": x * nz + my_z, "rep": y * 2 + c}
         all_peers.append((c * n_plane + x * ny + y, at))
+        if dc == 0:
+            plane_peers.append(at)
     line_peers = [
         {"region": my_x * nz + lax.rem(my_z + step, nz), "rep": rep}
         for step in sorted(range(1, nz), key=lambda d: -apart(d, nz))
@@ -387,7 +389,7 @@
     for pair in range(14, PAIRS_SECOND):
         put_gradient(full2_ref, send2_ref, pair, jnp.zeros((64, 128), F32))
 
-    def reducer(which, unit, full, send, parts, line, fin):
+    def reducer(which, unit, full, send, parts, line, fin, back_peers):
 
         def remote(stage, src, dst, device):
             return pltpu.make_async_remote_copy(
@@ -402,12 +404,16 @@
         place = pl.ds((core * n_plane + member) * unit, unit)
         parts_whole = parts.at[pl.ds(1, parts.shape[0] - 1)]
         line_whole = line.at[pl.ds(0, nz - 1)]
-        fin_whole = fin.at[pl.ds(0, (2 * n_plane - 1) * unit)]
+        fin_whole = fin.at[pl.ds(0, len(back_peers) * unit)]
+        fin_half = fin.at[pl.ds(core * n_plane * unit, n_plane * unit)]
         whole = [
             remote(0, parts_whole, parts_whole, twin),
             remote(1, line_whole, line_whole, twin),
             remote(2, fin_whole, fin_whole, twin),
         ]
+
+        def twin_copy():
+            return remote(3, fin_half, fin_half, twin)
 
         def start_parts():
             for i, (other, at) in enumerate(all_peers):
@@ -428,7 +434,7 @@
             for z in range(1, nz):
                 total = total + line[z].astype(F32)
             fin[place] = (total * scale).astype(BF16)
-            for _, at in all_peers:
+            for at in back_peers:
                 remote(2, fin.at[place], fin.at[place], at).start()
 
         def finish():
@@ -438,11 +444,11 @@
             for copy in whole:
                 copy.wait_send()
 
-        return start_parts, start_line, start_back, finish, sent
+        return start_parts, start_line, start_back, finish, sent, twin_copy
 
     unit1, unit2 = 4 * per_core1 // n_plane, 4 * per_core2 // n_plane
-    sum1 = reducer(0, unit1, full1_ref, send1_ref, parts1_ref, line1_ref, fin1_ref)
-    sum2 = reducer(1, unit2, full2_ref, send2_ref, parts2_ref, line2_ref, fin2_ref)
+    sum1 = reducer(0, unit1, full1_ref, send1_ref, parts1_ref, line1_ref, fin1_ref, [at for _, at in all_peers])
+    sum2 = reducer(1, unit2, full2_ref, send2_ref, parts2_ref, line2_ref, fin2_ref, plane_peers)
     sum2[0]()
 
     third = functools.partial(windows_second, c3_ref)
@@ -465,13 +471,20 @@
     sum2[2]()
     sum1[2]()
     sum2[3]()
-    for pair in range(14):
-        value = fin2_ref[4 * pair : 4 * pair + 4].reshape(64, 128).astype(F32).T
-        g2_ref[2 * pair] = value[0:64]
-        if pair < 13:
-            g2_ref[2 * pair + 1] = value[64:128]
+    sum2[5]().start()
+
+    def unpack_half(which_core):
+        for i in range(per_core2):
+            pair = which_core * per_core2 + i
+            value = fin2_ref[pl.ds(4 * pair, 4)].reshape(64, 128).astype(F32).T
+            g2_ref[pl.ds(2 * pair, 2)] = value.reshape(2, 64, 64)
+
+    unpack_half(core)
+    sum2[5]().wait_recv()
+    unpack_half(1 - core)
     sum1[3]()
     sum2[4]()
+    sum2[5]().wait_send()
     sum1[4]()
 
 
@@ -528,7 +541,7 @@
             out_shape=(
                 jax.ShapeDtypeStruct((512, 128), BF16),
                 jax.ShapeDtypeStruct((2 * core1, 16, 128), BF16),
-                jax.ShapeDtypeStruct((27, 64, 64), F32),
+                jax.ShapeDtypeStruct((2 * PAIRS_SECOND, 64, 64), F32),
             ),
             in_specs=[hbm, hbm, hbm, hbm, smem, hbm],
             out_specs=(vmem, vmem, vmem),
@@ -563,8 +576,8 @@
                 dma((5,)),
                 dma((3, 2)),
                 dma((3, 2)),
-                dma((2, 3)),
-                dma((2, 3)),
+                dma((2, 4)),
+                dma((2, 4)),
             ],
             compiler_params=pltpu.CompilerParams(
                 collective_id=0, has_side_effects=True, vmem_limit_bytes=40 * 2**20

time: 39.7 us -> 39.8 us (level)
  no operation moved by 1% of the time
where the time goes in v8:
time: 39.8 us; the launch traced here: 39.6 us
  Pallas kernels  39 us (98%)
  between operations  0.64 us (2%)
    pallas_call x1, Pallas kernels, body(): pl.pallas_call(functools.partial(main_kernel, sizes, scale), out_shape=(j...  37.9 us
    pallas_call x1, Pallas kernels, body(): pl.pallas_call(unpack_kernel, out_shape=(jax.ShapeDtypeStruct((512, 128),...  1.15 us

profile of v8, /device:TPU:1, one launch (start us, length us, event | category | flops | bytes accessed | tf_op | source)
XLA Modules:
  0.0 39.6 jit_solution(14999712856319592086)
XLA Ops:
  0.6 37.9 %shard_map.85 = (bf16[512,128]{1,0:T(8,128)(2,1)S(1)}, bf16[32,16,128]{2,1,0:T(8,128)(2,1)S(1)}, f32[32,64,64]{2,1,0:T(8,128)S(1)}) custom-call(bf16[64,512]{1,0:T(8,128)(2,1)} %bitcast.8, bf16[27,32,64]{2,1,0:T(8,128)(2,1)} %w1_hbm.1, bf16[27,64,64]{2,1,0:T(8,128)(2,1)} %w2_hbm.1, bf16[512,128]{1,0:T(8,128)(2,1)} %bitcast.7, s32[2,27]{1,0:T(2,128)} %bitcast.10, ...), custom_call_target="tpu_custom_call" | custom-call | tf_op jit(solution)/shard_map/pallas_call | solution.py:539
  38.5 1.2 %shard_map.86 = (bf16[512,128]{1,0:T(8,128)(2,1)}, f32[27,32,64]{2,1,0:T(8,128)}, f32[27,64,64]{2,1,0:T(8,128)}) custom-call(bf16[512,128]{1,0:T(8,128)(2,1)S(1)} %get-tuple-element.9.block_ref, bf16[32,16,128]{2,1,0:T(8,128)(2,1)S(1)} %get-tuple-element.10.fin_ref, f32[32,64,64]{2,1,0:T(8,128)S(1)} %get-tuple-element.11.g2_ref), custom_call_target="tpu_custom_call" | custom-call | tf_op jit(solution)/shard_map/pallas_call | solution.py:598

commit v9 on v7

--- a/solution.py
+++ b/solution.py
@@ -102,7 +102,7 @@
             continue
         x, y, c = lax.rem(my_x + dx, nx), lax.rem(my_y + dy, ny), lax.rem(core + dc, 2)
         at = {"region": x * nz + my_z, "rep": y * 2 + c}
-        all_peers.append((c * n_plane + x * ny + y, at))
+        all_peers.append((len(all_peers) + 1, c * n_plane + x * ny + y, at))
     line_peers = [
         {"region": my_x * nz + lax.rem(my_z + step, nz), "rep": rep}
         for step in sorted(range(1, nz), key=lambda d: -apart(d, nz))
@@ -112,8 +112,8 @@
 
     barrier = pltpu.get_barrier_semaphore()
     partners = [{"region": right, "rep": rep}, {"region": left, "rep": rep}]
-    partners += [at for _, at in all_peers] + line_peers
-    for at in partners:
+    partners += [at for _, _, at in all_peers] + line_peers
+    for at in partners[:2]:
         pl.semaphore_signal(barrier, inc=1, device_id=at, device_id_type=MESH)
     loads = [
         pltpu.make_async_copy(src, dst, load_sem.at[i])
@@ -129,6 +129,8 @@
     ]
     for load in loads:
         load.start()
+    for at in partners[2:]:
+        pl.semaphore_signal(barrier, inc=1, device_id=at, device_id_type=MESH)
     loads[0].wait()
     loads[1].wait()
 
@@ -409,9 +411,9 @@
             remote(2, fin_whole, fin_whole, twin),
         ]
 
-        def start_parts():
-            for i, (other, at) in enumerate(all_peers):
-                remote(0, send.at[pl.ds(other * unit, unit)], parts.at[i + 1], at).start()
+        def start_parts(peers):
+            for slot, other, at in peers:
+                remote(0, send.at[pl.ds(other * unit, unit)], parts.at[slot], at).start()
 
         def start_line():
             whole[0].wait_recv()
@@ -428,7 +430,7 @@
             for z in range(1, nz):
                 total = total + line[z].astype(F32)
             fin[place] = (total * scale).astype(BF16)
-            for _, at in all_peers:
+            for _, _, at in all_peers:
                 remote(2, fin.at[place], fin.at[place], at).start()
 
         def finish():
@@ -443,30 +445,41 @@
     unit1, unit2 = 4 * per_core1 // n_plane, 4 * per_core2 // n_plane
     sum1 = reducer(0, unit1, full1_ref, send1_ref, parts1_ref, line1_ref, fin1_ref)
     sum2 = reducer(1, unit2, full2_ref, send2_ref, parts2_ref, line2_ref, fin2_ref)
-    sum2[0]()
+    sum2[0](all_peers)
 
     third = functools.partial(windows_second, c3_ref)
     layer(2, c3_ref, store_second, split_second(), first_half, third, weight_back, dot_nt, 0, back_of)
     delta_t = face_ref[...].reshape(512, 128).T
-    for pair in range(PAIRS_FIRST):
+    def first_gradient(pair):
         both = []
-        for block in (2 * pair, min(2 * pair + 1, 14)):
-            a, r = block // 5, ROWS_FIRST[block % 5]
-            both.append(c1_ref[a : a + 8, r : r + 64, :].reshape(512, 128))
+        for j in range(2):
+            block = jnp.minimum(2 * pair + j, 14)
+            a, kind = block // 5, lax.rem(block, 5)
+            row = jnp.where(kind < 3, 80 * kind * (2 - kind) + 8 * kind * (kind - 1), 64 * kind - 48)
+            rows = pl.ds(pl.multiple_of(row, 16), 64)
+            both.append(c1_ref[pl.ds(a, 8), rows, :].reshape(512, 128))
         got = dot(delta_t, jnp.concatenate(both, axis=1))
         one, two = got[:, :128], got[:, 128:]
         straight = jnp.where(wide_quarter, one[0:64], two[64:128])
         crossed = jnp.where(wide_quarter, two[0:64], one[64:128])
         swapped = jnp.where(wide_quarter, pltpu.roll(crossed, 96, 1), pltpu.roll(crossed, 32, 1))
-        put_gradient(full1_ref, send1_ref, pair, straight + swapped)
-    sum1[0]()
+        value = (straight + swapped).reshape(4, 16, 128)
+        full1_ref[pl.ds(4 * pair, 4)] = value
+        send1_ref[pl.ds(4 * pair, 4)] = value.astype(BF16)
+
+    for i in range(per_core1):
+        first_gradient((1 - core) * per_core1 + i)
+    sum1[0]([peer for peer, offset in zip(all_peers, offsets) if offset[2] == 1])
+    for i in range(per_core1):
+        first_gradient(core * per_core1 + i)
+    sum1[0]([peer for peer, offset in zip(all_peers, offsets) if offset[2] == 0])
     sum2[1]()
     sum1[1]()
     sum2[2]()
     sum1[2]()
     sum2[3]()
     for pair in range(14):
-        value = fin2_ref[4 * pair : 4 * pair + 4].reshape(64, 128).astype(F32).T
+        value = fin2_ref[4 * pair : 4 * pair + 4].reshape(64, 128).T.astype(F32)
         g2_ref[2 * pair] = value[0:64]
         if pair < 13:
             g2_ref[2 * pair + 1] = value[64:128]
@@ -486,7 +499,7 @@
         copy.start()
     block_copy.start()
     for pair in range(PAIRS_FIRST):
-        value = fin_ref[4 * pair : 4 * pair + 4].reshape(64, 128).astype(F32).T
+        value = fin_ref[4 * pair : 4 * pair + 4].reshape(64, 128).T.astype(F32)
         for j in range(2):
             block = 2 * pair + j
             if block > 14:

time: 39.7 us -> 40 us (level)
  no operation moved by 1% of the time
where the time goes in v9:
time: 40 us; the launch traced here: 39.9 us
  Pallas kernels  39.3 us (98%)
  between operations  0.64 us (2%)
    pallas_call x1, Pallas kernels, body(): pl.pallas_call(functools.partial(main_kernel, sizes, scale), out_shape=(j...  38.1 us
    pallas_call x1, Pallas kernels, body(): pl.pallas_call(unpack_kernel, out_shape=(jax.ShapeDtypeStruct((512, 128),...  1.15 us

profile of v9, /device:TPU:1, one launch (start us, length us, event | category | flops | bytes accessed | tf_op | source)
XLA Modules:
  0.0 39.9 jit_solution(3633762929793299054)
XLA Ops:
  0.6 38.1 %shard_map.85 = (bf16[512,128]{1,0:T(8,128)(2,1)S(1)}, bf16[32,16,128]{2,1,0:T(8,128)(2,1)S(1)}, f32[27,64,64]{2,1,0:T(8,128)S(1)}) custom-call(bf16[64,512]{1,0:T(8,128)(2,1)} %bitcast.8, bf16[27,32,64]{2,1,0:T(8,128)(2,1)} %w1_hbm.1, bf16[27,64,64]{2,1,0:T(8,128)(2,1)} %w2_hbm.1, bf16[512,128]{1,0:T(8,128)(2,1)} %bitcast.7, s32[2,27]{1,0:T(2,128)} %bitcast.10, ...), custom_call_target="tpu_custom_call" | custom-call | tf_op jit(solution)/shard_map/pallas_call | solution.py:539
  38.8 1.2 %shard_map.86 = (bf16[512,128]{1,0:T(8,128)(2,1)}, f32[27,32,64]{2,1,0:T(8,128)}, f32[27,64,64]{2,1,0:T(8,128)}) custom-call(bf16[512,128]{1,0:T(8,128)(2,1)S(1)} %get-tuple-element.9.block_ref, bf16[32,16,128]{2,1,0:T(8,128)(2,1)S(1)} %get-tuple-element.10.fin_ref, f32[27,64,64]{2,1,0:T(8,128)S(1)} %get-tuple-element.11.g2_ref), custom_call_target="tpu_custom_call" | custom-call | tf_op jit(solution)/shard_map/pallas_call | solution.py:598

commit v10 on v7

--- a/solution.py
+++ b/solution.py
@@ -57,6 +57,9 @@
     field_ref,
     face_ref,
     halo_ref,
+    edge_ref,
+    rim_ref,
+    ext_ref,
     side_ref,
     far_ref,
     c1_ref,
@@ -109,11 +112,12 @@
     ]
 
     halo_ref[...] = jnp.zeros((3, 2, 64, 128), BF16)
+    rim_ref[...] = jnp.zeros((2, 3, 64, 128), BF16)
 
     barrier = pltpu.get_barrier_semaphore()
     partners = [{"region": right, "rep": rep}, {"region": left, "rep": rep}]
     partners += [at for _, at in all_peers] + line_peers
-    for at in partners:
+    for at in partners[:2]:
         pl.semaphore_signal(barrier, inc=1, device_id=at, device_id_type=MESH)
     loads = [
         pltpu.make_async_copy(src, dst, load_sem.at[i])
@@ -129,6 +133,8 @@
     ]
     for load in loads:
         load.start()
+    for at in partners[2:]:
+        pl.semaphore_signal(barrier, inc=1, device_id=at, device_id_type=MESH)
     loads[0].wait()
     loads[1].wait()
 
@@ -143,8 +149,8 @@
 
     def halo_copy(which, side):
         return pltpu.make_async_remote_copy(
-            src_ref=face_ref.at[7 if side == 0 else 0],
-            dst_ref=halo_ref.at[which, side],
+            src_ref=edge_ref.at[side] if which == 0 else face_ref.at[7 if side == 0 else 0],
+            dst_ref=rim_ref.at[side] if which == 0 else halo_ref.at[which, side],
             send_sem=halo_send.at[which, side],
             recv_sem=halo_recv.at[which, side],
             device_id={"region": right if side == 0 else left, "rep": rep},
@@ -166,9 +172,24 @@
         def _():
             halo_copy(which, 1).wait_recv()
 
+    def halo_sent(which):
         pl.when(has_right)(lambda: halo_copy(which, 0).wait_send())
         pl.when(has_left)(lambda: halo_copy(which, 1).wait_send())
 
+    wide_half = iota((64, 128), 1) < 64
+    wide_quarter = lax.rem(iota((64, 128), 1) // 32, 2) == 0
+    one_lane = wide_quarter[0:1]
+    links = []
+    for s in range(2):
+        for k in range(9):
+            named = [(nbr_ref[t, 9 + k] == 2 + s).astype(F32) for t in range(2)]
+            links.append(jnp.where(one_lane, named[0], named[1]))
+        links.append(jnp.zeros((23, 128), F32))
+    links = jnp.concatenate(links, axis=0).astype(BF16)
+    for side, face, inside in ((0, 7, 6), (1, 0, 1)):
+        edge_ref[side, 0] = jnp.where(wide_half, face_ref[face], face_ref[inside])
+        edge_ref[side, 1] = live_ref[face].astype(BF16)
+        edge_ref[side, 2] = links
     pl.semaphore_wait(barrier, len(partners))
     halo_start(0)
 
@@ -257,7 +278,8 @@
             store(c_ref, x + 1, *shifted(field_ref[x], load, tile_lane))
 
     def build_faces(which, c_ref, store, splitter, tile_lane):
-        whole = dot(halo_ref[which].reshape(128, 128), splitter)
+        source = rim_ref[:, 0] if which == 0 else halo_ref[which]
+        whole = dot(source.reshape(128, 128), splitter)
         for side in range(2):
             far_ref[side, 0] = whole[64 * side : 64 * side + 64, :128]
             far_ref[side, 1] = whole[64 * side : 64 * side + 64, 128:]
@@ -279,6 +301,55 @@
 
             store(c_ref, 9 * side, *shifted(None, load, tile_lane))
 
+    def build_cross():
+        for side, x, base, code in ((0, 0, 18, 0), (1, 7, 0, 4)):
+            named = []
+            for s in range(2):
+                row = []
+                for k in range(9):
+                    link = [nbr_ref[t, 26 - base - k] == code + s for t in range(2)]
+                    row.append(jnp.where(link[0], 0, jnp.where(link[1], 1, 2)))
+                named.append(row)
+
+            def load(b, c, start, stop):
+                k = 3 * b + c
+                return jnp.where(
+                    rows_of(even_quarter, (stop - start) // 8),
+                    side_ref[named[0][k], x, start:stop, :],
+                    side_ref[named[1][k], x, start:stop, :],
+                )
+
+            store_first(ext_ref.at[side], 2 - 2 * side, *shifted(None, load, even_quarter))
+
+    def build_rim():
+        source, target = iota((128, 384), 0), iota((128, 384), 1)
+        group, lane_in = target // 128, lax.rem(target, 128)
+        wanted = jnp.where(group == 0, lax.rem(lane_in, 64), (group - 1) * 32 + lax.rem(lane_in, 32))
+        for inside in range(2):
+            spread_out = (source == wanted + 64 * inside).astype(BF16)
+            whole = dot(rim_ref[:, 0].reshape(128, 128), spread_out)
+            for side in range(2):
+                part = whole[64 * side : 64 * side + 64]
+                table = rim_ref[side, 2].astype(F32)
+
+                def load(b, c, start, stop):
+                    k = 3 * b + c
+                    first = table[k : k + 1] * part[start:stop, 128:256]
+                    return first + table[32 + k : 33 + k] * part[start:stop, 256:384]
+
+                slab = 1 if inside == 0 else 2 * side
+                store_first(ext_ref.at[side], slab, *shifted(part[:, 0:128], load, even_quarter))
+
+    def hidden_beside():
+        windows = []
+        for a in range(3):
+            for r in ROWS_FIRST:
+                windows.append(ext_ref[:, a, r : r + 64, :].reshape(128, 128))
+        pre = dot(jnp.concatenate(windows, axis=1), w1b_ref[...].reshape(15 * 128, 128))
+        live = rim_ref[:, 1].reshape(128, 128).astype(F32)
+        hidden = (live * pre * jax.nn.sigmoid(pre)).astype(BF16)
+        halo_ref[1] = hidden.reshape(2, 64, 128)
+
     def windows_first(start, count):
         return [
             c1_ref[start : start + count, r : r + 64, :].reshape(count * 64, 128)
@@ -320,10 +391,18 @@
         conv_inner(windows, weight, product, columns)
         if between is not None:
             between()
+        if which == 0:
+            build_cross()
         pl.loop(1, 7, unroll=3)(activate)
-        halo_wait(which)
+        if which != 1:
+            halo_wait(which)
         build_faces(which, c_ref, store, splitter, tile_lane)
+        if which == 0:
+            build_rim()
+            hidden_beside()
         conv_faces(windows, weight, product, columns)
+        if which == 2:
+            halo_sent(2)
         pl.loop(0, 2, unroll=2)(lambda i: activate(7 * i))
 
     def hidden_of(x):
@@ -352,7 +431,6 @@
         face_ref[x] = (acc_ref[rows, :] * slope_ref[x]).astype(BF16)
 
     layer(0, c1_ref, store_first, split_first(), even_quarter, windows_first, weight_first, dot, 1, hidden_of)
-    halo_start(1)
 
     loads[3].wait()
     spread2 = dot(w2_ref[...].reshape(27 * 64, 64), put).astype(BF16)
@@ -466,13 +544,14 @@
     sum1[2]()
     sum2[3]()
     for pair in range(14):
-        value = fin2_ref[4 * pair : 4 * pair + 4].reshape(64, 128).astype(F32).T
+        value = fin2_ref[4 * pair : 4 * pair + 4].reshape(64, 128).T.astype(F32)
         g2_ref[2 * pair] = value[0:64]
         if pair < 13:
             g2_ref[2 * pair + 1] = value[64:128]
     sum1[3]()
     sum2[4]()
     sum1[4]()
+    halo_sent(0)
 
 
 def unpack_kernel(block_ref, fin_ref, g2_ref, out_hbm, g1_hbm, g2_hbm, g1_ref, sem):
@@ -486,7 +565,7 @@
         copy.start()
     block_copy.start()
     for pair in range(PAIRS_FIRST):
-        value = fin_ref[4 * pair : 4 * pair + 4].reshape(64, 128).astype(F32).T
+        value = fin_ref[4 * pair : 4 * pair + 4].reshape(64, 128).T.astype(F32)
         for j in range(2):
             block = 2 * pair + j
             if block > 14:
@@ -542,6 +621,9 @@
                 pltpu.VMEM((8, 64, 128), F32),
                 pltpu.VMEM((8, 64, 128), BF16),
                 pltpu.VMEM((3, 2, 64, 128), BF16),
+                pltpu.VMEM((2, 3, 64, 128), BF16),
+                pltpu.VMEM((2, 3, 64, 128), BF16),
+                pltpu.VMEM((2, 3, 272, 128), BF16),
                 pltpu.VMEM((3, 8, 64, 128), F32),
                 pltpu.VMEM((2, 3, 64, 128), F32),
                 pltpu.VMEM((10, 272, 128), BF16),

time: 39.7 us -> 39.3 us (0.990)
  Pallas kernels: 39 us -> 38.5 us
    pallas_call x1, Pallas kernels: 37.8 us -> 37.3 us  [body(): pl.pallas_call(functools.partial(main_kernel, sizes, scale), out_shape=(j...]
where the time goes in v10:
time: 39.3 us; the launch traced here: 39.1 us
  Pallas kernels  38.5 us (98%)
  between operations  0.64 us (2%)
    pallas_call x1, Pallas kernels, body(): pl.pallas_call(functools.partial(main_kernel, sizes, scale), out_shape=(j...  37.3 us
    pallas_call x1, Pallas kernels, body(): pl.pallas_call(unpack_kernel, out_shape=(jax.ShapeDtypeStruct((512, 128),...  1.15 us

profile of v10, /device:TPU:1, one launch (start us, length us, event | category | flops | bytes accessed | tf_op | source)
XLA Modules:
  0.0 39.1 jit_solution(7967447789338143969)
XLA Ops:
  0.6 37.3 %shard_map.85 = (bf16[512,128]{1,0:T(8,128)(2,1)S(1)}, bf16[32,16,128]{2,1,0:T(8,128)(2,1)S(1)}, f32[27,64,64]{2,1,0:T(8,128)S(1)}) custom-call(bf16[64,512]{1,0:T(8,128)(2,1)} %bitcast.8, bf16[27,32,64]{2,1,0:T(8,128)(2,1)} %w1_hbm.1, bf16[27,64,64]{2,1,0:T(8,128)(2,1)} %w2_hbm.1, bf16[512,128]{1,0:T(8,128)(2,1)} %bitcast.7, s32[2,27]{1,0:T(2,128)} %bitcast.10, ...), custom_call_target="tpu_custom_call" | custom-call | tf_op jit(solution)/shard_map/pallas_call | solution.py:605
  38.0 1.2 %shard_map.86 = (bf16[512,128]{1,0:T(8,128)(2,1)}, f32[27,32,64]{2,1,0:T(8,128)}, f32[27,64,64]{2,1,0:T(8,128)}) custom-call(bf16[512,128]{1,0:T(8,128)(2,1)S(1)} %get-tuple-element.9.block_ref, bf16[32,16,128]{2,1,0:T(8,128)(2,1)S(1)} %get-tuple-element.10.fin_ref, f32[27,64,64]{2,1,0:T(8,128)S(1)} %get-tuple-element.11.g2_ref), custom_call_target="tpu_custom_call" | custom-call | tf_op jit(solution)/shard_map/pallas_call | solution.py:667

commit v11 on v10

--- a/solution.py
+++ b/solution.py
@@ -73,6 +73,9 @@
     full2_ref,
     send1_ref,
     send2_ref,
+    pair2_ref,
+    half2_ref,
+    mine2_ref,
     parts1_ref,
     parts2_ref,
     line1_ref,
@@ -81,6 +84,7 @@
     load_sem,
     halo_send,
     halo_recv,
+    pair_sem,
     sum_send,
     sum_recv,
 ):
@@ -99,13 +103,15 @@
         ((dx, dy, dc) for dx in range(nx) for dy in range(ny) for dc in range(2)),
         key=lambda d: (-apart(d[0], nx) - apart(d[1], ny), d),
     )
-    all_peers = []
+    plane_peers, all_peers = [], []
     for dx, dy, dc in offsets:
         if (dx, dy, dc) == (0, 0, 0):
             continue
         x, y, c = lax.rem(my_x + dx, nx), lax.rem(my_y + dy, ny), lax.rem(core + dc, 2)
         at = {"region": x * nz + my_z, "rep": y * 2 + c}
         all_peers.append((c * n_plane + x * ny + y, at))
+        if dc == 0:
+            plane_peers.append((x * ny + y, at))
     line_peers = [
         {"region": my_x * nz + lax.rem(my_z + step, nz), "rep": rep}
         for step in sorted(range(1, nz), key=lambda d: -apart(d, nz))
@@ -389,11 +395,11 @@
     def layer(which, c_ref, store, splitter, tile_lane, windows, weight, product, columns, activate, between=None):
         build_inner(c_ref, store, splitter, tile_lane)
         conv_inner(windows, weight, product, columns)
-        if between is not None:
-            between()
         if which == 0:
             build_cross()
         pl.loop(1, 7, unroll=3)(activate)
+        if between is not None:
+            between()
         if which != 1:
             halo_wait(which)
         build_faces(which, c_ref, store, splitter, tile_lane)
@@ -465,7 +471,7 @@
     for pair in range(14, PAIRS_SECOND):
         put_gradient(full2_ref, send2_ref, pair, jnp.zeros((64, 128), F32))
 
-    def reducer(which, unit, full, send, parts, line, fin):
+    def reducer(which, unit, send, parts, line, fin):
 
         def remote(stage, src, dst, device):
             return pltpu.make_async_remote_copy(
@@ -487,13 +493,12 @@
             remote(2, fin_whole, fin_whole, twin),
         ]
 
-        def start_parts():
-            for i, (other, at) in enumerate(all_peers):
+        def start_parts(peers):
+            for i, (other, at) in enumerate(peers):
                 remote(0, send.at[pl.ds(other * unit, unit)], parts.at[i + 1], at).start()
 
-        def start_line():
+        def start_line(total):
             whole[0].wait_recv()
-            total = full[place]
             for i in range(1, parts.shape[0]):
                 total = total + parts[i].astype(F32)
             line[my_z] = total.astype(BF16)
@@ -519,12 +524,32 @@
         return start_parts, start_line, start_back, finish, sent
 
     unit1, unit2 = 4 * per_core1 // n_plane, 4 * per_core2 // n_plane
-    sum1 = reducer(0, unit1, full1_ref, send1_ref, parts1_ref, line1_ref, fin1_ref)
-    sum2 = reducer(1, unit2, full2_ref, send2_ref, parts2_ref, line2_ref, fin2_ref)
-    sum2[0]()
+    sum1 = reducer(0, unit1, send1_ref, parts1_ref, line1_ref, fin1_ref)
+    sum2 = reducer(1, unit2, half2_ref, parts2_ref, line2_ref, fin2_ref)
+    place1 = pl.ds((core * n_plane + member) * unit1, unit1)
+
+    def half_units(which_core):
+        return pl.ds(which_core * 4 * per_core2, 4 * per_core2)
+
+    pair_copy = pltpu.make_async_remote_copy(
+        src_ref=send2_ref.at[half_units(1 - core)],
+        dst_ref=pair2_ref,
+        send_sem=pair_sem.at[0],
+        recv_sem=pair_sem.at[1],
+        device_id=twin,
+        device_id_type=MESH,
+    )
+    pair_copy.start()
+
+    def start_second():
+        pair_copy.wait_recv()
+        total = full2_ref[half_units(core)] + pair2_ref[...].astype(F32)
+        mine2_ref[...] = total
+        half2_ref[...] = total.astype(BF16)
+        sum2[0](plane_peers)
 
     third = functools.partial(windows_second, c3_ref)
-    layer(2, c3_ref, store_second, split_second(), first_half, third, weight_back, dot_nt, 0, back_of)
+    layer(2, c3_ref, store_second, split_second(), first_half, third, weight_back, dot_nt, 0, back_of, start_second)
     delta_t = face_ref[...].reshape(512, 128).T
     for pair in range(PAIRS_FIRST):
         both = []
@@ -537,9 +562,9 @@
         crossed = jnp.where(wide_quarter, two[0:64], one[64:128])
         swapped = jnp.where(wide_quarter, pltpu.roll(crossed, 96, 1), pltpu.roll(crossed, 32, 1))
         put_gradient(full1_ref, send1_ref, pair, straight + swapped)
-    sum1[0]()
-    sum2[1]()
-    sum1[1]()
+    sum1[0](all_peers)
+    sum2[1](mine2_ref[pl.ds(member * unit2, unit2)])
+    sum1[1](full1_ref[place1])
     sum2[2]()
     sum1[2]()
     sum2[3]()
@@ -549,6 +574,7 @@
         if pair < 13:
             g2_ref[2 * pair + 1] = value[64:128]
     sum1[3]()
+    pair_copy.wait_send()
     sum2[4]()
     sum1[4]()
     halo_sent(0)
@@ -637,14 +663,18 @@
                 pltpu.VMEM((2 * core2, 16, 128), F32),
                 pltpu.VMEM((2 * core1, 16, 128), BF16),
                 pltpu.VMEM((2 * core2, 16, 128), BF16),
+                pltpu.VMEM((core2, 16, 128), BF16),
+                pltpu.VMEM((core2, 16, 128), BF16),
+                pltpu.VMEM((core2, 16, 128), F32),
                 pltpu.VMEM((2 * n_plane, unit1, 16, 128), BF16),
-                pltpu.VMEM((2 * n_plane, unit2, 16, 128), BF16),
+                pltpu.VMEM((n_plane, unit2, 16, 128), BF16),
                 pltpu.VMEM((nz, unit1, 16, 128), BF16),
                 pltpu.VMEM((nz, unit2, 16, 128), BF16),
                 pltpu.VMEM((2 * core2, 16, 128), BF16),
                 dma((5,)),
                 dma((3, 2)),
                 dma((3, 2)),
+                dma((2,)),
                 dma((2, 3)),
                 dma((2, 3)),
             ],

time: 39.3 us -> 39.3 us (level)
  no operation moved by 1% of the time
where the time goes in v11:
time: 39.3 us; the launch traced here: 39.1 us
  Pallas kernels  38.5 us (98%)
  between operations  0.64 us (2%)
    pallas_call x1, Pallas kernels, body(): pl.pallas_call(functools.partial(main_kernel, sizes, scale), out_shape=(j...  37.3 us
    pallas_call x1, Pallas kernels, body(): pl.pallas_call(unpack_kernel, out_shape=(jax.ShapeDtypeStruct((512, 128),...  1.15 us

profile of v11, /device:TPU:1, one launch (start us, length us, event | category | flops | bytes accessed | tf_op | source)
XLA Modules:
  0.0 39.1 jit_solution(7846951497672045760)
XLA Ops:
  0.6 37.3 %shard_map.85 = (bf16[512,128]{1,0:T(8,128)(2,1)S(1)}, bf16[32,16,128]{2,1,0:T(8,128)(2,1)S(1)}, f32[27,64,64]{2,1,0:T(8,128)S(1)}) custom-call(bf16[64,512]{1,0:T(8,128)(2,1)} %bitcast.8, bf16[27,32,64]{2,1,0:T(8,128)(2,1)} %w1_hbm.1, bf16[27,64,64]{2,1,0:T(8,128)(2,1)} %w2_hbm.1, bf16[512,128]{1,0:T(8,128)(2,1)} %bitcast.7, s32[2,27]{1,0:T(2,128)} %bitcast.10, ...), custom_call_target="tpu_custom_call" | custom-call | tf_op jit(solution)/shard_map/pallas_call | solution.py:631
  38.0 1.2 %shard_map.86 = (bf16[512,128]{1,0:T(8,128)(2,1)}, f32[27,32,64]{2,1,0:T(8,128)}, f32[27,64,64]{2,1,0:T(8,128)}) custom-call(bf16[512,128]{1,0:T(8,128)(2,1)S(1)} %get-tuple-element.9.block_ref, bf16[32,16,128]{2,1,0:T(8,128)(2,1)S(1)} %get-tuple-element.10.fin_ref, f32[27,64,64]{2,1,0:T(8,128)S(1)} %get-tuple-element.11.g2_ref), custom_call_target="tpu_custom_call" | custom-call | tf_op jit(solution)/shard_map/pallas_call | solution.py:697

commit v12 on v11

--- a/solution.py
+++ b/solution.py
@@ -392,6 +392,11 @@
     def weight_back(a):
         return jnp.concatenate([w2b_ref[26 - k] for k in range(9 * a, 9 * a + 9)], axis=1)
 
+    def conv_whole(windows, weight):
+        weights = jnp.concatenate([weight(0), weight(2), weight(1)], axis=1)
+        got = dot(jnp.concatenate(windows(0, 10), axis=1), weights)
+        acc_ref[...] = got[0:512, 0:128] + got[64:576, 256:384] + got[128:640, 128:256]
+
     def layer(which, c_ref, store, splitter, tile_lane, windows, weight, product, columns, activate, between=None):
         build_inner(c_ref, store, splitter, tile_lane)
         conv_inner(windows, weight, product, columns)
@@ -400,8 +405,7 @@
         pl.loop(1, 7, unroll=3)(activate)
         if between is not None:
             between()
-        if which != 1:
-            halo_wait(which)
+        halo_wait(which)
         build_faces(which, c_ref, store, splitter, tile_lane)
         if which == 0:
             build_rim()
@@ -444,8 +448,12 @@
     w2b_ref[:, 64:128, :] = spread2[:, 128:].reshape(27, 64, 128)
     second = functools.partial(windows_second, c2_ref)
     loads[4].wait()
-    layer(1, c2_ref, store_second, split_second(), first_half, second, weight_second, dot, 1, outputs_of)
+    build_inner(c2_ref, store_second, split_second(), first_half)
+    build_faces(1, c2_ref, store_second, split_second(), first_half)
+    conv_whole(second, weight_second)
+    pl.loop(0, 2, unroll=2)(lambda i: outputs_of(7 * i))
     halo_start(2)
+    pl.loop(1, 7, unroll=3)(outputs_of)
 
     wide_half = iota((64, 128), 1) < 64
     wide_quarter = lax.rem(iota((64, 128), 1) // 32, 2) == 0

time: 39.3 us -> 39.1 us (level)
  no operation moved by 1% of the time
where the time goes in v12:
time: 39.1 us; the launch traced here: 38.9 us
  Pallas kernels  38.3 us (98%)
  between operations  0.64 us (2%)
    pallas_call x1, Pallas kernels, body(): pl.pallas_call(functools.partial(main_kernel, sizes, scale), out_shape=(j...  37.1 us
    pallas_call x1, Pallas kernels, body(): pl.pallas_call(unpack_kernel, out_shape=(jax.ShapeDtypeStruct((512, 128),...  1.15 us

profile of v12, /device:TPU:1, one launch (start us, length us, event | category | flops | bytes accessed | tf_op | source)
XLA Modules:
  0.0 38.9 jit_solution(13557586467230922109)
XLA Ops:
  0.6 37.1 %shard_map.85 = (bf16[512,128]{1,0:T(8,128)(2,1)S(1)}, bf16[32,16,128]{2,1,0:T(8,128)(2,1)S(1)}, f32[27,64,64]{2,1,0:T(8,128)S(1)}) custom-call(bf16[64,512]{1,0:T(8,128)(2,1)} %bitcast.8, bf16[27,32,64]{2,1,0:T(8,128)(2,1)} %w1_hbm.1, bf16[27,64,64]{2,1,0:T(8,128)(2,1)} %w2_hbm.1, bf16[512,128]{1,0:T(8,128)(2,1)} %bitcast.7, s32[2,27]{1,0:T(2,128)} %bitcast.10, ...), custom_call_target="tpu_custom_call" | custom-call | tf_op jit(solution)/shard_map/pallas_call | solution.py:639
  37.8 1.2 %shard_map.86 = (bf16[512,128]{1,0:T(8,128)(2,1)}, f32[27,32,64]{2,1,0:T(8,128)}, f32[27,64,64]{2,1,0:T(8,128)}) custom-call(bf16[512,128]{1,0:T(8,128)(2,1)S(1)} %get-tuple-element.9.block_ref, bf16[32,16,128]{2,1,0:T(8,128)(2,1)S(1)} %get-tuple-element.10.fin_ref, f32[27,64,64]{2,1,0:T(8,128)S(1)} %get-tuple-element.11.g2_ref), custom_call_target="tpu_custom_call" | custom-call | tf_op jit(solution)/shard_map/pallas_call | solution.py:705

commit v13 on v12

--- a/solution.py
+++ b/solution.py
@@ -200,11 +200,10 @@
     halo_start(0)
 
     loads[2].wait()
-    eye = iota((64, 256), 0)
-    put = ((eye == iota((64, 256), 1)) | (eye == iota((64, 256), 1) - 192)).astype(BF16)
-    spread1 = dot(w1_ref[...].reshape(27 * 32, 64), put).astype(BF16)
-    top = spread1[:, :128].reshape(3, 3, 3, 32, 128)
-    low = spread1[:, 128:].reshape(3, 3, 3, 32, 128)
+    plain = w1_ref[...].reshape(3, 3, 3, 32, 64)
+    none = jnp.zeros((3, 3, 3, 32, 64), BF16)
+    top = jnp.concatenate([plain, none], axis=-1)
+    low = jnp.concatenate([none, plain], axis=-1)
     for b in range(3):
         for at, c in ((0, 0), (64, 2)):
             w1b_ref[:, b, at : at + 32, :] = top[:, b, c]
@@ -402,9 +401,9 @@
         conv_inner(windows, weight, product, columns)
         if which == 0:
             build_cross()
-        pl.loop(1, 7, unroll=3)(activate)
         if between is not None:
             between()
+        pl.loop(1, 7, unroll=3)(activate)
         halo_wait(which)
         build_faces(which, c_ref, store, splitter, tile_lane)
         if which == 0:
@@ -443,9 +442,9 @@
     layer(0, c1_ref, store_first, split_first(), even_quarter, windows_first, weight_first, dot, 1, hidden_of)
 
     loads[3].wait()
-    spread2 = dot(w2_ref[...].reshape(27 * 64, 64), put).astype(BF16)
-    w2b_ref[:, 0:64, :] = spread2[:, :128].reshape(27, 64, 128)
-    w2b_ref[:, 64:128, :] = spread2[:, 128:].reshape(27, 64, 128)
+    none = jnp.zeros((27, 64, 64), BF16)
+    w2b_ref[:, 0:64, :] = jnp.concatenate([w2_ref[...], none], axis=-1)
+    w2b_ref[:, 64:128, :] = jnp.concatenate([none, w2_ref[...]], axis=-1)
     second = functools.partial(windows_second, c2_ref)
     loads[4].wait()
     build_inner(c2_ref, store_second, split_second(), first_half)
@@ -594,7 +593,10 @@
         pltpu.make_async_copy(g2_ref.at[pl.ds(k, 9)], g2_hbm.at[pl.ds(k, 9)], sem.at[3 + k // 9])
         for k in (0, 9, 18)
     ]
-    first_copy = pltpu.make_async_copy(g1_ref, g1_hbm, sem.at[2])
+    first_copies = [
+        pltpu.make_async_copy(g1_ref.at[pl.ds(k, 9)], g1_hbm.at[pl.ds(k, 9)], sem.at[6 + k // 9])
+        for k in (0, 9, 18)
+    ]
     for copy in second_copies:
         copy.start()
     block_copy.start()
@@ -613,11 +615,13 @@
                 offsets = (9 * a + 4,)
             for i, k in enumerate(offsets):
                 g1_ref[k] = value[64 * i + 32 * j : 64 * i + 32 * j + 32]
-    first_copy.start()
+        if pair in (2, 4, 7):
+            first_copies[pair // 3].start()
     for copy in second_copies:
         copy.wait()
     block_copy.wait()
-    first_copy.wait()
+    for copy in first_copies:
+        copy.wait()
 
 
 def solution(mesh):
@@ -713,7 +717,7 @@
             out_specs=(anywhere, anywhere, anywhere),
             scratch_shapes=[
                 pltpu.VMEM((27, 32, 64), F32),
-                dma((6,)),
+                dma((9,)),
             ],
             compiler_params=pltpu.CompilerParams(vmem_limit_bytes=40 * 2**20),
         )(block, fin1, g2)

time: 39.1 us -> 38.7 us (0.990)
  Pallas kernels: 38.3 us -> 37.9 us
where the time goes in v13:
time: 38.7 us; the launch traced here: 38.6 us
  Pallas kernels  37.9 us (98%)
  between operations  0.64 us (2%)
    pallas_call x1, Pallas kernels, body(): pl.pallas_call(functools.partial(main_kernel, sizes, scale), out_shape=(j...  36.8 us
    pallas_call x1, Pallas kernels, body(): pl.pallas_call(unpack_kernel, out_shape=(jax.ShapeDtypeStruct((512, 128),...  1.17 us

profile of v13, /device:TPU:1, one launch (start us, length us, event | category | flops | bytes accessed | tf_op | source)
XLA Modules:
  0.0 38.6 jit_solution(18328649069867807466)
XLA Ops:
  0.6 36.8 %shard_map.85 = (bf16[512,128]{1,0:T(8,128)(2,1)S(1)}, bf16[32,16,128]{2,1,0:T(8,128)(2,1)S(1)}, f32[27,64,64]{2,1,0:T(8,128)S(1)}) custom-call(bf16[64,512]{1,0:T(8,128)(2,1)} %bitcast.8, bf16[27,32,64]{2,1,0:T(8,128)(2,1)} %w1_hbm.1, bf16[27,64,64]{2,1,0:T(8,128)(2,1)} %w2_hbm.1, bf16[512,128]{1,0:T(8,128)(2,1)} %bitcast.7, s32[2,27]{1,0:T(2,128)} %bitcast.10, ...), custom_call_target="tpu_custom_call" | custom-call | tf_op jit(solution)/shard_map/pallas_call | solution.py:643
  37.4 1.2 %shard_map.86 = (bf16[512,128]{1,0:T(8,128)(2,1)}, f32[27,32,64]{2,1,0:T(8,128)}, f32[27,64,64]{2,1,0:T(8,128)}) custom-call(bf16[512,128]{1,0:T(8,128)(2,1)S(1)} %get-tuple-element.9.block_ref, bf16[32,16,128]{2,1,0:T(8,128)(2,1)S(1)} %get-tuple-element.10.fin_ref, f32[27,64,64]{2,1,0:T(8,128)S(1)} %get-tuple-element.11.g2_ref), custom_call_target="tpu_custom_call" | custom-call | tf_op jit(solution)/shard_map/pallas_call | solution.py:709

commit v14 on v13

--- a/solution.py
+++ b/solution.py
@@ -478,7 +478,7 @@
     for pair in range(14, PAIRS_SECOND):
         put_gradient(full2_ref, send2_ref, pair, jnp.zeros((64, 128), F32))
 
-    def reducer(which, unit, send, parts, line, fin):
+    def reducer(which, unit, send, parts, line, fin, back_peers):
 
         def remote(stage, src, dst, device):
             return pltpu.make_async_remote_copy(
@@ -493,7 +493,8 @@
         place = pl.ds((core * n_plane + member) * unit, unit)
         parts_whole = parts.at[pl.ds(1, parts.shape[0] - 1)]
         line_whole = line.at[pl.ds(0, nz - 1)]
-        fin_whole = fin.at[pl.ds(0, (2 * n_plane - 1) * unit)]
+        fin_whole = fin.at[pl.ds(0, len(back_peers) * unit)]
+        fin_half = fin.at[pl.ds(core * n_plane * unit, n_plane * unit)]
         whole = [
             remote(0, parts_whole, parts_whole, twin),
             remote(1, line_whole, line_whole, twin),
@@ -518,21 +519,24 @@
             for z in range(1, nz):
                 total = total + line[z].astype(F32)
             fin[place] = (total * scale).astype(BF16)
-            for _, at in all_peers:
+            for _, at in back_peers:
                 remote(2, fin.at[place], fin.at[place], at).start()
 
         def finish():
             whole[2].wait_recv()
+
+        def twin_copy():
+            return remote(3, fin_half, fin_half, twin)
 
         def sent():
             for copy in whole:
                 copy.wait_send()
 
-        return start_parts, start_line, start_back, finish, sent
+        return start_parts, start_line, start_back, finish, sent, twin_copy
 
     unit1, unit2 = 4 * per_core1 // n_plane, 4 * per_core2 // n_plane
-    sum1 = reducer(0, unit1, send1_ref, parts1_ref, line1_ref, fin1_ref)
-    sum2 = reducer(1, unit2, half2_ref, parts2_ref, line2_ref, fin2_ref)
+    sum1 = reducer(0, unit1, send1_ref, parts1_ref, line1_ref, fin1_ref, all_peers)
+    sum2 = reducer(1, unit2, half2_ref, parts2_ref, line2_ref, fin2_ref, plane_peers)
     place1 = pl.ds((core * n_plane + member) * unit1, unit1)
 
     def half_units(which_core):
@@ -575,14 +579,21 @@
     sum2[2]()
     sum1[2]()
     sum2[3]()
-    for pair in range(14):
-        value = fin2_ref[4 * pair : 4 * pair + 4].reshape(64, 128).T.astype(F32)
-        g2_ref[2 * pair] = value[0:64]
-        if pair < 13:
-            g2_ref[2 * pair + 1] = value[64:128]
+    sum2[5]().start()
+
+    def unpack_half(which_core):
+        for i in range(per_core2):
+            pair = which_core * per_core2 + i
+            value = fin2_ref[pl.ds(4 * pair, 4)].reshape(64, 128).T.astype(F32)
+            g2_ref[pl.ds(2 * pair, 2)] = value.reshape(2, 64, 64)
+
+    unpack_half(core)
+    sum2[5]().wait_recv()
+    unpack_half(1 - core)
     sum1[3]()
     pair_copy.wait_send()
     sum2[4]()
+    sum2[5]().wait_send()
     sum1[4]()
     halo_sent(0)
 
@@ -645,7 +656,7 @@
             out_shape=(
                 jax.ShapeDtypeStruct((512, 128), BF16),
                 jax.ShapeDtypeStruct((2 * core1, 16, 128), BF16),
-                jax.ShapeDtypeStruct((27, 64, 64), F32),
+                jax.ShapeDtypeStruct((2 * PAIRS_SECOND, 64, 64), F32),
             ),
             in_specs=[hbm, hbm, hbm, hbm, smem, hbm],
             out_specs=(vmem, vmem, vmem),
@@ -687,8 +698,8 @@
                 dma((3, 2)),
                 dma((3, 2)),
                 dma((2,)),
-                dma((2, 3)),
-                dma((2, 3)),
+                dma((2, 4)),
+                dma((2, 4)),
             ],
             compiler_params=pltpu.CompilerParams(
                 collective_id=0, has_side_effects=True, vmem_limit_bytes=40 * 2**20

time: 38.7 us -> 38.7 us (level)
  no operation moved by 1% of the time
where the time goes in v14:
time: 38.7 us; the launch traced here: 38.6 us
  Pallas kernels  38 us (98%)
  between operations  0.64 us (2%)
    pallas_call x1, Pallas kernels, body(): pl.pallas_call(functools.partial(main_kernel, sizes, scale), out_shape=(j...  36.8 us
    pallas_call x1, Pallas kernels, body(): pl.pallas_call(unpack_kernel, out_shape=(jax.ShapeDtypeStruct((512, 128),...  1.17 us

profile of v14, /device:TPU:1, one launch (start us, length us, event | category | flops | bytes accessed | tf_op | source)
XLA Modules:
  0.0 38.6 jit_solution(12771790830108142033)
XLA Ops:
  0.6 36.8 %shard_map.85 = (bf16[512,128]{1,0:T(8,128)(2,1)S(1)}, bf16[32,16,128]{2,1,0:T(8,128)(2,1)S(1)}, f32[32,64,64]{2,1,0:T(8,128)S(1)}) custom-call(bf16[64,512]{1,0:T(8,128)(2,1)} %bitcast.8, bf16[27,32,64]{2,1,0:T(8,128)(2,1)} %w1_hbm.1, bf16[27,64,64]{2,1,0:T(8,128)(2,1)} %w2_hbm.1, bf16[512,128]{1,0:T(8,128)(2,1)} %bitcast.7, s32[2,27]{1,0:T(2,128)} %bitcast.10, ...), custom_call_target="tpu_custom_call" | custom-call | tf_op jit(solution)/shard_map/pallas_call | solution.py:654
  37.4 1.2 %shard_map.86 = (bf16[512,128]{1,0:T(8,128)(2,1)}, f32[27,32,64]{2,1,0:T(8,128)}, f32[27,64,64]{2,1,0:T(8,128)}) custom-call(bf16[512,128]{1,0:T(8,128)(2,1)S(1)} %get-tuple-element.9.block_ref, bf16[32,16,128]{2,1,0:T(8,128)(2,1)S(1)} %get-tuple-element.10.fin_ref, f32[32,64,64]{2,1,0:T(8,128)S(1)} %get-tuple-element.11.g2_ref), custom_call_target="tpu_custom_call" | custom-call | tf_op jit(solution)/shard_map/pallas_call | solution.py:720

commit v15 on v13

--- a/solution.py
+++ b/solution.py
@@ -589,16 +589,9 @@
 
 def unpack_kernel(block_ref, fin_ref, g2_ref, out_hbm, g1_hbm, g2_hbm, g1_ref, sem):
     block_copy = pltpu.make_async_copy(block_ref, out_hbm, sem.at[0])
-    second_copies = [
-        pltpu.make_async_copy(g2_ref.at[pl.ds(k, 9)], g2_hbm.at[pl.ds(k, 9)], sem.at[3 + k // 9])
-        for k in (0, 9, 18)
-    ]
-    first_copies = [
-        pltpu.make_async_copy(g1_ref.at[pl.ds(k, 9)], g1_hbm.at[pl.ds(k, 9)], sem.at[6 + k // 9])
-        for k in (0, 9, 18)
-    ]
-    for copy in second_copies:
-        copy.start()
+    second_copy = pltpu.make_async_copy(g2_ref, g2_hbm, sem.at[1])
+    first_copy = pltpu.make_async_copy(g1_ref, g1_hbm, sem.at[2])
+    second_copy.start()
     block_copy.start()
     for pair in range(PAIRS_FIRST):
         value = fin_ref[4 * pair : 4 * pair + 4].reshape(64, 128).T.astype(F32)
@@ -615,13 +608,10 @@
                 offsets = (9 * a + 4,)
             for i, k in enumerate(offsets):
                 g1_ref[k] = value[64 * i + 32 * j : 64 * i + 32 * j + 32]
-        if pair in (2, 4, 7):
-            first_copies[pair // 3].start()
-    for copy in second_copies:
-        copy.wait()
+    first_copy.start()
+    second_copy.wait()
     block_copy.wait()
-    for copy in first_copies:
-        copy.wait()
+    first_copy.wait()
 
 
 def solution(mesh):
@@ -717,7 +707,7 @@
             out_specs=(anywhere, anywhere, anywhere),
             scratch_shapes=[
                 pltpu.VMEM((27, 32, 64), F32),
-                dma((9,)),
+                dma((3,)),
             ],
             compiler_params=pltpu.CompilerParams(vmem_limit_bytes=40 * 2**20),
         )(block, fin1, g2)

time: 38.7 us -> 38.6 us (level)
  no operation moved by 1% of the time
where the time goes in v15:
time: 38.6 us; the launch traced here: 38.5 us
  Pallas kernels  37.9 us (98%)
  between operations  0.64 us (2%)
    pallas_call x1, Pallas kernels, body(): pl.pallas_call(functools.partial(main_kernel, sizes, scale), out_shape=(j...  36.8 us
    pallas_call x1, Pallas kernels, body(): pl.pallas_call(unpack_kernel, out_shape=(jax.ShapeDtypeStruct((512, 128),...  1.12 us

profile of v15, /device:TPU:1, one launch (start us, length us, event | category | flops | bytes accessed | tf_op | source)
XLA Modules:
  0.0 38.5 jit_solution(4024559675350436104)
XLA Ops:
  0.6 36.8 %shard_map.85 = (bf16[512,128]{1,0:T(8,128)(2,1)S(1)}, bf16[32,16,128]{2,1,0:T(8,128)(2,1)S(1)}, f32[27,64,64]{2,1,0:T(8,128)S(1)}) custom-call(bf16[64,512]{1,0:T(8,128)(2,1)} %bitcast.8, bf16[27,32,64]{2,1,0:T(8,128)(2,1)} %w1_hbm.1, bf16[27,64,64]{2,1,0:T(8,128)(2,1)} %w2_hbm.1, bf16[512,128]{1,0:T(8,128)(2,1)} %bitcast.7, s32[2,27]{1,0:T(2,128)} %bitcast.10, ...), custom_call_target="tpu_custom_call" | custom-call | tf_op jit(solution)/shard_map/pallas_call | solution.py:633
  37.4 1.1 %shard_map.86 = (bf16[512,128]{1,0:T(8,128)(2,1)}, f32[27,32,64]{2,1,0:T(8,128)}, f32[27,64,64]{2,1,0:T(8,128)}) custom-call(bf16[512,128]{1,0:T(8,128)(2,1)S(1)} %get-tuple-element.9.block_ref, bf16[32,16,128]{2,1,0:T(8,128)(2,1)S(1)} %get-tuple-element.10.fin_ref, f32[27,64,64]{2,1,0:T(8,128)S(1)} %get-tuple-element.11.g2_ref), custom_call_target="tpu_custom_call" | custom-call | tf_op jit(solution)/shard_map/pallas_call | solution.py:699
